TPU v7x, 32 devices: a whole 2x2x4 slice. The times are simulated.
32 devices in a mesh: branch: 4 (over x, core), dp: 4 (over z), mp: 2 (over y).
Axes of the slice: x: 2, y: 2, z: 4, core: 2. Of those that a mesh axis runs over, the one named last changes fastest.
Arguments:
- hidden_in: bfloat16 [2048, 7168], P(('branch', 'dp'), 'mp'), parts along dimension 0, may hold values from -54 to 54
- embed_in: bfloat16 [2048, 7168], P(('branch', 'dp'), 'mp'), parts along dimension 0, may hold values from -54 to 54
- hidden_gain: float32 [28672], P(('branch', 'mp')), parts along dimension 0, may hold values from 0.1 to 1.9
- embed_gain: float32 [28672], P(('branch', 'mp')), parts along dimension 0, may hold values from 0.1 to 1.9
- w_proj_hidden: bfloat16 [28672, 7168], P(('branch', 'mp'), 'dp'), parts along dimension 0, may hold values from -0.10022297 to 0.10022297
- w_proj_embed: bfloat16 [28672, 7168], P(('branch', 'mp'), 'dp'), parts along dimension 0, may hold values from -0.10022297 to 0.10022297
- attn_gain: float32 [28672], P(('branch', 'dp')), parts along dimension 0, may hold values from 0.1 to 1.9
- w_latent: bfloat16 [28672, 2112], P(('branch', 'dp')), parts along dimension 0, may hold values from -0.0625 to 0.0625
- q_gain: float32 [6144], P('branch'), parts along dimension 0, may hold values from 0.1 to 1.9
- kv_gain: float32 [2048], P('branch'), parts along dimension 0, may hold values from 0.1 to 1.9
Outputs:
- mtp_hidden: bfloat16 [2048, 7168], P(('branch', 'mp'), 'dp'), parts along dimension 0
- q_latent: bfloat16 [2048, 1536], P(('branch', 'mp', 'dp')), parts along dimension 0
- kv_latent: bfloat16 [2048, 512], P(('branch', 'mp', 'dp')), parts along dimension 0
- key_rope: bfloat16 [2048, 64], P(('branch', 'mp', 'dp')), parts along dimension 0
There are 4 independent parts, one for each index of `branch`. A program takes and returns all parts, laid end to end along the dimension named above; each array names one. Nothing has to cross between parts.
All inputs are finite; a program needn't handle non-finite values.
Results may differ from a plain program's by a relative error of at most 0.03.
Values may be sent and summed in bfloat16 or wider, within the bound.
No kernel may reach another device: no remote copies, remote signals or barrier semaphores. Data moves between devices by JAX's collectives and lax.ppermute only.
A program may use at most 128 MiB of HBM per device.

v0:
```python
import math

import jax
import jax.numpy as jnp
from jax import lax
from jax.sharding import PartitionSpec as P

D = 7168
Q_LAT = 1536
KV_LAT = 512
LENGTH = 2048


epsilon = 1e-06


def inverse_rms(squares_total, width):
    return lax.rsqrt(squares_total / width + epsilon)


def latent_norm(part, gain):
    scale_rows = inverse_rms(jnp.sum(part * part, axis=1), part.shape[1])
    return (part * scale_rows[:, None] * gain[None, :]).astype(jnp.bfloat16)


def rotate_keys(rope_part, positions):
    half_width = rope_part.shape[1] // 2
    frequency = jnp.exp(
        jnp.arange(half_width, dtype=jnp.float32) * (-2.0 * math.log(10000.0) / rope_part.shape[1])
    )
    angle_grid = positions.astype(jnp.float32)[:, None] * frequency[None, :]
    cosine = jnp.cos(angle_grid)
    sine_grid = jnp.sin(angle_grid)
    lower_half = rope_part[:, :half_width]
    upper_half = rope_part[:, half_width:]
    return jnp.concatenate(
        [
            lower_half * cosine - upper_half * sine_grid,
            lower_half * sine_grid + upper_half * cosine,
        ],
        axis=1,
    )


def shards(
    hidden_in,
    embed_in,
    hidden_gain,
    embed_gain,
    w_proj_hidden,
    w_proj_embed,
    attn_gain,
    w_latent,
    q_gain,
    kv_gain,
):
    hidden_wide = hidden_in.astype(jnp.float32)
    embed_wide = embed_in.astype(jnp.float32)
    entry_sums = lax.psum(
        (jnp.sum(hidden_wide * hidden_wide, axis=1), jnp.sum(embed_wide * embed_wide, axis=1)), "mp"
    )
    hidden_norm = (
        hidden_wide * inverse_rms(entry_sums[0], D)[:, None] * hidden_gain[None, :]
    ).astype(jnp.bfloat16)
    embed_norm = (embed_wide * inverse_rms(entry_sums[1], D)[:, None] * embed_gain[None, :]).astype(
        jnp.bfloat16
    )
    hidden_all = lax.all_gather(hidden_norm, "dp", axis=0, tiled=True)
    embed_all = lax.all_gather(embed_norm, "dp", axis=0, tiled=True)
    tok_share = hidden_all.shape[0] // lax.axis_size("mp")
    proj_sum = lax.psum_scatter(
        (
            jnp.dot(hidden_all, w_proj_hidden, preferred_element_type=jnp.float32)
            + jnp.dot(embed_all, w_proj_embed, preferred_element_type=jnp.float32)
        ).astype(jnp.bfloat16),
        "mp",
        scatter_dimension=0,
        tiled=True,
    )
    mtp_hidden = lax.optimization_barrier(proj_sum)
    proj_wide = mtp_hidden.astype(jnp.float32)
    square_rows = jnp.sum(proj_wide * proj_wide, axis=1)
    normed_rows = (proj_wide * attn_gain[None, :]).astype(jnp.bfloat16)
    rows_out = tok_share // lax.axis_size("dp")
    first_own = lax.axis_index("dp") * rows_out
    partial_latent = jnp.dot(normed_rows, w_latent, preferred_element_type=jnp.float32)
    latent_total, square_total = (
        lax.psum(partial_latent.astype(jnp.bfloat16), "dp").astype(jnp.float32),
        lax.psum(square_rows.astype(jnp.bfloat16), "dp").astype(jnp.float32),
    )
    latent_sum = lax.dynamic_slice_in_dim(latent_total, first_own, rows_out, 0)
    square_sum = lax.dynamic_slice_in_dim(square_total, first_own, rows_out, 0)
    latent = latent_sum * inverse_rms(square_sum, D)[:, None]
    first_token = lax.axis_index("mp") * tok_share + first_own
    positions = (first_token + jnp.arange(rows_out, dtype=jnp.int32)) % LENGTH
    q_latent = latent_norm(latent[:, :Q_LAT], q_gain)
    kv_latent = latent_norm(latent[:, Q_LAT : Q_LAT + KV_LAT], kv_gain)
    key_rope = rotate_keys(latent[:, Q_LAT + KV_LAT :], positions).astype(jnp.bfloat16)
    return (mtp_hidden, q_latent, kv_latent, key_rope)


def solution(mesh):
    placed = (
        P(("branch", "dp"), "mp"),
        P(("branch", "dp"), "mp"),
        P(("branch", "mp")),
        P(("branch", "mp")),
        P(("branch", "mp"), "dp"),
        P(("branch", "mp"), "dp"),
        P(("branch", "dp")),
        P(("branch", "dp"), None),
        P("branch"),
        P("branch"),
    )
    return jax.shard_map(
        shards,
        mesh=mesh,
        in_specs=placed,
        out_specs=(
            P(("branch", "mp"), "dp"),
            P(("branch", "mp", "dp"), None),
            P(("branch", "mp", "dp"), None),
            P(("branch", "mp", "dp"), None),
        ),
        check_vma=False,
    )
```

profile of v0, /device:TPU:8, one launch (start us, length us, event | category | flops | bytes accessed | tf_op | source)
XLA Modules:
  0.0 273.4 jit_solution(2996025339034074938)
XLA Ops:
  7.2 0.0 copy-start
  7.2 0.0 copy-start.3
  7.2 0.0 all-gather.3.cloned.1.call-start
  7.2 2.0 fusion
  9.2 0.0 copy-start.1
  9.2 0.0 copy-start.4
  9.2 5.1 %all-reduce = (f32[128]{0:T(128)S(1)}, f32[128]{0:T(128)S(1)}) all-reduce(f32[128]{0:T(128)S(1)} %get-tuple-element.12, f32[128]{0:T(128)S(1)} %get-tuple-element.13), channel_id=1, replica_groups=mesh['branch'=4,'dp'=4,'mp'=2] {'mp'}, use_global_device_ids=true, to_apply=%region_1.0 | all-reduce | flops 256 | bytes 2048 | tf_op jit(solution)/shard_map/psum | solution.py:59
  14.3 0.0 copy-done
  14.3 0.0 copy-done.3
  14.3 1.2 fusion.2
  15.5 0.0 all-gather.3.cloned.1.call-update
  15.5 0.0 all-gather.5.cloned.1.call-start
  15.6 0.0 copy-done.1
  15.6 0.0 copy-done.4
  15.6 1.2 fusion.5
  16.8 0.0 all-gather.5.cloned.1.call-update
  16.9 0.0 reduce-scatter.2.cloned.1.call-start
  16.9 69.5 %all-gather.3.cloned.1.call-done = bf16[512,3584]{1,0:T(8,128)(2,1)} async-done(((bf16[128,3584]{1,0:T(8,128)(2,1)}), bf16[512,3584]{1,0:T(8,128)(2,1)}) %all-gather.3.cloned.1.call-update) | async-done | bytes 3670032 | tf_op jit(solution)/shard_map/all_gather | solution.py:68
  86.4 13.5 %fusion.20 = f32[512,1792]{1,0:T(8,128)} fusion(bf16[512,3584]{1,0:T(8,128)(2,1)} %all-gather.3.cloned.1.call-done, bf16[3584,1792]{1,0:T(8,128)(2,1)} %param.14), kind=kOutput, calls=%fused_computation.44 | convolution fusion | flops 6576668672 | bytes 20185088 | tf_op jit(solution)/shard_map/dot_general | solution.py:73
  99.8 58.9 %all-gather.5.cloned.1.call-done = bf16[512,3584]{1,0:T(8,128)(2,1)} async-done(((bf16[128,3584]{1,0:T(8,128)(2,1)}), bf16[512,3584]{1,0:T(8,128)(2,1)}) %all-gather.5.cloned.1.call-update) | async-done | bytes 3670032 | tf_op jit(solution)/shard_map/all_gather | solution.py:69
  158.7 13.7 %add_convert_fusion = bf16[512,1792]{1,0:T(8,128)(2,1)} fusion(f32[512,1792]{1,0:T(8,128)} %fusion.20, bf16[512,3584]{1,0:T(8,128)(2,1)} %all-gather.5.cloned.1.call-done, bf16[3584,1792]{1,0:T(8,128)(2,1)} %param.15), kind=kOutput, calls=%fused_computation.1 | convolution fusion | flops 6578503680 | bytes 22020096 | tf_op jit(solution)/shard_map/dot_general | solution.py:74
  172.4 0.0 copy-start.7
  172.4 0.0 reduce-scatter.2.cloned.1.call-update
  172.5 0.0 all-reduce.3.cloned.1.call-start
  172.5 30.3 %reduce-scatter.2.cloned.1.call-done = bf16[256,1792]{1,0:T(8,128)(2,1)} async-done(((bf16[512,1792]{1,0:T(8,128)(2,1)}), bf16[256,1792]{1,0:T(8,128)(2,1)}) %reduce-scatter.2.cloned.1.call-update) | async-done | bytes 917520 | tf_op jit(solution)/shard_map/reduce_scatter | solution.py:71
  202.9 0.0 copy-done.7
  202.9 0.0 copy-start.2
  202.9 6.7 %convolution_convert_fusion = bf16[256,2112]{0,1:T(8,128)(2,1)} fusion(bf16[1792,2112]{0,1:T(8,128)(2,1)} %param.17, bf16[256,1792]{1,0:T(8,128)(2,1)} %reduce-scatter.2.cloned.1.call-done, f32[1792]{0:T(1024)S(1)} %copy-done.7), kind=kOutput, calls=%fused_computation | convolution fusion | flops 1939685376 | bytes 9575424 | tf_op jit(solution)/shard_map/dot_general | solution.py:86
  209.6 0.0 all-reduce.3.cloned.1.call-update
  209.6 0.0 copy-start.5
  209.6 0.0 copy-done.2
  209.7 0.3 fusion.7
  209.9 8.9 %psum.31 = bf16[256]{0:T(256)(128)(2,1)S(1)} all-reduce(bf16[256]{0:T(256)(128)(2,1)S(1)} %fusion.7), channel_id=1, replica_groups=mesh['branch'=4,'dp'=4,'mp'=2] {'dp'}, use_global_device_ids=true, to_apply=%region_7.0 | all-reduce | flops 256 | bytes 1024 | tf_op jit(solution)/shard_map/psum | solution.py:89
  218.9 0.1 add_rsqrt_fusion.2
  218.9 0.0 copy-start.6
  218.9 43.5 %all-reduce.3.cloned.1.call-done = bf16[256,2112]{0,1:T(8,128)(2,1)} async-done(((bf16[256,2112]{0,1:T(8,128)(2,1)}), bf16[256,2112]{0,1:T(8,128)(2,1)}) %all-reduce.3.cloned.1.call-update) | async-done | bytes 1081360 | tf_op jit(solution)/shard_map/psum | solution.py:88
  262.5 1.3 convert_multiply_fusion.6
  263.7 0.2 multiply_reduce_fusion
  264.0 0.1 multiply_reduce_fusion.1
  264.0 0.0 copy-done.5
  264.1 0.3 multiply_convert_fusion
  264.3 0.8 copy.15
  265.2 0.0 copy-done.6
  265.2 0.1 multiply_convert_fusion.1
  265.3 0.7 copy.16
  266.1 0.1 fusion.15
  266.2 0.7 copy.17
  (8 shorter events, 0.1 us)
Async XLA Ops:
  7.2 7.1 %copy-start = (bf16[128,3584]{1,0:T(8,128)(2,1)S(1)}, bf16[128,3584]{1,0:T(8,128)(2,1)}, u32[]{:S(2)}) copy-start(bf16[128,3584]{1,0:T(8,128)(2,1)} %param.10) | copy-start | bytes 2752516
  7.2 7.1 %copy-start.3 = (f32[3584]{0:T(1024)S(1)}, f32[3584]{0:T(1024)}, u32[]{:S(2)}) copy-start(f32[3584]{0:T(1024)} %param.12) | copy-start | bytes 43012
  7.2 79.2 %all-gather.3.cloned.1.call-start = ((), (), s32[]{:S(2)}) async-start(), calls=%async_computation.1 | async-start | bytes 4587520 | tf_op jit(solution)/shard_map/all_gather | solution.py:68
  9.2 6.4 %copy-start.1 = (bf16[128,3584]{1,0:T(8,128)(2,1)S(1)}, bf16[128,3584]{1,0:T(8,128)(2,1)}, u32[]{:S(2)}) copy-start(bf16[128,3584]{1,0:T(8,128)(2,1)} %param.11) | copy-start | bytes 2752516
  9.2 6.4 %copy-start.4 = (f32[3584]{0:T(1024)S(1)}, f32[3584]{0:T(1024)}, u32[]{:S(2)}) copy-start(f32[3584]{0:T(1024)} %param.13) | copy-start | bytes 43012
  15.5 143.2 %all-gather.5.cloned.1.call-start = ((), (), s32[]{:S(2)}) async-start(), calls=%async_computation.2 | async-start | bytes 4587520 | tf_op jit(solution)/shard_map/all_gather | solution.py:69
  16.9 186.0 %reduce-scatter.2.cloned.1.call-start = ((), (), s32[]{:S(2)}) async-start(), calls=%async_computation.3 | async-start | bytes 2752512 | tf_op jit(solution)/shard_map/reduce_scatter | solution.py:71
  172.4 30.4 %copy-start.7 = (f32[1792]{0:T(1024)S(1)}, f32[1792]{0:T(1024)}, u32[]{:S(2)}) copy-start(f32[1792]{0:T(1024)} %param.16) | copy-start | bytes 21508
  172.5 90.0 %all-reduce.3.cloned.1.call-start = ((), (), s32[]{:S(2)}) async-start(), calls=%async_computation.4 | async-start | bytes 2162688 | tf_op jit(solution)/shard_map/psum | solution.py:88
  202.9 6.8 %copy-start.2 = (bf16[256,1792]{1,0:T(8,128)(2,1)S(1)}, bf16[256,1792]{1,0:T(8,128)(2,1)}, u32[]{:S(2)}) copy-start(bf16[256,1792]{1,0:T(8,128)(2,1)} %reduce-scatter.2.cloned.1.call-done) | copy-start | bytes 2752516
  209.6 54.5 %copy-start.5 = (f32[1536]{0:T(1024)S(1)}, f32[1536]{0:T(1024)}, u32[]{:S(2)}) copy-start(f32[1536]{0:T(1024)} %param.18) | copy-start | bytes 18436
  218.9 46.2 %copy-start.6 = (f32[512]{0:T(512)S(1)}, f32[512]{0:T(512)}, u32[]{:S(2)}) copy-start(f32[512]{0:T(512)} %param.19) | copy-start | bytes 6148
Sparse Core Ops, SparseCore 0:
  15.7 70.6 all-gather.2
  87.9 70.7 all-gather.4
  172.6 30.2 reduce-scatter.1
  209.7 52.7 all-reduce.2
where the time goes:
time: 275 us; the launch traced here: 273 us
  waiting for transfers between devices  202 us (73%)
  matrix products  33.9 us (12%)
  blocking collectives  14 us (5%)
  between operations  13.9 us (5%)
  other arithmetic  6.9 us (3%)
    all_gather x1, waiting for transfers between devices, shards(): hidden_all = lax.all_gather(hidden_norm, 'dp', axis=0, tiled=True)  69.5 us
    all_gather x1, waiting for transfers between devices, shards(): embed_all = lax.all_gather(embed_norm, 'dp', axis=0, tiled=True)  58.9 us
    psum x1, waiting for transfers between devices, shards(): lax.psum(partial_latent.astype(jnp.bfloat16), 'dp').astype(jnp.float32)  43.5 us
    reduce_scatter x1, waiting for transfers between devices, shards(): lax.psum_scatter((jnp.dot(hidden_all, w_proj_hidden, preferred_element_ty...  30.3 us
    dot_general x1, matrix products, shards(): jnp.dot(embed_all, w_proj_embed, preferred_element_type=jnp.float32)  13.7 us
    dot_general x1, matrix products, shards(): jnp.dot(hidden_all, w_proj_hidden, preferred_element_type=jnp.float32)  13.5 us
    psum x1, blocking collectives, shards(): lax.psum(square_rows.astype(jnp.bfloat16), 'dp').astype(jnp.float32)  8.94 us
    dot_general x1, matrix products, shards(): jnp.dot(normed_rows, w_latent, preferred_element_type=jnp.float32)  6.71 us
  transfers between devices with their start and end apart: 4, of which 4 were waited for; matrix products, arithmetic and copies ran while one was open for 6% of the time, Pallas kernels for 0%

commit v1 on v0

v1 whole, which is shorter than its diff:
```python
import math

import jax
import jax.numpy as jnp
from jax import lax
from jax.experimental import pallas as pl
from jax.experimental.pallas import tpu as pltpu
from jax.sharding import PartitionSpec as P

D = 7168
Q_LAT = 1536
KV_LAT = 512
LENGTH = 2048
LANES = 128
VMEM_BYTES = 48 * 1024 * 1024

epsilon = 1e-06


def inverse_rms(squares_total, width):
    return lax.rsqrt(squares_total / width + epsilon)


def latent_norm(part, gain):
    scale_rows = inverse_rms(jnp.sum(part * part, axis=1), part.shape[1])
    return (part * scale_rows[:, None] * gain[None, :]).astype(jnp.bfloat16)


def rope_tables(width, positions):
    half_width = width // 2
    frequency = jnp.exp(
        jnp.arange(half_width, dtype=jnp.float32) * (-2.0 * math.log(10000.0) / width)
    )
    angle_grid = positions.astype(jnp.float32)[:, None] * frequency[None, :]
    return jnp.cos(angle_grid), jnp.sin(angle_grid)


def rotate_keys(rope_part, cosine, sine_grid):
    half_width = rope_part.shape[1] // 2
    lower_half = rope_part[:, :half_width]
    upper_half = rope_part[:, half_width:]
    return jnp.concatenate(
        [
            lower_half * cosine - upper_half * sine_grid,
            lower_half * sine_grid + upper_half * cosine,
        ],
        axis=1,
    )


def block_of(size, most):
    best = LANES
    for width in range(LANES, most + 1, LANES):
        if size % width == 0:
            best = width
    return best


def project(groups, scales, hidden_gain, embed_gain, w_hidden, w_embed, own_first=None):
    depth, width = w_hidden.shape
    step = block_of(depth, 512)
    steps = depth // step
    counts = [len(group) for group in groups]
    arrays = [array for group in groups for array in group]
    rows = [group[0].shape[0] for group in groups]
    total = sum(rows)
    swaps = own_first is not None

    def body(*refs):
        refs = list(refs)
        flag = refs.pop(0) if swaps else None
        hidden_refs = refs[: len(arrays)]
        embed_refs = refs[len(arrays) : 2 * len(arrays)]
        scale_ref, hgain_ref, egain_ref, wh_ref, we_ref = refs[2 * len(arrays) : 2 * len(arrays) + 5]
        outs = refs[2 * len(arrays) + 5 : -1]
        acc = refs[-1]
        index = pl.program_id(0)

        @pl.when(index == 0)
        def _():
            acc[...] = jnp.zeros_like(acc)

        def normed(sources, gain_ref, column):
            parts = []
            at = 0
            for count in counts:
                value = sources[at][...].astype(jnp.float32)
                for other in sources[at + 1 : at + count]:
                    value = value + other[...].astype(jnp.float32)
                at += count
                parts.append(value)
            whole = parts[0] if len(parts) == 1 else jnp.concatenate(parts, axis=0)
            return (whole * scale_ref[:, column : column + 1] * gain_ref[...]).astype(jnp.bfloat16)

        acc[...] += jnp.dot(
            normed(hidden_refs, hgain_ref, 0), wh_ref[...], preferred_element_type=jnp.float32
        ) + jnp.dot(
            normed(embed_refs, egain_ref, 1), we_ref[...], preferred_element_type=jnp.float32
        )

        @pl.when(index == steps - 1)
        def _():
            if swaps:
                first = acc[: rows[0], :].astype(jnp.bfloat16)
                second = acc[rows[0] :, :].astype(jnp.bfloat16)
                keep = flag[0] == 1
                outs[0][...] = jnp.where(keep, first, second)
                outs[1][...] = jnp.where(keep, second, first)
            else:
                outs[0][...] = acc[...].astype(jnp.bfloat16)

    in_specs = [pl.BlockSpec(memory_space=pltpu.SMEM)] if swaps else []
    for array in arrays:
        in_specs.append(pl.BlockSpec((array.shape[0], step), lambda k: (0, k)))
    for array in arrays:
        in_specs.append(pl.BlockSpec((array.shape[0], step), lambda k: (0, steps + k)))
    in_specs += [
        pl.BlockSpec((total, 2), lambda k: (0, 0)),
        pl.BlockSpec((1, step), lambda k: (0, k)),
        pl.BlockSpec((1, step), lambda k: (0, k)),
        pl.BlockSpec((step, width), lambda k: (k, 0)),
        pl.BlockSpec((step, width), lambda k: (k, 0)),
    ]
    out_rows = rows if swaps else [total]
    result = pl.pallas_call(
        body,
        grid=(steps,),
        in_specs=in_specs,
        out_specs=[pl.BlockSpec((r, width), lambda k: (0, 0)) for r in out_rows],
        out_shape=[jax.ShapeDtypeStruct((r, width), jnp.bfloat16) for r in out_rows],
        scratch_shapes=[pltpu.VMEM((total, width), jnp.float32)],
        compiler_params=pltpu.CompilerParams(vmem_limit_bytes=VMEM_BYTES),
        cost_estimate=pl.CostEstimate(
            flops=4 * total * depth * width, bytes_accessed=4 * depth * width, transcendentals=0
        ),
        name="project",
    )(
        *([own_first] if swaps else []),
        *arrays,
        *arrays,
        scales,
        hidden_gain[None, :],
        embed_gain[None, :],
        w_hidden,
        w_embed,
    )
    return result if swaps else result[0]


def latent_partial(own, received, gain, w_latent):
    rows, width = own.shape
    lat = w_latent.shape[1]
    padded = -(-(lat + 2) // LANES) * LANES
    edge = padded - LANES
    step = block_of(width, 256)
    steps = width // step

    def body(own_ref, received_ref, gain_ref, w_ref, mtp_ref, lat_ref, acc, squares):
        index = pl.program_id(0)

        @pl.when(index == 0)
        def _():
            acc[...] = jnp.zeros_like(acc)
            squares[...] = jnp.zeros_like(squares)

        mtp = (own_ref[...].astype(jnp.float32) + received_ref[...].astype(jnp.float32)).astype(
            jnp.bfloat16
        )
        mtp_ref[...] = mtp
        wide = mtp.astype(jnp.float32)
        squares[...] += jnp.sum(wide * wide, axis=1, keepdims=True)
        normed = (wide * gain_ref[...]).astype(jnp.bfloat16)
        acc[:, :lat] += jnp.dot(normed, w_ref[...], preferred_element_type=jnp.float32)

        @pl.when(index == steps - 1)
        def _():
            lat_ref[:, :edge] = acc[:, :edge].astype(jnp.bfloat16)
            column = lax.broadcasted_iota(jnp.int32, (rows, LANES), 1)
            total = squares[...]
            high = total.astype(jnp.bfloat16).astype(jnp.float32)
            tail = jnp.where(column == lat - edge, high, jnp.where(column == lat - edge + 1, total - high, 0.0))
            tail = jnp.where(column < lat - edge, acc[:, edge:], tail)
            lat_ref[:, edge:] = tail.astype(jnp.bfloat16)

    return pl.pallas_call(
        body,
        grid=(steps,),
        in_specs=[
            pl.BlockSpec((rows, step), lambda k: (0, k)),
            pl.BlockSpec((rows, step), lambda k: (0, k)),
            pl.BlockSpec((1, step), lambda k: (0, k)),
            pl.BlockSpec((step, lat), lambda k: (k, 0)),
        ],
        out_specs=[
            pl.BlockSpec((rows, step), lambda k: (0, k)),
            pl.BlockSpec((rows, padded), lambda k: (0, 0)),
        ],
        out_shape=[
            jax.ShapeDtypeStruct((rows, width), jnp.bfloat16),
            jax.ShapeDtypeStruct((rows, padded), jnp.bfloat16),
        ],
        scratch_shapes=[
            pltpu.VMEM((rows, padded), jnp.float32),
            pltpu.VMEM((rows, 1), jnp.float32),
        ],
        compiler_params=pltpu.CompilerParams(vmem_limit_bytes=VMEM_BYTES),
        cost_estimate=pl.CostEstimate(
            flops=2 * rows * width * lat, bytes_accessed=2 * width * lat, transcendentals=0
        ),
        name="latent_partial",
    )(own, received, gain[None, :], w_latent)


def finish(base, late, q_gain, kv_gain, cosine, sine_grid):
    rows = base.shape[0]
    lat = Q_LAT + KV_LAT
    rope = 2 * cosine.shape[1]

    def body(base_ref, *refs):
        late_refs = refs[: len(late)]
        qg_ref, kg_ref, cos_ref, sin_ref, q_ref, kv_ref, rope_ref, total = refs[len(late) :]
        total[...] = base_ref[...]
        for (at, array), ref in zip(late, late_refs, strict=True):
            total[at : at + array.shape[0], :] += ref[...].astype(jnp.float32)
        whole = total[...]
        squares = whole[:, lat + rope : lat + rope + 1] + whole[:, lat + rope + 1 : lat + rope + 2]
        latent = whole * inverse_rms(squares, D)
        q = latent[:, :Q_LAT]
        kv = latent[:, Q_LAT:lat]
        q_scale = inverse_rms(jnp.sum(q * q, axis=1, keepdims=True), Q_LAT)
        kv_scale = inverse_rms(jnp.sum(kv * kv, axis=1, keepdims=True), KV_LAT)
        q_ref[...] = (q * q_scale * qg_ref[...]).astype(jnp.bfloat16)
        kv_ref[...] = (kv * kv_scale * kg_ref[...]).astype(jnp.bfloat16)
        keys = rotate_keys(latent[:, lat : lat + rope], cos_ref[...], sin_ref[...])
        rope_ref[...] = keys.astype(jnp.bfloat16)

    return pl.pallas_call(
        body,
        out_shape=[
            jax.ShapeDtypeStruct((rows, Q_LAT), jnp.bfloat16),
            jax.ShapeDtypeStruct((rows, KV_LAT), jnp.bfloat16),
            jax.ShapeDtypeStruct((rows, rope), jnp.bfloat16),
        ],
        scratch_shapes=[pltpu.VMEM(base.shape, jnp.float32)],
        compiler_params=pltpu.CompilerParams(vmem_limit_bytes=VMEM_BYTES),
        name="finish",
    )(base, *[array for _, array in late], q_gain[None, :], kv_gain[None, :], cosine, sine_grid)


def rounds_of(pairs):
    lists = []
    for source, target in pairs:
        for chosen in lists:
            if all(source != s and target != t for s, t in chosen):
                chosen.append((source, target))
                break
        else:
            lists.append([(source, target)])
    return lists


def shards_line(
    hidden_in, embed_in, hidden_gain, embed_gain, w_hidden, w_embed, attn_gain, w_latent, q_gain, kv_gain
):
    line = lax.axis_size("dp")
    shard = hidden_in.shape[0]
    rows_out = shard // 2
    cuts = ((0, rows_out), (rows_out, shard))
    me = lax.axis_index("dp")
    mine = lax.axis_index("mp")
    last = line - 1

    def owner(s):
        return s // 2

    def device(d, m):
        return d * 2 + m

    pieces = [
        jnp.concatenate([hidden_in[low:high], embed_in[low:high]], axis=1) for low, high in cuts
    ]

    hidden_wide = hidden_in.astype(jnp.float32)
    embed_wide = embed_in.astype(jnp.float32)
    sums = jnp.stack(
        [jnp.sum(hidden_wide * hidden_wide, axis=1), jnp.sum(embed_wide * embed_wide, axis=1)], axis=1
    )
    sums = sums + lax.ppermute(sums, "mp", [(0, 1), (1, 0)])
    scale_all = inverse_rms(lax.all_gather(sums, "dp", axis=0, tiled=True), D)

    def scale_rows(s, low, high):
        return lax.dynamic_slice_in_dim(scale_all, s * shard + low, high - low, 0)

    def rows(groups, scales, own_first=None):
        return project(groups, scales, hidden_gain, embed_gain, w_hidden, w_embed, own_first)

    def to_owner(value, senders):
        pairs = [(device(d, 1 - m), device(d, m)) for d, m in senders]
        return lax.ppermute(value, ("dp", "mp"), pairs)

    def shard_of(k, d):
        return sorted({s for s in (d - k, d + k) if 0 <= s < line})

    def senders_of(k):
        return [(d, owner(s)) for d in range(line) for s in shard_of(k, d)]

    def send_latent(k, low, value):
        pairs = []
        for d in range(line):
            for s in shard_of(k, d):
                target = (s % 2) * 2 + low // rows_out
                if target != d:
                    pairs.append((device(d, owner(s)), device(target, owner(s))))
        return [lax.ppermute(value, ("dp", "mp"), chosen) for chosen in rounds_of(pairs)]

    mtp_steps = []
    own_steps = []
    early = []
    late = []
    forward = list(pieces)
    backward = list(pieces)
    got = rows([[piece] for piece in pieces], scale_rows(me, 0, shard))
    mtp, lat = latent_partial(got, to_owner(got, senders_of(0)), attn_gain, w_latent)
    mtp_steps.append(mtp)
    own_steps.append(lat)
    for low, high in cuts:
        early += [(low % rows_out, array) for array in send_latent(0, low, lat[low:high])]
    for k in range(1, line):
        forward = [lax.ppermute(x, "dp", [(i, i + 1) for i in range(k - 1, last)]) for x in forward]
        backward = [lax.ppermute(x, "dp", [(i + 1, i) for i in range(0, line - k)]) for x in backward]
        mtps = []
        lats = []
        for (low, high), ahead, back in zip(cuts, forward, backward, strict=True):
            if k < line // 2:
                first = jnp.where(me >= 1, owner(me - 1) == mine, owner(me + 1) != mine)
                scales = jnp.concatenate(
                    [
                        scale_rows(jnp.maximum(me - k, 0), low, high),
                        scale_rows(jnp.minimum(me + k, last), low, high),
                    ],
                    axis=0,
                )
                got, other = rows([[ahead], [back]], scales, first.astype(jnp.int32)[None])
            else:
                got = rows([[ahead, back]], scale_rows(jnp.where(me >= k, me - k, jnp.minimum(me + k, last)), low, high))
                other = got
            mtp, lat = latent_partial(got, to_owner(other, senders_of(k)), attn_gain, w_latent)
            mtps.append(mtp)
            lats.append(lat)
            arrays = [(low % rows_out, array) for array in send_latent(k, low, lat)]
            if k == last:
                late += arrays
            else:
                early += arrays
        mtp_steps.append(jnp.concatenate(mtps, axis=0))
        own_steps.append(jnp.concatenate(lats, axis=0) if k < last else None)

    halves = []
    for offset in range(2):
        distance = jnp.abs(me - (2 * mine + offset))
        halves.append(lax.select_n(distance, *mtp_steps))
    mtp_hidden = jnp.concatenate(halves, axis=0)

    distance = jnp.abs(me - (2 * mine + me // 2))
    whole = lax.select_n(distance, *own_steps[:-1])
    base = lax.dynamic_slice_in_dim(whole, (me % 2) * rows_out, rows_out, 0).astype(jnp.float32)
    for at, array in early:
        base = base + jnp.pad(array.astype(jnp.float32), ((at, rows_out - at - array.shape[0]), (0, 0)))
    first_token = (mine * line + me) * rows_out
    positions = (first_token + jnp.arange(rows_out, dtype=jnp.int32)) % LENGTH
    cosine, sine_grid = rope_tables(w_latent.shape[1] - Q_LAT - KV_LAT, positions)
    q_latent, kv_latent, key_rope = finish(base, late, q_gain, kv_gain, cosine, sine_grid)
    return (mtp_hidden, q_latent, kv_latent, key_rope)


def shards_any(
    hidden_in, embed_in, hidden_gain, embed_gain, w_hidden, w_embed, attn_gain, w_latent, q_gain, kv_gain
):
    hidden_wide = hidden_in.astype(jnp.float32)
    embed_wide = embed_in.astype(jnp.float32)
    entry_sums = lax.psum(
        (jnp.sum(hidden_wide * hidden_wide, axis=1), jnp.sum(embed_wide * embed_wide, axis=1)), "mp"
    )
    hidden_norm = (hidden_wide * inverse_rms(entry_sums[0], D)[:, None] * hidden_gain[None, :]).astype(jnp.bfloat16)
    embed_norm = (embed_wide * inverse_rms(entry_sums[1], D)[:, None] * embed_gain[None, :]).astype(jnp.bfloat16)
    hidden_all = lax.all_gather(hidden_norm, "dp", axis=0, tiled=True)
    embed_all = lax.all_gather(embed_norm, "dp", axis=0, tiled=True)
    tok_share = hidden_all.shape[0] // lax.axis_size("mp")
    proj_sum = lax.psum_scatter(
        (
            jnp.dot(hidden_all, w_hidden, preferred_element_type=jnp.float32)
            + jnp.dot(embed_all, w_embed, preferred_element_type=jnp.float32)
        ).astype(jnp.bfloat16),
        "mp",
        scatter_dimension=0,
        tiled=True,
    )
    mtp_hidden = lax.optimization_barrier(proj_sum)
    proj_wide = mtp_hidden.astype(jnp.float32)
    normed_rows = (proj_wide * attn_gain[None, :]).astype(jnp.bfloat16)
    partial_latent = jnp.dot(normed_rows, w_latent, preferred_element_type=jnp.float32)
    rows_out = tok_share // lax.axis_size("dp")
    square_total = lax.psum(jnp.sum(proj_wide * proj_wide, axis=1), "dp")
    latent_sum = lax.psum_scatter(
        partial_latent.astype(jnp.bfloat16), "dp", scatter_dimension=0, tiled=True
    ).astype(jnp.float32)
    first_own = lax.axis_index("dp") * rows_out
    square_sum = lax.dynamic_slice_in_dim(square_total, first_own, rows_out, 0)
    latent = latent_sum * inverse_rms(square_sum, D)[:, None]
    first_token = lax.axis_index("mp") * tok_share + first_own
    positions = (first_token + jnp.arange(rows_out, dtype=jnp.int32)) % LENGTH
    q_latent = latent_norm(latent[:, :Q_LAT], q_gain)
    kv_latent = latent_norm(latent[:, Q_LAT : Q_LAT + KV_LAT], kv_gain)
    rope_part = latent[:, Q_LAT + KV_LAT :]
    key_rope = rotate_keys(rope_part, *rope_tables(rope_part.shape[1], positions)).astype(jnp.bfloat16)
    return (mtp_hidden, q_latent, kv_latent, key_rope)


def solution(mesh):
    placed = (
        P(("branch", "dp"), "mp"),
        P(("branch", "dp"), "mp"),
        P(("branch", "mp")),
        P(("branch", "mp")),
        P(("branch", "mp"), "dp"),
        P(("branch", "mp"), "dp"),
        P(("branch", "dp")),
        P(("branch", "dp"), None),
        P("branch"),
        P("branch"),
    )
    in_line = mesh.shape["dp"] == 4 and mesh.shape["mp"] == 2
    return jax.shard_map(
        shards_line if in_line else shards_any,
        mesh=mesh,
        in_specs=placed,
        out_specs=(
            P(("branch", "mp"), "dp"),
            P(("branch", "mp", "dp"), None),
            P(("branch", "mp", "dp"), None),
            P(("branch", "mp", "dp"), None),
        ),
        check_vma=False,
    )
```

time: 275 us -> 271 us (0.985)
  waiting for transfers between devices: 202 us -> 17.4 us
  Pallas kernels: 0 us -> 130 us
  starting transfers between devices: 0.16 us -> 62.1 us
  matrix products: 33.9 us -> 0 us
  blocking collectives: 14 us -> 39.3 us
  local copies, waits for them, and re-layouts: 2.31 us -> 14.8 us
  between operations: 13.9 us -> 1.53 us
  other arithmetic: 6.9 us -> 2.63 us
    pallas_call x0 -> x15, Pallas kernels: none -> 130 us  [the longest x7 83.3 us: project(): pl.pallas_call(body, grid=(steps,), in_specs=in_specs, out_specs=[pl.Bloc...]
    all_gather x2 -> x0, waiting for transfers between devices: 128 us -> none  [the longest x1 69.5 us: shards(): hidden_all = lax.all_gather(hidden_norm, 'dp', axis=0, tiled=True)]
    ppermute x0 -> x30, starting transfers between devices: none -> 62.1 us  [the longest x6 16.9 us: shards_line(): lax.ppermute(x, 'dp', [(i, i + 1) for i in range(k - 1, last)])]
    psum x1 -> x0, waiting for transfers between devices: 43.5 us -> none  [shards(): lax.psum(partial_latent.astype(jnp.bfloat16), 'dp').astype(jnp.float32)]
    all_gather x0 -> x1, blocking collectives: none -> 39.3 us  [shards_line(): scale_all = inverse_rms(lax.all_gather(sums, 'dp', axis=0, tiled=True), D)]
    dot_general x3 -> x0, matrix products: 33.9 us -> none  [the longest x1 13.7 us: shards(): jnp.dot(embed_all, w_proj_embed, preferred_element_type=jnp.float32)]
    reduce_scatter x1 -> x0, waiting for transfers between devices: 30.3 us -> none  [shards(): lax.psum_scatter((jnp.dot(hidden_all, w_proj_hidden, preferred_element_ty...]
    ppermute x0 -> x30, waiting for transfers between devices: none -> 17.4 us  [the longest x10 12.1 us: send_latent(): lax.ppermute(value, ('dp', 'mp'), chosen)]
  transfers between devices with their start and end apart: 4 -> 30, of which waited for: 4 -> 4; matrix products, arithmetic and copies ran while one was open for 6% -> 6% of each run, Pallas kernels for 0% -> 48%
where the time goes in v1:
time: 271 us; the launch traced here: 268 us
  Pallas kernels  130 us (48%)
  starting transfers between devices  62.1 us (23%)
  blocking collectives  39.3 us (15%)
  waiting for transfers between devices  17.4 us (6%)
  local copies, waits for them, and re-layouts  14.8 us (5%)
    pallas_call x7, Pallas kernels, project(): pl.pallas_call(body, grid=(steps,), in_specs=in_specs, out_specs=[pl.Bloc...  83.3 us
    pallas_call x7, Pallas kernels, latent_partial(): pl.pallas_call(body, grid=(steps,), in_specs=[pl.BlockSpec((rows, step),...  45.9 us
    all_gather x1, blocking collectives, shards_line(): scale_all = inverse_rms(lax.all_gather(sums, 'dp', axis=0, tiled=True), D)  39.3 us
    ppermute x6, starting transfers between devices, shards_line(): lax.ppermute(x, 'dp', [(i, i + 1) for i in range(k - 1, last)])  16.9 us
    ppermute x7, starting transfers between devices, to_owner(): return lax.ppermute(value, ('dp', 'mp'), pairs)  16.7 us
    ppermute x6, starting transfers between devices, shards_line(): lax.ppermute(x, 'dp', [(i + 1, i) for i in range(0, line - k)])  15.9 us
    unnamed x20, local copies, waits for them, and re-layouts  12.1 us
    ppermute x10, waiting for transfers between devices, send_latent(): lax.ppermute(value, ('dp', 'mp'), chosen)  12.1 us
  transfers between devices with their start and end apart: 30, of which 4 were waited for; matrix products, arithmetic and copies ran while one was open for 6% of the time, Pallas kernels for 48%

profile of v1, /device:TPU:8, one launch (start us, length us, event | category | flops | bytes accessed | tf_op | source)
XLA Modules:
  0.0 268.0 jit_solution(18423191817152632355)
XLA Ops:
  0.6 1.6 fusion.6
  2.3 2.1 collective-permute-start.3
  4.3 3.9 %collective-permute-start.2 = (bf16[64,7168]{1,0:T(8,128)(2,1)S(1)}, bf16[64,7168]{1,0:T(8,128)(2,1)}, u32[]{:S(2)}, u32[]{:S(2)}) collective-permute-start(bf16[64,7168]{1,0:T(8,128)(2,1)S(1)} %pad_maximum_fusion.refs_0_.refs_2_), channel_id=1, source_target_pairs={{0,2},{2,4},{4,6},{1,3},{3,5},{5,7},{8,10},{10,12},{12,14},{9,11},... | collective-permute-start | bytes 2752520 | tf_op jit(solution)/shard_map/ppermute | solution.py:329
  8.4 2.9 %collective-permute-start.6 = (bf16[64,7168]{1,0:T(8,128)(2,1)S(1)}, bf16[64,7168]{1,0:T(8,128)(2,1)}, u32[]{:S(2)}, u32[]{:S(2)}) collective-permute-start(bf16[64,7168]{1,0:T(8,128)(2,1)S(1)} %pad_maximum_fusion.1.refs_1_.refs_3_), channel_id=1, source_target_pairs={{2,0},{4,2},{6,4},{3,1},{5,3},{7,5},{10,8},{12,10},{14,12},{11,9},... | collective-permute-start | bytes 2752520 | tf_op jit(solution)/shard_map/ppermute | solution.py:330
  11.3 3.4 %collective-permute-start.5 = (bf16[64,7168]{1,0:T(8,128)(2,1)S(1)}, bf16[64,7168]{1,0:T(8,128)(2,1)S(1)}, u32[]{:S(2)}, u32[]{:S(2)}) collective-permute-start(bf16[64,7168]{1,0:T(8,128)(2,1)S(1)} %pad_maximum_fusion.1.refs_1_.refs_3_), channel_id=1, source_target_pairs={{0,2},{2,4},{4,6},{1,3},{3,5},{5,7},{8,10},{10,12},{12,14},{9,11},... | collective-permute-start | bytes 2752520 | tf_op jit(solution)/shard_map/ppermute | solution.py:329
  15.4 1.6 collective-permute-start
  17.0 2.7 collective-permute-done
  19.7 39.3 %all_gather.3 = f32[512,2]{1,0:T(8,128)S(1)} all-gather(f32[128,2]{1,0:T(8,128)S(1)} %add.136), channel_id=1, replica_groups=mesh['branch'=4,'dp'=4,'mp'=2] {'dp'}, dimensions={0}, use_global_device_ids=true | all-gather | bytes 5120 | tf_op jit(solution)/shard_map/all_gather | solution.py:289
  59.8 11.6 %project.7.own_ref = bf16[128,1792]{1,0:T(8,128)(2,1)S(1)} custom-call(bf16[64,7168]{1,0:T(8,128)(2,1)S(1)} %pad_maximum_fusion.refs_0_.refs_2_, bf16[64,7168]{1,0:T(8,128)(2,1)S(1)} %pad_maximum_fusion.1.refs_1_.refs_3_, bf16[64,7168]{1,0:T(8,128)(2,1)S(1)} %pad_maximum_fusion.refs_0_.refs_2_, bf16[64,7168]{1,0:T(8,128)(2,1)S(1)} %pad_maximum_fusion.1.refs_1_.refs_3_, ...), custom_call_target="tpu_custom_call" | custom-call | flops 3288334336 | bytes 25690112 | tf_op jit(solution)/shard_map/project/pallas_call | solution.py:125
  71.4 1.3 collective-permute-start.1
  73.1 11.3 %copy.40.w_ref = bf16[1792,2112]{1,0:T(8,128)(2,1)} copy(bf16[1792,2112]{0,1:T(8,128)(2,1)} %param.17) | data formatting | bytes 15138816 | tf_op args[7]
  84.4 0.9 constant_dynamic-slice_fusion.5
  85.3 6.8 %latent_partial.7 = (bf16[128,1792]{1,0:T(8,128)(2,1)S(1)}, bf16[128,2176]{1,0:T(8,128)(2,1)S(1)}) custom-call(bf16[128,1792]{1,0:T(8,128)(2,1)S(1)} %project.7.own_ref, bf16[128,1792]{1,0:T(8,128)(2,1)} %collective-permute-done.1.received_ref, f32[1,1792]{1,0:T(1,128)S(1)} %broadcast_in_dim.16.gain_ref, bf16[1792,2112]{1,0:T(8,128)(2,1)} %copy.40.w_ref), custom_call_target="tpu_custom_call" | custom-call | flops 968884224 | bytes 7569408 | tf_op jit(solution)/shard_map/latent_partial/pallas_call | solution.py:185
  92.1 11.8 %project.9 = (bf16[64,1792]{1,0:T(8,128)(2,1)S(1)}, bf16[64,1792]{1,0:T(8,128)(2,1)S(1)}) custom-call(s32[1]{0:T(128)} %bitcast.2.refs_0_, bf16[64,7168]{1,0:T(8,128)(2,1)S(1)} %collective-permute-done.5.refs_1_.refs_3_, bf16[64,7168]{1,0:T(8,128)(2,1)} %collective-permute-done.6.refs_2_.refs_4_, ...), custom_call_target="tpu_custom_call" | custom-call | flops 3288334336 | bytes 25690112 | tf_op jit(solution)/shard_map/project/pallas_call | solution.py:125
  104.0 5.3 %collective-permute-start.7 = (bf16[64,1792]{1,0:T(8,128)(2,1)S(1)}, bf16[64,1792]{1,0:T(8,128)(2,1)S(1)}, u32[]{:S(2)}, u32[]{:S(2)}) collective-permute-start(bf16[64,1792]{1,0:T(8,128)(2,1)S(1)} %get-tuple-element.30), channel_id=1, source_target_pairs={{1,0},{3,2},{2,3},{5,4},{4,5},{6,7},{9,8},{11,10},{10,11},{13,12},... | collective-permute-start | bytes 688136 | tf_op jit(solution)/shard_map/ppermute | solution.py:299
  109.3 12.0 %project.8 = (bf16[64,1792]{1,0:T(8,128)(2,1)S(1)}, bf16[64,1792]{1,0:T(8,128)(2,1)S(1)}) custom-call(s32[1]{0:T(128)} %bitcast.2.refs_0_, bf16[64,7168]{1,0:T(8,128)(2,1)} %collective-permute-done.2.refs_1_.refs_3_, bf16[64,7168]{1,0:T(8,128)(2,1)} %collective-permute-done.3.refs_2_.refs_4_, bf16[64,7168]{1,0:T(8,128)(2,1)} %collective-permute-done.2.refs_1_.refs_3_, ...), custom_call_target="tpu_custom_call" | custom-call | flops 3288334336 | bytes 25690112 | tf_op jit(solution)/shard_map/project/pallas_call | solution.py:125
  121.3 1.9 collective-permute-start.4
  123.2 1.9 collective-permute-start.9
  125.1 4.0 %collective-permute-start.8 = (bf16[64,7168]{1,0:T(8,128)(2,1)}, bf16[64,7168]{1,0:T(8,128)(2,1)S(1)}, u32[]{:S(2)}, u32[]{:S(2)}) collective-permute-start(bf16[64,7168]{1,0:T(8,128)(2,1)} %collective-permute-done.2.refs_1_.refs_3_), channel_id=1, source_target_pairs={{2,4},{4,6},{3,5},{5,7},{10,12},{12,14},{11,13},{13,15},{18,20},{2... | collective-permute-start | bytes 2752520 | tf_op jit(solution)/shard_map/ppermute | solution.py:329
  129.2 1.9 collective-permute-start.12
  131.1 4.0 %collective-permute-start.11 = (bf16[64,7168]{1,0:T(8,128)(2,1)S(1)}, bf16[64,7168]{1,0:T(8,128)(2,1)S(1)}, u32[]{:S(2)}, u32[]{:S(2)}) collective-permute-start(bf16[64,7168]{1,0:T(8,128)(2,1)S(1)} %collective-permute-done.5.refs_1_.refs_3_), channel_id=1, source_target_pairs={{2,4},{4,6},{3,5},{5,7},{10,12},{12,14},{11,13},{13,15},{18,20},{2... | collective-permute-start | bytes 2752520 | tf_op jit(solution)/shard_map/ppermute | solution.py:329
  135.2 6.5 %latent_partial.9 = (bf16[64,1792]{1,0:T(8,128)(2,1)S(1)}, bf16[64,2176]{1,0:T(8,128)(2,1)S(1)}) custom-call(bf16[64,1792]{1,0:T(8,128)(2,1)S(1)} %get-tuple-element.29.own_ref, bf16[64,1792]{1,0:T(8,128)(2,1)S(1)} %collective-permute-done.7.received_ref, f32[1,1792]{1,0:T(1,128)S(1)} %broadcast_in_dim.16.gain_ref, bf16[1792,2112]{1,0:T(8,128)(2,1)} %copy.40.w_ref), custom_call_target="tpu_custom_call" | custom-call | flops 484442112 | bytes 7569408 | tf_op jit(solution)/shard_map/latent_partial/pallas_call | solution.py:185
  141.7 1.9 collective-permute-start.20
  143.6 6.5 %latent_partial.8 = (bf16[64,1792]{1,0:T(8,128)(2,1)S(1)}, bf16[64,2176]{1,0:T(8,128)(2,1)S(1)}) custom-call(bf16[64,1792]{1,0:T(8,128)(2,1)S(1)} %get-tuple-element.26.own_ref, bf16[64,1792]{1,0:T(8,128)(2,1)S(1)} %collective-permute-done.4.received_ref, f32[1,1792]{1,0:T(1,128)S(1)} %broadcast_in_dim.16.gain_ref, bf16[1792,2112]{1,0:T(8,128)(2,1)} %copy.40.w_ref), custom_call_target="tpu_custom_call" | custom-call | flops 484442112 | bytes 7569408 | tf_op jit(solution)/shard_map/latent_partial/pallas_call | solution.py:185
  150.2 1.9 collective-permute-start.21
  152.1 12.0 %project.10.own_ref = bf16[64,1792]{1,0:T(8,128)(2,1)S(1)} custom-call(bf16[64,7168]{1,0:T(8,128)(2,1)S(1)} %collective-permute-done.8.refs_0_.refs_2_, bf16[64,7168]{1,0:T(8,128)(2,1)S(1)} %collective-permute-done.9.refs_1_.refs_3_, bf16[64,7168]{1,0:T(8,128)(2,1)S(1)} %collective-permute-done.8.refs_0_.refs_2_, ...), custom_call_target="tpu_custom_call" | custom-call | flops 1644167168 | bytes 25690112 | tf_op jit(solution)/shard_map/project/pallas_call | solution.py:125
  164.1 2.1 collective-permute-start.10
  166.2 3.2 %collective-permute-start.15 = (bf16[64,7168]{1,0:T(8,128)(2,1)S(1)}, bf16[64,7168]{1,0:T(8,128)(2,1)S(1)}, u32[]{:S(2)}, u32[]{:S(2)}) collective-permute-start(bf16[64,7168]{1,0:T(8,128)(2,1)S(1)} %collective-permute-done.9.refs_1_.refs_3_), channel_id=1, source_target_pairs={{2,0},{3,1},{10,8},{11,9},{18,16},{19,17},{26,24},{27,25}} | collective-permute-start | bytes 2752520 | tf_op jit(solution)/shard_map/ppermute | solution.py:330
  169.4 0.7 collective-permute-start.14
  170.2 12.0 %project.11.own_ref = bf16[64,1792]{1,0:T(8,128)(2,1)S(1)} custom-call(bf16[64,7168]{1,0:T(8,128)(2,1)S(1)} %collective-permute-done.11.refs_0_.refs_2_, bf16[64,7168]{1,0:T(8,128)(2,1)S(1)} %collective-permute-done.12.refs_1_.refs_3_, bf16[64,7168]{1,0:T(8,128)(2,1)S(1)} %collective-permute-done.11.refs_0_.refs_2_, ...), custom_call_target="tpu_custom_call" | custom-call | flops 1644167168 | bytes 25690112 | tf_op jit(solution)/shard_map/project/pallas_call | solution.py:125
  182.2 4.6 %collective-permute-start.13 = (bf16[64,1792]{1,0:T(8,128)(2,1)S(1)}, bf16[64,1792]{1,0:T(8,128)(2,1)S(1)}, u32[]{:S(2)}, u32[]{:S(2)}) collective-permute-start(bf16[64,1792]{1,0:T(8,128)(2,1)S(1)} %project.11.own_ref), channel_id=1, source_target_pairs={{0,1},{2,3},{5,4},{7,6},{8,9},{10,11},{13,12},{15,14},{16,17},{18,... | collective-permute-start | bytes 688136 | tf_op jit(solution)/shard_map/ppermute | solution.py:299
  187.5 1.3 collective-permute-start.22
  188.8 1.5 collective-permute-done.13.received_ref
  191.0 6.5 %latent_partial.11 = (bf16[64,1792]{1,0:T(8,128)(2,1)S(1)}, bf16[64,2176]{1,0:T(8,128)(2,1)S(1)}) custom-call(bf16[64,1792]{1,0:T(8,128)(2,1)S(1)} %project.11.own_ref, bf16[64,1792]{1,0:T(8,128)(2,1)S(1)} %collective-permute-done.13.received_ref, f32[1,1792]{1,0:T(1,128)S(1)} %broadcast_in_dim.16.gain_ref, bf16[1792,2112]{1,0:T(8,128)(2,1)} %copy.40.w_ref), custom_call_target="tpu_custom_call" | custom-call | flops 484442112 | bytes 7569408 | tf_op jit(solution)/shard_map/latent_partial/pallas_call | solution.py:185
  197.5 6.5 %latent_partial.10 = (bf16[64,1792]{1,0:T(8,128)(2,1)S(1)}, bf16[64,2176]{1,0:T(8,128)(2,1)S(1)}) custom-call(bf16[64,1792]{1,0:T(8,128)(2,1)S(1)} %project.10.own_ref, bf16[64,1792]{1,0:T(8,128)(2,1)S(1)} %collective-permute-done.10.received_ref, f32[1,1792]{1,0:T(1,128)S(1)} %broadcast_in_dim.16.gain_ref, bf16[1792,2112]{1,0:T(8,128)(2,1)} %copy.40.w_ref), custom_call_target="tpu_custom_call" | custom-call | flops 484442112 | bytes 7569408 | tf_op jit(solution)/shard_map/latent_partial/pallas_call | solution.py:185
  205.4 1.3 collective-permute-start.27
  206.8 3.9 %collective-permute-start.18 = (bf16[64,7168]{1,0:T(8,128)(2,1)S(1)}, bf16[64,7168]{1,0:T(8,128)(2,1)S(1)}, u32[]{:S(2)}, u32[]{:S(2)}) collective-permute-start(bf16[64,7168]{1,0:T(8,128)(2,1)S(1)} %collective-permute-done.12.refs_1_.refs_3_), channel_id=1, source_target_pairs={{2,0},{3,1},{10,8},{11,9},{18,16},{19,17},{26,24},{27,25}} | collective-permute-start | bytes 2752520 | tf_op jit(solution)/shard_map/ppermute | solution.py:330
  210.7 0.7 collective-permute-start.17
  211.4 12.0 %project.12.own_ref = bf16[64,1792]{1,0:T(8,128)(2,1)S(1)} custom-call(bf16[64,7168]{1,0:T(8,128)(2,1)S(1)} %collective-permute-done.14.refs_0_.refs_2_, bf16[64,7168]{1,0:T(8,128)(2,1)S(1)} %collective-permute-done.15.refs_1_.refs_3_, bf16[64,7168]{1,0:T(8,128)(2,1)S(1)} %collective-permute-done.14.refs_0_.refs_2_, ...), custom_call_target="tpu_custom_call" | custom-call | flops 1644167168 | bytes 25690112 | tf_op jit(solution)/shard_map/project/pallas_call | solution.py:125
  223.4 0.9 collective-permute-start.16
  224.9 1.2 collective-permute-done.18.refs_1_.refs_3_
  226.0 11.9 %project.13.own_ref = bf16[64,1792]{1,0:T(8,128)(2,1)S(1)} custom-call(bf16[64,7168]{1,0:T(8,128)(2,1)S(1)} %collective-permute-done.17.refs_0_.refs_2_, bf16[64,7168]{1,0:T(8,128)(2,1)S(1)} %collective-permute-done.18.refs_1_.refs_3_, bf16[64,7168]{1,0:T(8,128)(2,1)S(1)} %collective-permute-done.17.refs_0_.refs_2_, ...), custom_call_target="tpu_custom_call" | custom-call | flops 1644167168 | bytes 25690112 | tf_op jit(solution)/shard_map/project/pallas_call | solution.py:125
  238.7 6.5 %latent_partial.12 = (bf16[64,1792]{1,0:T(8,128)(2,1)S(1)}, bf16[64,2176]{1,0:T(8,128)(2,1)S(1)}) custom-call(bf16[64,1792]{1,0:T(8,128)(2,1)S(1)} %project.12.own_ref, bf16[64,1792]{1,0:T(8,128)(2,1)S(1)} %collective-permute-done.16.received_ref, f32[1,1792]{1,0:T(1,128)S(1)} %broadcast_in_dim.16.gain_ref, bf16[1792,2112]{1,0:T(8,128)(2,1)} %copy.40.w_ref), custom_call_target="tpu_custom_call" | custom-call | flops 484442112 | bytes 7569408 | tf_op jit(solution)/shard_map/latent_partial/pallas_call | solution.py:185
  245.9 6.5 %latent_partial.13 = (bf16[64,1792]{1,0:T(8,128)(2,1)S(1)}, bf16[64,2176]{1,0:T(8,128)(2,1)S(1)}) custom-call(bf16[64,1792]{1,0:T(8,128)(2,1)S(1)} %project.13.own_ref, bf16[64,1792]{1,0:T(8,128)(2,1)S(1)} %collective-permute-done.19.received_ref, f32[1,1792]{1,0:T(1,128)S(1)} %broadcast_in_dim.16.gain_ref, bf16[1792,2112]{1,0:T(8,128)(2,1)} %copy.40.w_ref), custom_call_target="tpu_custom_call" | custom-call | flops 484442112 | bytes 7569408 | tf_op jit(solution)/shard_map/latent_partial/pallas_call | solution.py:185
  252.5 1.3 collective-permute-start.29
  253.9 1.0 pad_maximum_fusion.2
  254.9 12.0 %collective-permute-done.29.refs_1_ = bf16[64,2176]{1,0:T(8,128)(2,1)S(1)} collective-permute-done((bf16[64,2176]{1,0:T(8,128)(2,1)S(1)}, bf16[64,2176]{1,0:T(8,128)(2,1)S(1)}, u32[]{:S(2)}, u32[]{:S(2)}) %collective-permute-start.29) | collective-permute-done | bytes 278560 | tf_op jit(solution)/shard_map/ppermute | solution.py:314
  266.9 1.0 finish.1
  (75 shorter events, 6.8 us)
Async XLA Ops:
  2.2 12.5 %copy-start.1 = (bf16[128,3584]{1,0:T(8,128)(2,1)S(1)}, bf16[128,3584]{1,0:T(8,128)(2,1)}, u32[]{:S(2)}) copy-start(bf16[128,3584]{1,0:T(8,128)(2,1)} %param.10) | copy-start | bytes 2752516
  2.3 12.7 %copy-start.2 = (bf16[128,3584]{1,0:T(8,128)(2,1)S(1)}, bf16[128,3584]{1,0:T(8,128)(2,1)}, u32[]{:S(2)}) copy-start(bf16[128,3584]{1,0:T(8,128)(2,1)} %param.11) | copy-start | bytes 2752516
  2.3 107.0 %collective-permute-start.3 = (bf16[64,7168]{1,0:T(8,128)(2,1)S(1)}, bf16[64,7168]{1,0:T(8,128)(2,1)}, u32[]{:S(2)}, u32[]{:S(2)}) collective-permute-start(bf16[64,7168]{1,0:T(8,128)(2,1)S(1)} %pad_maximum_fusion.refs_0_.refs_2_), channel_id=1, source_target_pairs={{2,0},{4,2},{6,4},{3,1},{5,3},{7,5},{10,8},{12,10},{14,12},{11,9},... | collective-permute-start | bytes 2752520 | tf_op jit(solution)/shard_map/ppermute | solution.py:330
  4.3 104.9 %collective-permute-start.2 = (bf16[64,7168]{1,0:T(8,128)(2,1)S(1)}, bf16[64,7168]{1,0:T(8,128)(2,1)}, u32[]{:S(2)}, u32[]{:S(2)}) collective-permute-start(bf16[64,7168]{1,0:T(8,128)(2,1)S(1)} %pad_maximum_fusion.refs_0_.refs_2_), channel_id=1, source_target_pairs={{0,2},{2,4},{4,6},{1,3},{3,5},{5,7},{8,10},{10,12},{12,14},{9,11},... | collective-permute-start | bytes 2752520 | tf_op jit(solution)/shard_map/ppermute | solution.py:329
  8.3 8.7 %copy-start.4 = (f32[3584]{0:T(1024)S(1)}, f32[3584]{0:T(1024)}, u32[]{:S(2)}) copy-start(f32[3584]{0:T(1024)} %param.12) | copy-start | bytes 43012
  8.3 8.7 %copy-start.5 = (f32[3584]{0:T(1024)S(1)}, f32[3584]{0:T(1024)}, u32[]{:S(2)}) copy-start(f32[3584]{0:T(1024)} %param.13) | copy-start | bytes 43012
  8.4 83.7 %collective-permute-start.6 = (bf16[64,7168]{1,0:T(8,128)(2,1)S(1)}, bf16[64,7168]{1,0:T(8,128)(2,1)}, u32[]{:S(2)}, u32[]{:S(2)}) collective-permute-start(bf16[64,7168]{1,0:T(8,128)(2,1)S(1)} %pad_maximum_fusion.1.refs_1_.refs_3_), channel_id=1, source_target_pairs={{2,0},{4,2},{6,4},{3,1},{5,3},{7,5},{10,8},{12,10},{14,12},{11,9},... | collective-permute-start | bytes 2752520 | tf_op jit(solution)/shard_map/ppermute | solution.py:330
  11.3 80.8 %collective-permute-start.5 = (bf16[64,7168]{1,0:T(8,128)(2,1)S(1)}, bf16[64,7168]{1,0:T(8,128)(2,1)S(1)}, u32[]{:S(2)}, u32[]{:S(2)}) collective-permute-start(bf16[64,7168]{1,0:T(8,128)(2,1)S(1)} %pad_maximum_fusion.1.refs_1_.refs_3_), channel_id=1, source_target_pairs={{0,2},{2,4},{4,6},{1,3},{3,5},{5,7},{8,10},{10,12},{12,14},{9,11},... | collective-permute-start | bytes 2752520 | tf_op jit(solution)/shard_map/ppermute | solution.py:329
  15.4 4.3 %collective-permute-start = (f32[128,2]{1,0:T(8,128)S(1)}, f32[128,2]{1,0:T(8,128)S(1)}, u32[]{:S(2)}, u32[]{:S(2)}) collective-permute-start(f32[128,2]{1,0:T(8,128)S(1)} %copy.39), channel_id=1, source_target_pairs={{0,1},{1,0},{2,3},{3,2},{4,5},{5,4},{6,7},{7,6},{8,9},{9,8},{10,11... | collective-permute-start | bytes 3080 | tf_op jit(solution)/shard_map/ppermute | solution.py:288
  59.0 0.7 copy-start.3
  59.7 13.3 %copy-start.6 = (f32[1536]{0:T(1024)S(1)}, f32[1536]{0:T(1024)}, u32[]{:S(2)}) copy-start(f32[1536]{0:T(1024)} %param.18) | copy-start | bytes 18436
  59.7 13.3 %copy-start.7 = (f32[1792]{0:T(1024)S(1)}, f32[1792]{0:T(1024)}, u32[]{:S(2)}) copy-start(f32[1792]{0:T(1024)} %param.16) | copy-start | bytes 21508
  71.4 13.9 %collective-permute-start.1 = (bf16[128,1792]{1,0:T(8,128)(2,1)S(1)}, bf16[128,1792]{1,0:T(8,128)(2,1)}, u32[]{:S(2)}, u32[]{:S(2)}) collective-permute-start(bf16[128,1792]{1,0:T(8,128)(2,1)S(1)} %project.7.own_ref), channel_id=1, source_target_pairs={{1,0},{3,2},{4,5},{6,7},{9,8},{11,10},{12,13},{14,15},{17,16},{19,... | collective-permute-start | bytes 1376264 | tf_op jit(solution)/shard_map/ppermute | solution.py:299
  104.0 27.1 %collective-permute-start.7 = (bf16[64,1792]{1,0:T(8,128)(2,1)S(1)}, bf16[64,1792]{1,0:T(8,128)(2,1)S(1)}, u32[]{:S(2)}, u32[]{:S(2)}) collective-permute-start(bf16[64,1792]{1,0:T(8,128)(2,1)S(1)} %get-tuple-element.30), channel_id=1, source_target_pairs={{1,0},{3,2},{2,3},{5,4},{4,5},{6,7},{9,8},{11,10},{10,11},{13,12},... | collective-permute-start | bytes 688136 | tf_op jit(solution)/shard_map/ppermute | solution.py:299
  121.3 20.5 %collective-permute-start.4 = (bf16[64,1792]{1,0:T(8,128)(2,1)S(1)}, bf16[64,1792]{1,0:T(8,128)(2,1)S(1)}, u32[]{:S(2)}, u32[]{:S(2)}) collective-permute-start(bf16[64,1792]{1,0:T(8,128)(2,1)S(1)} %get-tuple-element.27), channel_id=1, source_target_pairs={{1,0},{3,2},{2,3},{5,4},{4,5},{6,7},{9,8},{11,10},{10,11},{13,12},... | collective-permute-start | bytes 688136 | tf_op jit(solution)/shard_map/ppermute | solution.py:299
  123.2 27.0 %collective-permute-start.9 = (bf16[64,7168]{1,0:T(8,128)(2,1)}, bf16[64,7168]{1,0:T(8,128)(2,1)S(1)}, u32[]{:S(2)}, u32[]{:S(2)}) collective-permute-start(bf16[64,7168]{1,0:T(8,128)(2,1)} %collective-permute-done.3.refs_2_.refs_4_), channel_id=1, source_target_pairs={{2,0},{4,2},{3,1},{5,3},{10,8},{12,10},{11,9},{13,11},{18,16},{20,... | collective-permute-start | bytes 2752520 | tf_op jit(solution)/shard_map/ppermute | solution.py:330
  125.1 27.0 %collective-permute-start.8 = (bf16[64,7168]{1,0:T(8,128)(2,1)}, bf16[64,7168]{1,0:T(8,128)(2,1)S(1)}, u32[]{:S(2)}, u32[]{:S(2)}) collective-permute-start(bf16[64,7168]{1,0:T(8,128)(2,1)} %collective-permute-done.2.refs_1_.refs_3_), channel_id=1, source_target_pairs={{2,4},{4,6},{3,5},{5,7},{10,12},{12,14},{11,13},{13,15},{18,20},{2... | collective-permute-start | bytes 2752520 | tf_op jit(solution)/shard_map/ppermute | solution.py:329
  129.2 37.0 %collective-permute-start.12 = (bf16[64,7168]{1,0:T(8,128)(2,1)}, bf16[64,7168]{1,0:T(8,128)(2,1)S(1)}, u32[]{:S(2)}, u32[]{:S(2)}) collective-permute-start(bf16[64,7168]{1,0:T(8,128)(2,1)} %collective-permute-done.6.refs_2_.refs_4_), channel_id=1, source_target_pairs={{2,0},{4,2},{3,1},{5,3},{10,8},{12,10},{11,9},{13,11},{18,16},{20,... | collective-permute-start | bytes 2752520 | tf_op jit(solution)/shard_map/ppermute | solution.py:330
  131.1 38.3 %collective-permute-start.11 = (bf16[64,7168]{1,0:T(8,128)(2,1)S(1)}, bf16[64,7168]{1,0:T(8,128)(2,1)S(1)}, u32[]{:S(2)}, u32[]{:S(2)}) collective-permute-start(bf16[64,7168]{1,0:T(8,128)(2,1)S(1)} %collective-permute-done.5.refs_1_.refs_3_), channel_id=1, source_target_pairs={{2,4},{4,6},{3,5},{5,7},{10,12},{12,14},{11,13},{13,15},{18,20},{2... | collective-permute-start | bytes 2752520 | tf_op jit(solution)/shard_map/ppermute | solution.py:329
  141.7 40.4 %collective-permute-start.20 = (bf16[64,2176]{1,0:T(8,128)(2,1)S(1)}, bf16[64,2176]{1,0:T(8,128)(2,1)S(1)}, u32[]{:S(2)}, u32[]{:S(2)}) collective-permute-start(bf16[64,2176]{1,0:T(8,128)(2,1)S(1)} %get-tuple-element.52), channel_id=1, source_target_pairs={{2,4},{5,1},{7,5},{10,12},{13,9},{15,13},{18,20},{21,17},{23,21},{... | collective-permute-start | bytes 835592 | tf_op jit(solution)/shard_map/ppermute | solution.py:314
  150.2 36.6 %collective-permute-start.21 = (bf16[64,2176]{1,0:T(8,128)(2,1)S(1)}, bf16[64,2176]{1,0:T(8,128)(2,1)S(1)}, u32[]{:S(2)}, u32[]{:S(2)}) collective-permute-start(bf16[64,2176]{1,0:T(8,128)(2,1)S(1)} %get-tuple-element.53), channel_id=1, source_target_pairs={{0,2},{2,6},{5,3},{8,10},{10,14},{13,11},{16,18},{18,22},{21,19},{... | collective-permute-start | bytes 835592 | tf_op jit(solution)/shard_map/ppermute | solution.py:314
  164.1 23.4 %collective-permute-start.10 = (bf16[64,1792]{1,0:T(8,128)(2,1)S(1)}, bf16[64,1792]{1,0:T(8,128)(2,1)S(1)}, u32[]{:S(2)}, u32[]{:S(2)}) collective-permute-start(bf16[64,1792]{1,0:T(8,128)(2,1)S(1)} %project.10.own_ref), channel_id=1, source_target_pairs={{0,1},{2,3},{5,4},{7,6},{8,9},{10,11},{13,12},{15,14},{16,17},{18,... | collective-permute-start | bytes 688136 | tf_op jit(solution)/shard_map/ppermute | solution.py:299
  166.2 40.6 %collective-permute-start.15 = (bf16[64,7168]{1,0:T(8,128)(2,1)S(1)}, bf16[64,7168]{1,0:T(8,128)(2,1)S(1)}, u32[]{:S(2)}, u32[]{:S(2)}) collective-permute-start(bf16[64,7168]{1,0:T(8,128)(2,1)S(1)} %collective-permute-done.9.refs_1_.refs_3_), channel_id=1, source_target_pairs={{2,0},{3,1},{10,8},{11,9},{18,16},{19,17},{26,24},{27,25}} | collective-permute-start | bytes 2752520 | tf_op jit(solution)/shard_map/ppermute | solution.py:330
  169.4 41.2 %collective-permute-start.14 = (bf16[64,7168]{1,0:T(8,128)(2,1)S(1)}, bf16[64,7168]{1,0:T(8,128)(2,1)S(1)}, u32[]{:S(2)}, u32[]{:S(2)}) collective-permute-start(bf16[64,7168]{1,0:T(8,128)(2,1)S(1)} %collective-permute-done.8.refs_0_.refs_2_), channel_id=1, source_target_pairs={{4,6},{5,7},{12,14},{13,15},{20,22},{21,23},{28,30},{29,31}} | collective-permute-start | bytes 2752520 | tf_op jit(solution)/shard_map/ppermute | solution.py:329
  182.2 8.1 %collective-permute-start.13 = (bf16[64,1792]{1,0:T(8,128)(2,1)S(1)}, bf16[64,1792]{1,0:T(8,128)(2,1)S(1)}, u32[]{:S(2)}, u32[]{:S(2)}) collective-permute-start(bf16[64,1792]{1,0:T(8,128)(2,1)S(1)} %project.11.own_ref), channel_id=1, source_target_pairs={{0,1},{2,3},{5,4},{7,6},{8,9},{10,11},{13,12},{15,14},{16,17},{18,... | collective-permute-start | bytes 688136 | tf_op jit(solution)/shard_map/ppermute | solution.py:299
  186.8 17.2 %collective-permute-start.23 = (bf16[64,2176]{1,0:T(8,128)(2,1)S(1)}, bf16[64,2176]{1,0:T(8,128)(2,1)S(1)}, u32[]{:S(2)}, u32[]{:S(2)}) collective-permute-start(bf16[64,2176]{1,0:T(8,128)(2,1)S(1)} %get-tuple-element.37), channel_id=1, source_target_pairs={{7,1},{15,9},{23,17},{31,25}} | collective-permute-start | bytes 835592 | tf_op jit(solution)/shard_map/ppermute | solution.py:314
  187.5 17.2 %collective-permute-start.22 = (bf16[64,2176]{1,0:T(8,128)(2,1)S(1)}, bf16[64,2176]{1,0:T(8,128)(2,1)S(1)}, u32[]{:S(2)}, u32[]{:S(2)}) collective-permute-start(bf16[64,2176]{1,0:T(8,128)(2,1)S(1)} %get-tuple-element.37), channel_id=1, source_target_pairs={{0,4},{2,0},{3,1},{8,12},{10,8},{11,9},{16,20},{18,16},{19,17},{24... | collective-permute-start | bytes 835592 | tf_op jit(solution)/shard_map/ppermute | solution.py:314
  190.3 15.1 %collective-permute-start.25 = (bf16[64,2176]{1,0:T(8,128)(2,1)S(1)}, bf16[64,2176]{1,0:T(8,128)(2,1)S(1)}, u32[]{:S(2)}, u32[]{:S(2)}) collective-permute-start(bf16[64,2176]{1,0:T(8,128)(2,1)S(1)} %get-tuple-element.38), channel_id=1, source_target_pairs={{4,6},{12,14},{20,22},{28,30}} | collective-permute-start | bytes 835592 | tf_op jit(solution)/shard_map/ppermute | solution.py:314
  204.1 19.3 %collective-permute-start.24 = (bf16[64,2176]{1,0:T(8,128)(2,1)S(1)}, bf16[64,2176]{1,0:T(8,128)(2,1)S(1)}, u32[]{:S(2)}, u32[]{:S(2)}) collective-permute-start(bf16[64,2176]{1,0:T(8,128)(2,1)S(1)} %get-tuple-element.38), channel_id=1, source_target_pairs={{0,6},{5,7},{7,3},{8,14},{13,15},{15,11},{16,22},{21,23},{23,19},{... | collective-permute-start | bytes 835592 | tf_op jit(solution)/shard_map/ppermute | solution.py:314
  204.8 19.5 %collective-permute-start.26 = (bf16[64,2176]{1,0:T(8,128)(2,1)S(1)}, bf16[64,2176]{1,0:T(8,128)(2,1)S(1)}, u32[]{:S(2)}, u32[]{:S(2)}) collective-permute-start(bf16[64,2176]{1,0:T(8,128)(2,1)S(1)} %get-tuple-element.39), channel_id=1, source_target_pairs={{3,5},{4,0},{6,4},{11,13},{12,8},{14,12},{19,21},{20,16},{22,20},{... | collective-permute-start | bytes 835592 | tf_op jit(solution)/shard_map/ppermute | solution.py:314
  205.4 18.8 %collective-permute-start.27 = (bf16[64,2176]{1,0:T(8,128)(2,1)S(1)}, bf16[64,2176]{1,0:T(8,128)(2,1)S(1)}, u32[]{:S(2)}, u32[]{:S(2)}) collective-permute-start(bf16[64,2176]{1,0:T(8,128)(2,1)S(1)} %get-tuple-element.40), channel_id=1, source_target_pairs={{1,3},{3,7},{4,2},{9,11},{11,15},{12,10},{17,19},{19,23},{20,18},{... | collective-permute-start | bytes 835592 | tf_op jit(solution)/shard_map/ppermute | solution.py:314
  206.8 19.3 %collective-permute-start.18 = (bf16[64,7168]{1,0:T(8,128)(2,1)S(1)}, bf16[64,7168]{1,0:T(8,128)(2,1)S(1)}, u32[]{:S(2)}, u32[]{:S(2)}) collective-permute-start(bf16[64,7168]{1,0:T(8,128)(2,1)S(1)} %collective-permute-done.12.refs_1_.refs_3_), channel_id=1, source_target_pairs={{2,0},{3,1},{10,8},{11,9},{18,16},{19,17},{26,24},{27,25}} | collective-permute-start | bytes 2752520 | tf_op jit(solution)/shard_map/ppermute | solution.py:330
  210.7 15.4 %collective-permute-start.17 = (bf16[64,7168]{1,0:T(8,128)(2,1)S(1)}, bf16[64,7168]{1,0:T(8,128)(2,1)S(1)}, u32[]{:S(2)}, u32[]{:S(2)}) collective-permute-start(bf16[64,7168]{1,0:T(8,128)(2,1)S(1)} %collective-permute-done.11.refs_0_.refs_2_), channel_id=1, source_target_pairs={{4,6},{5,7},{12,14},{13,15},{20,22},{21,23},{28,30},{29,31}} | collective-permute-start | bytes 2752520 | tf_op jit(solution)/shard_map/ppermute | solution.py:329
  223.4 15.3 %collective-permute-start.16 = (bf16[64,1792]{1,0:T(8,128)(2,1)S(1)}, bf16[64,1792]{1,0:T(8,128)(2,1)S(1)}, u32[]{:S(2)}, u32[]{:S(2)}) collective-permute-start(bf16[64,1792]{1,0:T(8,128)(2,1)S(1)} %project.12.own_ref), channel_id=1, source_target_pairs={{0,1},{7,6},{8,9},{15,14},{16,17},{23,22},{24,25},{31,30}} | collective-permute-start | bytes 688136 | tf_op jit(solution)/shard_map/ppermute | solution.py:299
  238.0 7.9 %collective-permute-start.19 = (bf16[64,1792]{1,0:T(8,128)(2,1)S(1)}, bf16[64,1792]{1,0:T(8,128)(2,1)S(1)}, u32[]{:S(2)}, u32[]{:S(2)}) collective-permute-start(bf16[64,1792]{1,0:T(8,128)(2,1)S(1)} %project.13.own_ref), channel_id=1, source_target_pairs={{0,1},{7,6},{8,9},{15,14},{16,17},{23,22},{24,25},{31,30}} | collective-permute-start | bytes 688136 | tf_op jit(solution)/shard_map/ppermute | solution.py:299
  245.2 9.7 %collective-permute-start.28 = (bf16[64,2176]{1,0:T(8,128)(2,1)S(1)}, bf16[64,2176]{1,0:T(8,128)(2,1)S(1)}, u32[]{:S(2)}, u32[]{:S(2)}) collective-permute-start(bf16[64,2176]{1,0:T(8,128)(2,1)S(1)} %get-tuple-element.41), channel_id=1, source_target_pairs={{1,5},{6,0},{9,13},{14,8},{17,21},{22,16},{25,29},{30,24}} | collective-permute-start | bytes 835592 | tf_op jit(solution)/shard_map/ppermute | solution.py:314
  252.5 14.5 %collective-permute-start.29 = (bf16[64,2176]{1,0:T(8,128)(2,1)S(1)}, bf16[64,2176]{1,0:T(8,128)(2,1)S(1)}, u32[]{:S(2)}, u32[]{:S(2)}) collective-permute-start(bf16[64,2176]{1,0:T(8,128)(2,1)S(1)} %get-tuple-element.42), channel_id=1, source_target_pairs={{1,7},{6,2},{9,15},{14,10},{17,23},{22,18},{25,31},{30,26}} | collective-permute-start | bytes 835592 | tf_op jit(solution)/shard_map/ppermute | solution.py:314
  253.8 13.1 %copy-start = (f32[512]{0:T(512)S(1)}, f32[512]{0:T(512)}, u32[]{:S(2)}) copy-start(f32[512]{0:T(512)} %param.19) | copy-start | bytes 6148

commit v2 on v0

v2 whole, which is shorter than its diff:
```python
import math

import jax
import jax.numpy as jnp
from jax import lax
from jax.experimental import pallas as pl
from jax.experimental.pallas import tpu as pltpu
from jax.sharding import PartitionSpec as P

D = 7168
Q_LAT = 1536
KV_LAT = 512
LENGTH = 2048
LANES = 128
TERMS = 3
VMEM_BYTES = 9 * 1024 * 1024

epsilon = 1e-06


def inverse_rms(squares_total, width):
    return lax.rsqrt(squares_total / width + epsilon)


def latent_norm(part, gain):
    scale_rows = inverse_rms(jnp.sum(part * part, axis=1), part.shape[1])
    return (part * scale_rows[:, None] * gain[None, :]).astype(jnp.bfloat16)


def rope_tables(width, positions):
    half_width = width // 2
    frequency = jnp.exp(
        jnp.arange(half_width, dtype=jnp.float32) * (-2.0 * math.log(10000.0) / width)
    )
    angle_grid = positions.astype(jnp.float32)[:, None] * frequency[None, :]
    return jnp.cos(angle_grid), jnp.sin(angle_grid)


def rotate_keys(rope_part, cosine, sine_grid):
    half_width = rope_part.shape[1] // 2
    lower_half = rope_part[:, :half_width]
    upper_half = rope_part[:, half_width:]
    return jnp.concatenate(
        [
            lower_half * cosine - upper_half * sine_grid,
            lower_half * sine_grid + upper_half * cosine,
        ],
        axis=1,
    )


def resident(array):
    return pltpu.with_memory_space_constraint(array, pltpu.VMEM)


def after(value, *others):
    return lax.optimization_barrier((value, *others))[0]


VMEM = pl.BlockSpec(memory_space=pltpu.VMEM)
NO_COST = pl.CostEstimate(flops=0, bytes_accessed=0, transcendentals=0)
SOME_COST = pl.CostEstimate(flops=0, bytes_accessed=15_000_000, transcendentals=0)
MORE_COST = pl.CostEstimate(flops=0, bytes_accessed=100_000_000, transcendentals=0)


def kernel(body, name, inputs, outputs, scratch=(), cost=NO_COST):
    return pl.pallas_call(
        body,
        in_specs=[VMEM] * len(inputs),
        out_specs=[VMEM] * len(outputs),
        out_shape=[jax.ShapeDtypeStruct(shape, kind) for shape, kind in outputs],
        scratch_shapes=list(scratch),
        compiler_params=pltpu.CompilerParams(vmem_limit_bytes=VMEM_BYTES),
        cost_estimate=cost,
        name=name,
    )(*inputs)


def enter(hidden, embed, cuts):
    rows, depth = hidden.shape

    def body(hidden_ref, embed_ref, *outs):
        sums = []
        for column, ref in enumerate((hidden_ref, embed_ref)):
            for (low, high), out in zip(cuts[:-1], outs, strict=False):
                out[:, column * depth : (column + 1) * depth] = ref[low:high, :]
            wide = ref[...].astype(jnp.float32)
            sums.append(jnp.sum(wide * wide, axis=1, keepdims=True))
        lane = lax.broadcasted_iota(jnp.int32, (rows, LANES), 1)
        outs[-1][...] = jnp.where(lane == 0, sums[0], jnp.where(lane == 1, sums[1], 0.0))

    outputs = [((high - low, 2 * depth), jnp.bfloat16) for low, high in cuts[:-1]]
    *pieces, sums = kernel(body, "enter", [hidden, embed], outputs + [((rows, LANES), jnp.float32)])
    return pieces, sums


def pack(hidden, embed, sums, other_sums, low):
    rows, depth = hidden.shape
    height = rows - low

    def body(hidden_ref, embed_ref, sums_ref, other_ref, piece_ref, total_ref):
        total = sums_ref[...] + other_ref[...]
        total_ref[...] = total
        piece_ref[:, :depth] = hidden_ref[low:, :]
        piece_ref[:, depth : 2 * depth] = embed_ref[low:, :]
        lane = lax.broadcasted_iota(jnp.int32, (height, LANES), 1)
        spare = jnp.zeros((height, LANES), jnp.float32)
        at = 0
        for start in range(0, rows, height):
            for column in range(2):
                rest = total[start : start + height, column : column + 1]
                for _ in range(TERMS):
                    term = rest.astype(jnp.bfloat16).astype(jnp.float32)
                    rest = rest - term
                    spare = jnp.where(lane == at, term, spare)
                    at += 1
        piece_ref[:, 2 * depth :] = spare.astype(jnp.bfloat16)

    outputs = [((height, 2 * depth + LANES), jnp.bfloat16), (sums.shape, jnp.float32)]
    return kernel(body, "pack", [hidden, embed, sums, other_sums], outputs)


def project(groups, weights, own_first=None, cost=NO_COST):
    hidden_gain, embed_gain, w_hidden, w_embed = weights
    depth, width = w_hidden.shape
    packed = [isinstance(group[1], list) for group in groups]
    inputs = []
    for arrays, sums, _ in groups:
        inputs += [*arrays, *(sums if isinstance(sums, list) else [sums])]
    distinct = []
    for array in inputs:
        if all(array is not other for other in distinct):
            distinct.append(array)
    place = {id(array): at for at, array in enumerate(distinct)}
    sizes = [group[0][0].shape[0] for group in groups]
    total = sum(sizes)
    padded = max(total, LANES)

    def squares_of(refs, low, size):
        height = refs[0].shape[0]
        parts = []
        for start in range(low, low + size, height):
            spare = sum(ref[:, 2 * depth :].astype(jnp.float32) for ref in refs)
            at = start // height * 2 * TERMS
            parts.append(
                [
                    sum(spare[:, first + t : first + t + 1] for t in range(TERMS))
                    for first in (at, at + TERMS)
                ]
            )
        return [jnp.concatenate(column, axis=0) for column in zip(*parts, strict=True)]

    def body(*refs):
        sources = refs[: len(distinct)]
        hgain_ref, egain_ref, wh_ref, we_ref, *outs, normed = refs[len(distinct) :]
        at = 0
        for (arrays, sums, low), size, is_packed in zip(groups, sizes, packed, strict=True):
            arrays = [sources[place[id(array)]] for array in arrays]
            if is_packed:
                squares = squares_of([sources[place[id(array)]] for array in sums], low, size)
            else:
                known = sources[place[id(sums)]]
                squares = [known[low : low + size, column : column + 1] for column in range(2)]
            for column, gain_ref in enumerate((hgain_ref, egain_ref)):
                part = pl.ds(column * depth, depth)
                value = arrays[0][:, part].astype(jnp.float32)
                for other in arrays[1:]:
                    value = value + other[:, part].astype(jnp.float32)
                normed[at : at + size, part] = (
                    value * inverse_rms(squares[column], D) * gain_ref[...]
                ).astype(jnp.bfloat16)
            at += size
        result = (
            jnp.dot(normed[:, :depth], wh_ref[...], preferred_element_type=jnp.float32)
            + jnp.dot(normed[:, depth:], we_ref[...], preferred_element_type=jnp.float32)
        ).astype(jnp.bfloat16)
        if own_first is not None:
            first = result[: total // 2, :]
            second = result[total // 2 : total, :]
            keep = own_first()
            outs[0][...] = jnp.where(keep, first, second)
            outs[1][...] = jnp.where(keep, second, first)
        else:
            outs[0][...] = result[:total, :]

    outputs = [((total, width), jnp.bfloat16)]
    if own_first is not None:
        outputs = [((total // 2, width), jnp.bfloat16)] * 2
    result = kernel(
        body,
        "project",
        [*distinct, hidden_gain, embed_gain, resident(w_hidden), resident(w_embed)],
        outputs,
        [pltpu.VMEM((padded, 2 * depth), jnp.bfloat16)],
        cost,
    )
    return result if own_first is not None else result[0]


def latent_partial(own, received, gain, w_latent, cuts, known=(), route=()):
    rows, width = own.shape
    lat = w_latent.shape[0]
    padded = -(-(lat + 2) // LANES) * LANES
    edge = padded - LANES

    def body(own_ref, received_ref, gain_ref, w_ref, *refs):
        known_refs, mtp_ref, lat_refs = refs[: len(known)], refs[len(known)], refs[len(known) + 1 :]
        mtp = (own_ref[...].astype(jnp.float32) + received_ref[...].astype(jnp.float32)).astype(
            jnp.bfloat16
        )
        mtp_ref[...] = mtp
        wide = mtp.astype(jnp.float32)
        total = jnp.sum(wide * wide, axis=1, keepdims=True)
        normed = (wide * gain_ref[...]).astype(jnp.bfloat16)
        over = (((1,), (1,)), ((), ()))
        main = lax.dot_general(
            normed, w_ref[:edge, :], over, preferred_element_type=jnp.float32
        ).astype(jnp.bfloat16)
        last = lax.dot_general(normed, w_ref[edge:, :], over, preferred_element_type=jnp.float32)
        column = lax.broadcasted_iota(jnp.int32, (rows, padded - lat), 1)
        high_half = total.astype(jnp.bfloat16).astype(jnp.float32)
        spare = jnp.where(column == 0, high_half, jnp.where(column == 1, total - high_half, 0.0))
        last = jnp.concatenate([last, spare], axis=1).astype(jnp.bfloat16)

        def put(ref, part):
            if part < len(known):
                ref[...] = known_refs[part][...]
            else:
                low, high = cuts[part - len(known)]
                ref[:, :edge] = main[low:high, :]
                ref[:, edge:] = last[low:high, :]

        if not route:
            for part, ref in enumerate(lat_refs):
                put(ref, part)
        else:
            lat_refs[0][...] = jnp.zeros_like(lat_refs[0])
            for when, ref in zip(route, lat_refs, strict=True):
                for part in range(len(known) + len(cuts)):
                    pl.when(when(part))(lambda ref=ref, part=part: put(ref, part))

    sizes = [high - low for low, high in cuts]
    outputs = [((rows, width), jnp.bfloat16)]
    outputs += [((size, padded), jnp.bfloat16) for size in ([sizes[0]] * len(route) if route else sizes)]
    mtp, *parts = kernel(body, "latent_partial", [own, received, gain, resident(w_latent), *known], outputs)
    return mtp, parts


def add_early(choices, arrays, rows):
    shape = (rows, choices[0][1].shape[1])

    def body(*refs):
        total = refs[-1]
        value = jnp.zeros(shape, jnp.float32)
        for (when, _), ref in zip(choices, refs, strict=False):
            part = ref[...].astype(jnp.float32)
            value = value + (part if when is None else jnp.where(when(), part, 0.0))
        total[...] = value
        for (at, array), ref in zip(arrays, refs[len(choices) : -1], strict=True):
            total[at : at + array.shape[0], :] += ref[...].astype(jnp.float32)

    inputs = [array for _, array in choices] + [array for _, array in arrays]
    return kernel(body, "add_early", inputs, [(shape, jnp.float32)])[0]


def place_rows(choices, blocks, shape):
    height = shape[0] // blocks

    def body(*refs):
        out = refs[-1]
        for (block, row, when, array), ref in zip(choices, refs, strict=False):

            @pl.when(when())
            def _(block=block, row=row, array=array, ref=ref):
                out[block * height + row : block * height + row + array.shape[0], :] = ref[...]

    return kernel(body, "place_rows", [choice[-1] for choice in choices], [(shape, jnp.bfloat16)])[0]


def finish(base, late, q_gain, kv_gain, cosine, sine_grid, first_row):
    rows = base.shape[0]
    lat = Q_LAT + KV_LAT
    rope = 2 * cosine.shape[1]

    def body(base_ref, *refs):
        late_refs = refs[: len(late)]
        qg_ref, kg_ref, cos_ref, sin_ref, q_ref, kv_ref, rope_ref, total = refs[len(late) :]
        total[...] = base_ref[...]
        for (at, array), ref in zip(late, late_refs, strict=True):
            total[at : at + array.shape[0], :] += ref[...].astype(jnp.float32)
        whole = total[...]
        squares = whole[:, lat + rope : lat + rope + 1] + whole[:, lat + rope + 1 : lat + rope + 2]
        latent = whole * inverse_rms(squares, D)
        q = latent[:, :Q_LAT]
        kv = latent[:, Q_LAT:lat]
        q_scale = inverse_rms(jnp.sum(q * q, axis=1, keepdims=True), Q_LAT)
        kv_scale = inverse_rms(jnp.sum(kv * kv, axis=1, keepdims=True), KV_LAT)
        q_ref[...] = (q * q_scale * qg_ref[...]).astype(jnp.bfloat16)
        kv_ref[...] = (kv * kv_scale * kg_ref[...]).astype(jnp.bfloat16)
        own = pl.ds(pl.multiple_of(first_row(), rows), rows)
        keys = rotate_keys(latent[:, lat : lat + rope], cos_ref[own, :], sin_ref[own, :])
        rope_ref[...] = keys.astype(jnp.bfloat16)

    return kernel(
        body,
        "finish",
        [base, *[array for _, array in late], q_gain, kv_gain, cosine, sine_grid],
        [((rows, Q_LAT), jnp.bfloat16), ((rows, KV_LAT), jnp.bfloat16), ((rows, rope), jnp.bfloat16)],
        [pltpu.VMEM(base.shape, jnp.float32)],
    )


def rounds_of(pairs):
    lists = []
    for source, target in pairs:
        for chosen in lists:
            if all(source != s and target != t for s, t in chosen):
                chosen.append((source, target))
                break
        else:
            lists.append([(source, target)])
    return lists


def shards_line(
    hidden_in, embed_in, hidden_gain, embed_gain, w_hidden, w_embed, attn_gain, w_latent, q_gain, kv_gain
):
    line = lax.axis_size("dp")
    last = line - 1
    shard = hidden_in.shape[0]
    rows_out = shard // 2
    cuts = cuts_of(shard)
    halves = ((0, rows_out), (rows_out, shard))

    def me():
        return lax.axis_index("dp")

    def mine():
        return lax.axis_index("mp")

    def owner(s):
        return s // 2

    def device(d, m):
        return d * 2 + m

    def to_owner(value, senders):
        pairs = [(device(d, 1 - m), device(d, m)) for d, m in senders]
        return lax.ppermute(value, ("dp", "mp"), pairs)

    def shard_of(k, d):
        return sorted({s for s in (d - k, d + k) if 0 <= s < line})

    def senders_of(k):
        return [(d, owner(s)) for d in range(line) for s in shard_of(k, d)]

    def send_latent(k, low, value):
        pairs = []
        for d in range(line):
            for s in shard_of(k, d):
                target = (s % 2) * 2 + low // rows_out
                if target != d:
                    pairs.append((device(d, owner(s)), device(target, owner(s))))
        return [
            (low % rows_out, lax.ppermute(value, ("dp", "mp"), chosen)) for chosen in rounds_of(pairs)
        ]

    pieces, sums = enter(hidden_in, embed_in, cuts)
    tokens = lax.axis_size("mp") * line * rows_out
    tables = rope_tables(
        w_latent.shape[1] - Q_LAT - KV_LAT, jnp.arange(tokens, dtype=jnp.int32) % LENGTH
    )
    small = [gain[None, :] for gain in (hidden_gain, embed_gain, attn_gain, q_gain, kv_gain)] + list(tables)
    (w_hidden, w_embed, w_latent), small = lax.optimization_barrier(((w_hidden, w_embed, w_latent.T), small))
    hidden_gain, embed_gain, attn_gain, q_gain, kv_gain, cosine, sine_grid = small
    weights = (hidden_gain, embed_gain, w_hidden, w_embed)

    other_sums = lax.ppermute(sums, "mp", [(0, 1), (1, 0)])
    piece, sums = pack(hidden_in, embed_in, sums, other_sums, cuts[-1][0])
    pieces.append(piece)
    ahead = [pieces]
    back = [pieces]
    for k in range(1, line):
        if k == 2:
            ahead[1][0], back[1][0], sums = lax.optimization_barrier((ahead[1][0], back[1][0], sums))
            groups = [([piece], sums, low) for piece, (low, _) in zip(pieces, cuts, strict=True)]
            got_own = project(groups, weights, cost=SOME_COST)
            ahead[1][-1], back[1][-1], got_own, sums = lax.optimization_barrier(
                (ahead[1][-1], back[1][-1], got_own, sums)
            )
        ahead.append([lax.ppermute(x, "dp", [(i, i + 1) for i in range(k - 1, last)]) for x in ahead[-1]])
        back.append([lax.ppermute(x, "dp", [(i + 1, i) for i in range(0, line - k)]) for x in back[-1]])
    mtp_own, lat_own = latent_partial(got_own, to_owner(got_own, senders_of(0)), attn_gain, w_latent, halves)
    sums_three = lax.ppermute(sums, "dp", [(0, last), (last, 0)])

    def ahead_is_own():
        near = jnp.where(me() >= 1, me() - 1, me() + 1)
        owned = jnp.where(near >= line // 2, 1, 0) == mine()
        return jnp.where(me() >= 1, owned, jnp.logical_not(owned))

    def routed(offset):
        def when(part):
            to = me() + offset
            to = jnp.where(to >= line, to - line, to)
            upper = jnp.where(to >= line // 2, 1, 0)
            step = jnp.abs(me() - (2 * mine() + upper))
            return jnp.logical_and(step == part // 2, to - upper * (line // 2) == part % 2)

        return when

    one = lax.optimization_barrier((ahead[1], back[1], ahead[2], back[2], lat_own))
    groups = [([x], [one[0][-1]], low) for x, (low, _) in zip(one[0], cuts, strict=True)]
    groups += [([x], [one[1][-1]], low) for x, (low, _) in zip(one[1], cuts, strict=True)]
    got, other = project(groups, weights, own_first=ahead_is_own)
    mtp_one, (lat_base, *lat_routed) = latent_partial(
        got,
        to_owner(other, senders_of(1)),
        attn_gain,
        w_latent,
        halves,
        known=one[4],
        route=[routed(offset) for offset in range(line)],
    )
    early = []
    for offset, part in enumerate(lat_routed, 1):
        pairs = []
        for m in range(2):
            for d in range(line):
                to = (d + offset) % line
                if abs(d - (2 * m + to // 2)) <= 1:
                    pairs.append((device(d, m), device(to, m)))
        early.append((0, lax.ppermute(part, ("dp", "mp"), pairs)))

    two = lax.optimization_barrier((ahead[2], back[2], got))
    groups = [([x, y], [two[0][-1], two[1][-1]], low) for x, y, (low, _) in zip(*two[:2], cuts, strict=True)]
    got = project(groups, weights)
    mtp_two, lat_two = latent_partial(got, to_owner(got, senders_of(2)), attn_gain, w_latent, halves)
    early_two = []
    for (low, _), part in zip(halves, lat_two, strict=True):
        early_two += send_latent(2, low, part)

    mtp_three = []
    late = []
    sums_three = after(sums_three, got, lat_base)
    for x, y, (low, high) in zip(ahead[3], back[3], cuts, strict=True):
        ends = high == shard
        got = project([([x, y], sums_three, low)], weights, cost=MORE_COST if ends else SOME_COST)
        received = to_owner(got, senders_of(3))
        if ends:
            received = after(received, early, early_two)
        mtp, (lat,) = latent_partial(got, received, attn_gain, w_latent, ((0, high - low),))
        mtp_three.append(mtp)
        late += send_latent(3, low, lat)
        sums_three = after(sums_three, got, lat_two)
    early += early_two

    def distance(offset):
        return jnp.abs(me() - (2 * mine() + offset))

    choices = []
    for offset in range(2):
        for k, mtp in enumerate((mtp_own, mtp_one, mtp_two)):
            choices.append((offset, 0, lambda offset=offset, k=k: distance(offset) == k, mtp))
        for (low, _), mtp in zip(cuts, mtp_three, strict=True):
            choices.append((offset, low, lambda offset=offset: distance(offset) == last, mtp))
    mtp_hidden = place_rows(choices, 2, (2 * shard, w_hidden.shape[1]))

    choices = [(None, lat_base)]
    for half, part in enumerate(lat_two):
        choices.append((lambda half=half: routed(0)(2 * 2 + half), part))
    base = add_early(choices, early, rows_out)
    q_latent, kv_latent, key_rope = finish(
        base, late, q_gain, kv_gain, cosine, sine_grid, lambda: (mine() * line + me()) * rows_out
    )
    return (mtp_hidden, q_latent, kv_latent, key_rope)


def cuts_of(shard):
    return ((0, shard // 2), (shard // 2, shard))


def shards_any(
    hidden_in, embed_in, hidden_gain, embed_gain, w_hidden, w_embed, attn_gain, w_latent, q_gain, kv_gain
):
    hidden_wide = hidden_in.astype(jnp.float32)
    embed_wide = embed_in.astype(jnp.float32)
    entry_sums = lax.psum(
        (jnp.sum(hidden_wide * hidden_wide, axis=1), jnp.sum(embed_wide * embed_wide, axis=1)), "mp"
    )
    hidden_norm = (hidden_wide * inverse_rms(entry_sums[0], D)[:, None] * hidden_gain[None, :]).astype(jnp.bfloat16)
    embed_norm = (embed_wide * inverse_rms(entry_sums[1], D)[:, None] * embed_gain[None, :]).astype(jnp.bfloat16)
    hidden_all = lax.all_gather(hidden_norm, "dp", axis=0, tiled=True)
    embed_all = lax.all_gather(embed_norm, "dp", axis=0, tiled=True)
    tok_share = hidden_all.shape[0] // lax.axis_size("mp")
    proj_sum = lax.psum_scatter(
        (
            jnp.dot(hidden_all, w_hidden, preferred_element_type=jnp.float32)
            + jnp.dot(embed_all, w_embed, preferred_element_type=jnp.float32)
        ).astype(jnp.bfloat16),
        "mp",
        scatter_dimension=0,
        tiled=True,
    )
    mtp_hidden = lax.optimization_barrier(proj_sum)
    proj_wide = mtp_hidden.astype(jnp.float32)
    normed_rows = (proj_wide * attn_gain[None, :]).astype(jnp.bfloat16)
    partial_latent = jnp.dot(normed_rows, w_latent, preferred_element_type=jnp.float32)
    rows_out = tok_share // lax.axis_size("dp")
    square_total = lax.psum(jnp.sum(proj_wide * proj_wide, axis=1), "dp")
    latent_sum = lax.psum_scatter(
        partial_latent.astype(jnp.bfloat16), "dp", scatter_dimension=0, tiled=True
    ).astype(jnp.float32)
    first_own = lax.axis_index("dp") * rows_out
    square_sum = lax.dynamic_slice_in_dim(square_total, first_own, rows_out, 0)
    latent = latent_sum * inverse_rms(square_sum, D)[:, None]
    first_token = lax.axis_index("mp") * tok_share + first_own
    positions = (first_token + jnp.arange(rows_out, dtype=jnp.int32)) % LENGTH
    q_latent = latent_norm(latent[:, :Q_LAT], q_gain)
    kv_latent = latent_norm(latent[:, Q_LAT : Q_LAT + KV_LAT], kv_gain)
    rope_part = latent[:, Q_LAT + KV_LAT :]
    key_rope = rotate_keys(rope_part, *rope_tables(rope_part.shape[1], positions)).astype(jnp.bfloat16)
    return (mtp_hidden, q_latent, kv_latent, key_rope)


def solution(mesh):
    placed = (
        P(("branch", "dp"), "mp"),
        P(("branch", "dp"), "mp"),
        P(("branch", "mp")),
        P(("branch", "mp")),
        P(("branch", "mp"), "dp"),
        P(("branch", "mp"), "dp"),
        P(("branch", "dp")),
        P(("branch", "dp"), None),
        P("branch"),
        P("branch"),
    )
    in_line = mesh.shape["dp"] == 4 and mesh.shape["mp"] == 2
    return jax.shard_map(
        shards_line if in_line else shards_any,
        mesh=mesh,
        in_specs=placed,
        out_specs=(
            P(("branch", "mp"), "dp"),
            P(("branch", "mp", "dp"), None),
            P(("branch", "mp", "dp"), None),
            P(("branch", "mp", "dp"), None),
        ),
        check_vma=False,
    )
```

time: 275 us -> 185 us (0.67)
  waiting for transfers between devices: 202 us -> 65.3 us
  starting transfers between devices: 0.16 us -> 55.8 us
  Pallas kernels: 0 us -> 40.6 us
  matrix products: 33.9 us -> 0 us
  local copies, waits for them, and re-layouts: 2.31 us -> 20 us
  blocking collectives: 14 us -> 0 us
  between operations: 13.9 us -> 1.16 us
  other arithmetic: 6.9 us -> 0.99 us
    all_gather x2 -> x0, waiting for transfers between devices: 128 us -> none  [the longest x1 69.5 us: shards(): hidden_all = lax.all_gather(hidden_norm, 'dp', axis=0, tiled=True)]
    ppermute x0 -> x26, waiting for transfers between devices: none -> 65.3 us  [the longest x6 22.4 us: shards_line(): lax.ppermute(x, 'dp', [(i, i + 1) for i in range(k - 1, last)])]
    ppermute x0 -> x26, starting transfers between devices: none -> 55.8 us  [the longest x6 18.3 us: shards_line(): lax.ppermute(x, 'dp', [(i + 1, i) for i in range(0, line - k)])]
    psum x1 -> x0, waiting for transfers between devices: 43.5 us -> none  [shards(): lax.psum(partial_latent.astype(jnp.bfloat16), 'dp').astype(jnp.float32)]
    pallas_call x0 -> x15, Pallas kernels: none -> 40.6 us  [kernel(): pl.pallas_call(body, in_specs=[VMEM] * len(inputs), out_specs=[VMEM] * le...]
    dot_general x3 -> x0, matrix products: 33.9 us -> none  [the longest x1 13.7 us: shards(): jnp.dot(embed_all, w_proj_embed, preferred_element_type=jnp.float32)]
    reduce_scatter x1 -> x0, waiting for transfers between devices: 30.3 us -> none  [shards(): lax.psum_scatter((jnp.dot(hidden_all, w_proj_hidden, preferred_element_ty...]
    unnamed x19 -> x28, local copies, waits for them, and re-layouts: 2.31 us -> 17.2 us
  transfers between devices with their start and end apart: 4 -> 26, of which waited for: 4 -> 11; matrix products, arithmetic and copies ran while one was open for 6% -> 2% of each run, Pallas kernels for 0% -> 21%
where the time goes in v2:
time: 185 us; the launch traced here: 184 us
  waiting for transfers between devices  65.3 us (35%)
  starting transfers between devices  55.8 us (30%)
  Pallas kernels  40.6 us (22%)
  local copies, waits for them, and re-layouts  20 us (11%)
    pallas_call x15, Pallas kernels, kernel(): pl.pallas_call(body, in_specs=[VMEM] * len(inputs), out_specs=[VMEM] * le...  40.6 us
    ppermute x6, waiting for transfers between devices, shards_line(): lax.ppermute(x, 'dp', [(i, i + 1) for i in range(k - 1, last)])  22.4 us
    ppermute x6, starting transfers between devices, shards_line(): lax.ppermute(x, 'dp', [(i + 1, i) for i in range(0, line - k)])  18.3 us
    ppermute x4, waiting for transfers between devices, send_latent(): lax.ppermute(value, ('dp', 'mp'), chosen)  17.3 us
    unnamed x28, local copies, waits for them, and re-layouts  17.2 us
    ppermute x6, starting transfers between devices, shards_line(): lax.ppermute(x, 'dp', [(i, i + 1) for i in range(k - 1, last)])  17 us
    ppermute x6, waiting for transfers between devices, shards_line(): lax.ppermute(x, 'dp', [(i + 1, i) for i in range(0, line - k)])  11 us
    ppermute x5, starting transfers between devices, to_owner(): return lax.ppermute(value, ('dp', 'mp'), pairs)  9.51 us
  transfers between devices with their start and end apart: 26, of which 11 were waited for; matrix products, arithmetic and copies ran while one was open for 2% of the time, Pallas kernels for 21%

profile of v2, /device:TPU:8, one launch (start us, length us, event | category | flops | bytes accessed | tf_op | source)
XLA Modules:
  0.0 183.9 jit_solution(13047416417484160485)
XLA Ops:
  0.6 1.2 copy-done.5
  1.8 1.2 copy-done.6
  3.4 3.5 %collective-permute-start.3 = (bf16[64,7168]{1,0:T(8,128)(2,1)S(1)}, bf16[64,7168]{1,0:T(8,128)(2,1)}, u32[]{:S(2)}, u32[]{:S(2)}) collective-permute-start(bf16[64,7168]{1,0:T(8,128)(2,1)S(1)} %get-tuple-element.60.refs_0_), channel_id=1, source_target_pairs={{0,2},{2,4},{4,6},{1,3},{3,5},{5,7},{8,10},{10,12},{12,14},{9,11},... | collective-permute-start | bytes 2752520 | tf_op jit(solution)/shard_map/ppermute | solution.py:391
  6.9 3.3 %collective-permute-start.4 = (bf16[64,7168]{1,0:T(8,128)(2,1)S(1)}, bf16[64,7168]{1,0:T(8,128)(2,1)}, u32[]{:S(2)}, u32[]{:S(2)}) collective-permute-start(bf16[64,7168]{1,0:T(8,128)(2,1)S(1)} %get-tuple-element.60.refs_0_), channel_id=1, source_target_pairs={{2,0},{4,2},{6,4},{3,1},{5,3},{7,5},{10,8},{12,10},{14,12},{11,9},... | collective-permute-start | bytes 2752520 | tf_op jit(solution)/shard_map/ppermute | solution.py:392
  10.2 1.6 collective-permute-start
  11.8 2.7 %collective-permute-done.other_ref = f32[128,128]{1,0:T(8,128)S(1)} collective-permute-done((f32[128,128]{1,0:T(8,128)S(1)}, f32[128,128]{1,0:T(8,128)S(1)}, u32[]{:S(2)}, u32[]{:S(2)}) %collective-permute-start) | collective-permute-done | bytes 65568 | tf_op jit(solution)/shard_map/ppermute | solution.py:378
  14.6 2.6 %collective-permute-start.1 = (bf16[64,7296]{1,0:T(8,128)(2,1)S(1)}, bf16[64,7296]{1,0:T(8,128)(2,1)S(1)}, u32[]{:S(2)}, u32[]{:S(2)}) collective-permute-start(bf16[64,7296]{1,0:T(8,128)(2,1)S(1)} %get-tuple-element.59.refs_2_), channel_id=1, source_target_pairs={{0,2},{2,4},{4,6},{1,3},{3,5},{5,7},{8,10},{10,12},{12,14},{9,11},... | collective-permute-start | bytes 2801672 | tf_op jit(solution)/shard_map/ppermute | solution.py:391
  17.2 3.3 %collective-permute-start.2 = (bf16[64,7296]{1,0:T(8,128)(2,1)S(1)}, bf16[64,7296]{1,0:T(8,128)(2,1)S(1)}, u32[]{:S(2)}, u32[]{:S(2)}) collective-permute-start(bf16[64,7296]{1,0:T(8,128)(2,1)S(1)} %get-tuple-element.59.refs_2_), channel_id=1, source_target_pairs={{2,0},{4,2},{6,4},{3,1},{5,3},{7,5},{10,8},{12,10},{14,12},{11,9},... | collective-permute-start | bytes 2801672 | tf_op jit(solution)/shard_map/ppermute | solution.py:392
  20.6 8.1 %collective-permute-done.3.refs_0_ = bf16[64,7168]{1,0:T(8,128)(2,1)} collective-permute-done((bf16[64,7168]{1,0:T(8,128)(2,1)S(1)}, bf16[64,7168]{1,0:T(8,128)(2,1)}, u32[]{:S(2)}, u32[]{:S(2)}) %collective-permute-start.3) | collective-permute-done | bytes 917536 | tf_op jit(solution)/shard_map/ppermute | solution.py:391
  28.7 3.5 %collective-permute-done.4.refs_2_ = bf16[64,7168]{1,0:T(8,128)(2,1)} collective-permute-done((bf16[64,7168]{1,0:T(8,128)(2,1)S(1)}, bf16[64,7168]{1,0:T(8,128)(2,1)}, u32[]{:S(2)}, u32[]{:S(2)}) %collective-permute-start.4) | collective-permute-done | bytes 917536 | tf_op jit(solution)/shard_map/ppermute | solution.py:392
  32.2 4.4 %collective-permute-start.6 = (bf16[64,7168]{1,0:T(8,128)(2,1)}, bf16[64,7168]{1,0:T(8,128)(2,1)}, u32[]{:S(2)}, u32[]{:S(2)}) collective-permute-start(bf16[64,7168]{1,0:T(8,128)(2,1)} %collective-permute-done.3.refs_0_), channel_id=1, source_target_pairs={{2,4},{4,6},{3,5},{5,7},{10,12},{12,14},{11,13},{13,15},{18,20},{2... | collective-permute-start | bytes 2752520 | tf_op jit(solution)/shard_map/ppermute | solution.py:391
  39.5 1.9 %collective-permute-start.8 = (bf16[64,7168]{1,0:T(8,128)(2,1)}, bf16[64,7168]{1,0:T(8,128)(2,1)}, u32[]{:S(2)}, u32[]{:S(2)}) collective-permute-start(bf16[64,7168]{1,0:T(8,128)(2,1)} %collective-permute-done.4.refs_2_), channel_id=1, source_target_pairs={{2,0},{4,2},{3,1},{5,3},{10,8},{12,10},{11,9},{13,11},{18,16},{20,... | collective-permute-start | bytes 2752520 | tf_op jit(solution)/shard_map/ppermute | solution.py:392
  42.4 4.6 %copy-done = bf16[3584,1792]{1,0:T(8,128)(2,1)S(1)} copy-done((bf16[3584,1792]{1,0:T(8,128)(2,1)S(1)}, bf16[3584,1792]{1,0:T(8,128)(2,1)}, u32[]{:S(2)}) %copy-start) | copy-done | bytes 12845080
  47.0 4.6 %copy-done.2 = bf16[3584,1792]{1,0:T(8,128)(2,1)S(1)} copy-done((bf16[3584,1792]{1,0:T(8,128)(2,1)S(1)}, bf16[3584,1792]{1,0:T(8,128)(2,1)}, u32[]{:S(2)}) %copy-start.2) | copy-done | bytes 12845080
  51.7 1.2 copy-done.10
  52.9 3.5 %project.5.own_ref = bf16[128,1792]{1,0:T(8,128)(2,1)S(1)} custom-call(bf16[64,7168]{1,0:T(8,128)(2,1)S(1)} %copy-done.10, f32[128,128]{1,0:T(8,128)S(1)} %get-tuple-element.91.refs_1_, bf16[64,7296]{1,0:T(8,128)(2,1)S(1)} %get-tuple-element.59.refs_2_, f32[1,3584]{1,0:T(1,128)S(1)} %broadcast_in_dim.17.refs_3_.refs_4_, ...), custom_call_target="tpu_custom_call" | custom-call | bytes 15000000 | tf_op jit(solution)/shard_map/project/pallas_call | solution.py:67
  56.5 5.2 %collective-permute-start.7 = (bf16[64,7296]{1,0:T(8,128)(2,1)S(1)}, bf16[64,7296]{1,0:T(8,128)(2,1)S(1)}, u32[]{:S(2)}, u32[]{:S(2)}) collective-permute-start(bf16[64,7296]{1,0:T(8,128)(2,1)S(1)} %collective-permute-done.1.refs_1_), channel_id=1, source_target_pairs={{2,4},{4,6},{3,5},{5,7},{10,12},{12,14},{11,13},{13,15},{18,20},{2... | collective-permute-start | bytes 2801672 | tf_op jit(solution)/shard_map/ppermute | solution.py:391
  61.6 1.9 %collective-permute-start.9 = (bf16[64,7296]{1,0:T(8,128)(2,1)S(1)}, bf16[64,7296]{1,0:T(8,128)(2,1)S(1)}, u32[]{:S(2)}, u32[]{:S(2)}) collective-permute-start(bf16[64,7296]{1,0:T(8,128)(2,1)S(1)} %collective-permute-done.2.refs_3_), channel_id=1, source_target_pairs={{2,0},{4,2},{3,1},{5,3},{10,8},{12,10},{11,9},{13,11},{18,16},{20,... | collective-permute-start | bytes 2801672 | tf_op jit(solution)/shard_map/ppermute | solution.py:392
  63.6 1.3 collective-permute-start.5
  64.9 2.6 %collective-permute-done.6.refs_0_ = bf16[64,7168]{1,0:T(8,128)(2,1)} collective-permute-done((bf16[64,7168]{1,0:T(8,128)(2,1)}, bf16[64,7168]{1,0:T(8,128)(2,1)}, u32[]{:S(2)}, u32[]{:S(2)}) %collective-permute-start.6) | collective-permute-done | bytes 917536 | tf_op jit(solution)/shard_map/ppermute | solution.py:391
  68.1 3.7 %collective-permute-done.8.refs_1_ = bf16[64,7168]{1,0:T(8,128)(2,1)} collective-permute-done((bf16[64,7168]{1,0:T(8,128)(2,1)}, bf16[64,7168]{1,0:T(8,128)(2,1)}, u32[]{:S(2)}, u32[]{:S(2)}) %collective-permute-start.8) | collective-permute-done | bytes 917536 | tf_op jit(solution)/shard_map/ppermute | solution.py:392
  71.9 3.3 %collective-permute-start.13 = (bf16[64,7168]{1,0:T(8,128)(2,1)}, bf16[64,7168]{1,0:T(8,128)(2,1)S(1)}, u32[]{:S(2)}, u32[]{:S(2)}) collective-permute-start(bf16[64,7168]{1,0:T(8,128)(2,1)} %collective-permute-done.8.refs_1_), channel_id=1, source_target_pairs={{2,0},{3,1},{10,8},{11,9},{18,16},{19,17},{26,24},{27,25}} | collective-permute-start | bytes 2752520 | tf_op jit(solution)/shard_map/ppermute | solution.py:392
  75.9 11.7 %collective-permute-done.7.refs_2_ = bf16[64,7296]{1,0:T(8,128)(2,1)S(1)} collective-permute-done((bf16[64,7296]{1,0:T(8,128)(2,1)S(1)}, bf16[64,7296]{1,0:T(8,128)(2,1)S(1)}, u32[]{:S(2)}, u32[]{:S(2)}) %collective-permute-start.7) | collective-permute-done | bytes 933920 | tf_op jit(solution)/shard_map/ppermute | solution.py:391
  88.3 3.7 %collective-permute-done.9.refs_3_ = bf16[64,7296]{1,0:T(8,128)(2,1)S(1)} collective-permute-done((bf16[64,7296]{1,0:T(8,128)(2,1)S(1)}, bf16[64,7296]{1,0:T(8,128)(2,1)S(1)}, u32[]{:S(2)}, u32[]{:S(2)}) %collective-permute-start.9) | collective-permute-done | bytes 933920 | tf_op jit(solution)/shard_map/ppermute | solution.py:392
  92.0 4.6 %collective-permute-start.17 = (bf16[64,7296]{1,0:T(8,128)(2,1)S(1)}, bf16[64,7296]{1,0:T(8,128)(2,1)S(1)}, u32[]{:S(2)}, u32[]{:S(2)}) collective-permute-start(bf16[64,7296]{1,0:T(8,128)(2,1)S(1)} %collective-permute-done.9.refs_3_), channel_id=1, source_target_pairs={{2,0},{3,1},{10,8},{11,9},{18,16},{19,17},{26,24},{27,25}} | collective-permute-start | bytes 2801672 | tf_op jit(solution)/shard_map/ppermute | solution.py:392
  96.7 3.1 %copy-done.4 = bf16[1792,2112]{0,1:T(8,128)(2,1)S(1)} copy-done((bf16[1792,2112]{0,1:T(8,128)(2,1)S(1)}, bf16[1792,2112]{0,1:T(8,128)(2,1)}, u32[]{:S(2)}) %copy-start.4) | copy-done | bytes 7569432
  99.8 2.6 %latent_partial.5 = (bf16[128,1792]{1,0:T(8,128)(2,1)S(1)}, bf16[64,2176]{1,0:T(8,128)(2,1)S(1)}, bf16[64,2176]{1,0:T(8,128)(2,1)S(1)}) custom-call(bf16[128,1792]{1,0:T(8,128)(2,1)S(1)} %project.5.own_ref, bf16[128,1792]{1,0:T(8,128)(2,1)S(1)} %collective-permute-done.5.received_ref, f32[1,1792]{1,0:T(1,128)S(1)} %broadcast_in_dim.19.gain_ref, ...), custom_call_target="tpu_custom_call" | custom-call | tf_op jit(solution)/shard_map/latent_partial/pallas_call | solution.py:67
  102.5 1.2 copy-done.8
  103.6 8.6 %project.6 = (bf16[128,1792]{1,0:T(8,128)(2,1)S(1)}, bf16[128,1792]{1,0:T(8,128)(2,1)S(1)}) custom-call(bf16[64,7168]{1,0:T(8,128)(2,1)} %collective-permute-done.3.refs_0_, bf16[64,7296]{1,0:T(8,128)(2,1)S(1)} %collective-permute-done.1.refs_1_, bf16[64,7168]{1,0:T(8,128)(2,1)} %collective-permute-done.4.refs_2_, bf16[64,7296]{1,0:T(8,128)(2,1)S(1)} %copy-done.8, ...), custom_call_target="tpu_custom_call" | custom-call | tf_op jit(solution)/shard_map/project/pallas_call | solution.py:67
  112.2 3.4 %collective-permute-start.10 = (bf16[128,1792]{1,0:T(8,128)(2,1)S(1)}, bf16[128,1792]{1,0:T(8,128)(2,1)S(1)}, u32[]{:S(2)}, u32[]{:S(2)}) collective-permute-start(bf16[128,1792]{1,0:T(8,128)(2,1)S(1)} %get-tuple-element.82), channel_id=1, source_target_pairs={{1,0},{3,2},{2,3},{5,4},{4,5},{6,7},{9,8},{11,10},{10,11},{13,12},... | collective-permute-start | bytes 1376264 | tf_op jit(solution)/shard_map/ppermute | solution.py:349
  115.7 5.3 %project.7.own_ref = bf16[128,1792]{1,0:T(8,128)(2,1)S(1)} custom-call(bf16[64,7168]{1,0:T(8,128)(2,1)} %collective-permute-done.6.refs_0_, bf16[64,7168]{1,0:T(8,128)(2,1)} %collective-permute-done.8.refs_1_, bf16[64,7296]{1,0:T(8,128)(2,1)S(1)} %collective-permute-done.7.refs_2_, bf16[64,7296]{1,0:T(8,128)(2,1)S(1)} %collective-permute-done.9.refs_3_, ...), custom_call_target="tpu_custom_call" | custom-call | tf_op jit(solution)/shard_map/project/pallas_call | solution.py:67
  121.0 2.4 %collective-permute-done.10.received_ref = bf16[128,1792]{1,0:T(8,128)(2,1)S(1)} collective-permute-done((bf16[128,1792]{1,0:T(8,128)(2,1)S(1)}, bf16[128,1792]{1,0:T(8,128)(2,1)S(1)}, u32[]{:S(2)}, u32[]{:S(2)}) %collective-permute-start.10) | collective-permute-done | bytes 458784 | tf_op jit(solution)/shard_map/ppermute | solution.py:349
  123.4 3.4 %collective-permute-start.11 = (bf16[128,1792]{1,0:T(8,128)(2,1)S(1)}, bf16[128,1792]{1,0:T(8,128)(2,1)S(1)}, u32[]{:S(2)}, u32[]{:S(2)}) collective-permute-start(bf16[128,1792]{1,0:T(8,128)(2,1)S(1)} %project.7.own_ref), channel_id=1, source_target_pairs={{0,1},{2,3},{5,4},{7,6},{8,9},{10,11},{13,12},{15,14},{16,17},{18,... | collective-permute-start | bytes 1376264 | tf_op jit(solution)/shard_map/ppermute | solution.py:349
  126.9 2.7 %latent_partial.6 = (bf16[128,1792]{1,0:T(8,128)(2,1)S(1)}, bf16[64,2176]{1,0:T(8,128)(2,1)S(1)}, bf16[64,2176]{1,0:T(8,128)(2,1)S(1)}, bf16[64,2176]{1,0:T(8,128)(2,1)S(1)}, bf16[64,2176]{1,0:T(8,128)(2,1)S(1)}) custom-call(bf16[128,1792]{1,0:T(8,128)(2,1)S(1)} %get-tuple-element.81.own_ref, bf16[128,1792]{1,0:T(8,128)(2,1)S(1)} %collective-permute-done.10.received_ref, ...), custom_call_target="tpu_custom_call" | custom-call | tf_op jit(solution)/shard_map/latent_partial/pallas_call | solution.py:67
  129.7 2.1 %collective-permute-start.19 = (bf16[64,2176]{1,0:T(8,128)(2,1)S(1)}, bf16[64,2176]{1,0:T(8,128)(2,1)S(1)}, u32[]{:S(2)}, u32[]{:S(2)}) collective-permute-start(bf16[64,2176]{1,0:T(8,128)(2,1)S(1)} %get-tuple-element.98), channel_id=1, source_target_pairs={{0,2},{2,4},{4,6},{5,7},{7,1},{8,10},{10,12},{12,14},{13,15},{15,9... | collective-permute-start | bytes 835592 | tf_op jit(solution)/shard_map/ppermute | solution.py:432
  131.8 3.7 %project.8.own_ref = bf16[64,1792]{1,0:T(8,128)(2,1)S(1)} custom-call(bf16[64,7168]{1,0:T(8,128)(2,1)S(1)} %collective-permute-done.12.refs_0_, bf16[64,7168]{1,0:T(8,128)(2,1)S(1)} %collective-permute-done.13.refs_1_, f32[128,128]{1,0:T(8,128)S(1)} %collective-permute-done.14.refs_2_, f32[1,3584]{1,0:T(1,128)S(1)} %broadcast_in_dim.17.refs_3_.refs_4_, ...), custom_call_target="tpu_custom_call" | custom-call | bytes 15000000 | tf_op jit(solution)/shard_map/project/pallas_call | solution.py:67
  136.2 1.3 collective-permute-start.20
  137.5 2.6 %latent_partial.7 = (bf16[128,1792]{1,0:T(8,128)(2,1)S(1)}, bf16[64,2176]{1,0:T(8,128)(2,1)S(1)}, bf16[64,2176]{1,0:T(8,128)(2,1)S(1)}) custom-call(bf16[128,1792]{1,0:T(8,128)(2,1)S(1)} %project.7.own_ref, bf16[128,1792]{1,0:T(8,128)(2,1)S(1)} %collective-permute-done.11.received_ref, f32[1,1792]{1,0:T(1,128)S(1)} %broadcast_in_dim.19.gain_ref, ...), custom_call_target="tpu_custom_call" | custom-call | tf_op jit(solution)/shard_map/latent_partial/pallas_call | solution.py:67
  140.1 9.4 %collective-permute-done.19.refs_3_ = bf16[64,2176]{1,0:T(8,128)(2,1)S(1)} collective-permute-done((bf16[64,2176]{1,0:T(8,128)(2,1)S(1)}, bf16[64,2176]{1,0:T(8,128)(2,1)S(1)}, u32[]{:S(2)}, u32[]{:S(2)}) %collective-permute-start.19) | collective-permute-done | bytes 278560 | tf_op jit(solution)/shard_map/ppermute | solution.py:432
  149.5 1.3 collective-permute-start.21
  151.5 1.3 collective-permute-start.23
  152.8 3.7 %project.9.own_ref = bf16[64,1792]{1,0:T(8,128)(2,1)S(1)} custom-call(bf16[64,7296]{1,0:T(8,128)(2,1)S(1)} %collective-permute-done.16.refs_0_, bf16[64,7296]{1,0:T(8,128)(2,1)S(1)} %collective-permute-done.17.refs_1_, f32[128,128]{1,0:T(8,128)S(1)} %collective-permute-done.14.refs_2_, f32[1,3584]{1,0:T(1,128)S(1)} %broadcast_in_dim.17.refs_3_.refs_4_, ...), custom_call_target="tpu_custom_call" | custom-call | bytes 100000000 | tf_op jit(solution)/shard_map/project/pallas_call | solution.py:67
  157.2 2.4 %latent_partial.8 = (bf16[64,1792]{1,0:T(8,128)(2,1)S(1)}, bf16[64,2176]{1,0:T(8,128)(2,1)S(1)}) custom-call(bf16[64,1792]{1,0:T(8,128)(2,1)S(1)} %project.8.own_ref, bf16[64,1792]{1,0:T(8,128)(2,1)S(1)} %collective-permute-done.15.received_ref, f32[1,1792]{1,0:T(1,128)S(1)} %broadcast_in_dim.19.gain_ref, bf16[2112,1792]{1,0:T(8,128)(2,1)S(1)} %bitcast.7), custom_call_target="tpu_custom_call" | custom-call | tf_op jit(solution)/shard_map/latent_partial/pallas_call | solution.py:67
  160.3 10.8 %collective-permute-done.23.refs_7_ = bf16[64,2176]{1,0:T(8,128)(2,1)S(1)} collective-permute-done((bf16[64,2176]{1,0:T(8,128)(2,1)S(1)}, bf16[64,2176]{1,0:T(8,128)(2,1)S(1)}, u32[]{:S(2)}, u32[]{:S(2)}) %collective-permute-start.23) | collective-permute-done | bytes 278560 | tf_op jit(solution)/shard_map/ppermute | solution.py:365
  171.2 2.4 %latent_partial.9 = (bf16[64,1792]{1,0:T(8,128)(2,1)S(1)}, bf16[64,2176]{1,0:T(8,128)(2,1)S(1)}) custom-call(bf16[64,1792]{1,0:T(8,128)(2,1)S(1)} %project.9.own_ref, bf16[64,1792]{1,0:T(8,128)(2,1)S(1)} %collective-permute-done.18.received_ref, f32[1,1792]{1,0:T(1,128)S(1)} %broadcast_in_dim.19.gain_ref, bf16[2112,1792]{1,0:T(8,128)(2,1)S(1)} %bitcast.8), custom_call_target="tpu_custom_call" | custom-call | tf_op jit(solution)/shard_map/latent_partial/pallas_call | solution.py:67
  173.6 1.3 collective-permute-start.25
  175.4 1.0 place_rows.1
  176.4 6.5 %collective-permute-done.25.refs_1_ = bf16[64,2176]{1,0:T(8,128)(2,1)S(1)} collective-permute-done((bf16[64,2176]{1,0:T(8,128)(2,1)S(1)}, bf16[64,2176]{1,0:T(8,128)(2,1)S(1)}, u32[]{:S(2)}, u32[]{:S(2)}) %collective-permute-start.25) | collective-permute-done | bytes 278560 | tf_op jit(solution)/shard_map/ppermute | solution.py:365
  (55 shorter events, 10.9 us)
Async XLA Ops:
  0.6 1.2 copy-start.5
  1.8 1.2 copy-start.6
  3.4 39.0 %copy-start.9 = (bf16[64,7168]{1,0:T(8,128)(2,1)}, bf16[64,7168]{1,0:T(8,128)(2,1)S(1)}, u32[]{:S(2)}) copy-start(bf16[64,7168]{1,0:T(8,128)(2,1)S(1)} %get-tuple-element.60.refs_0_) | copy-start | bytes 2752516
  3.4 25.2 %collective-permute-start.3 = (bf16[64,7168]{1,0:T(8,128)(2,1)S(1)}, bf16[64,7168]{1,0:T(8,128)(2,1)}, u32[]{:S(2)}, u32[]{:S(2)}) collective-permute-start(bf16[64,7168]{1,0:T(8,128)(2,1)S(1)} %get-tuple-element.60.refs_0_), channel_id=1, source_target_pairs={{0,2},{2,4},{4,6},{1,3},{3,5},{5,7},{8,10},{10,12},{12,14},{9,11},... | collective-permute-start | bytes 2752520 | tf_op jit(solution)/shard_map/ppermute | solution.py:391
  6.9 25.3 %collective-permute-start.4 = (bf16[64,7168]{1,0:T(8,128)(2,1)S(1)}, bf16[64,7168]{1,0:T(8,128)(2,1)}, u32[]{:S(2)}, u32[]{:S(2)}) collective-permute-start(bf16[64,7168]{1,0:T(8,128)(2,1)S(1)} %get-tuple-element.60.refs_0_), channel_id=1, source_target_pairs={{2,0},{4,2},{6,4},{3,1},{5,3},{7,5},{10,8},{12,10},{14,12},{11,9},... | collective-permute-start | bytes 2752520 | tf_op jit(solution)/shard_map/ppermute | solution.py:392
  10.2 4.3 %collective-permute-start = (f32[128,128]{1,0:T(8,128)S(1)}, f32[128,128]{1,0:T(8,128)S(1)}, u32[]{:S(2)}, u32[]{:S(2)}) collective-permute-start(f32[128,128]{1,0:T(8,128)S(1)} %get-tuple-element.58.sums_ref), channel_id=1, source_target_pairs={{0,1},{1,0},{2,3},{3,2},{4,5},{5,4},{6,7},{7,6},{8,9},{9,8},{10,11... | collective-permute-start | bytes 196616 | tf_op jit(solution)/shard_map/ppermute | solution.py:378
  14.6 41.8 %collective-permute-start.1 = (bf16[64,7296]{1,0:T(8,128)(2,1)S(1)}, bf16[64,7296]{1,0:T(8,128)(2,1)S(1)}, u32[]{:S(2)}, u32[]{:S(2)}) collective-permute-start(bf16[64,7296]{1,0:T(8,128)(2,1)S(1)} %get-tuple-element.59.refs_2_), channel_id=1, source_target_pairs={{0,2},{2,4},{4,6},{1,3},{3,5},{5,7},{8,10},{10,12},{12,14},{9,11},... | collective-permute-start | bytes 2801672 | tf_op jit(solution)/shard_map/ppermute | solution.py:391
  17.2 39.2 %collective-permute-start.2 = (bf16[64,7296]{1,0:T(8,128)(2,1)S(1)}, bf16[64,7296]{1,0:T(8,128)(2,1)S(1)}, u32[]{:S(2)}, u32[]{:S(2)}) collective-permute-start(bf16[64,7296]{1,0:T(8,128)(2,1)S(1)} %get-tuple-element.59.refs_2_), channel_id=1, source_target_pairs={{2,0},{4,2},{6,4},{3,1},{5,3},{7,5},{10,8},{12,10},{14,12},{11,9},... | collective-permute-start | bytes 2801672 | tf_op jit(solution)/shard_map/ppermute | solution.py:392
  32.2 35.2 %collective-permute-start.6 = (bf16[64,7168]{1,0:T(8,128)(2,1)}, bf16[64,7168]{1,0:T(8,128)(2,1)}, u32[]{:S(2)}, u32[]{:S(2)}) collective-permute-start(bf16[64,7168]{1,0:T(8,128)(2,1)} %collective-permute-done.3.refs_0_), channel_id=1, source_target_pairs={{2,4},{4,6},{3,5},{5,7},{10,12},{12,14},{11,13},{13,15},{18,20},{2... | collective-permute-start | bytes 2752520 | tf_op jit(solution)/shard_map/ppermute | solution.py:391
  39.5 32.4 %collective-permute-start.8 = (bf16[64,7168]{1,0:T(8,128)(2,1)}, bf16[64,7168]{1,0:T(8,128)(2,1)}, u32[]{:S(2)}, u32[]{:S(2)}) collective-permute-start(bf16[64,7168]{1,0:T(8,128)(2,1)} %collective-permute-done.4.refs_2_), channel_id=1, source_target_pairs={{2,0},{4,2},{3,1},{5,3},{10,8},{12,10},{11,9},{13,11},{18,16},{20,... | collective-permute-start | bytes 2752520 | tf_op jit(solution)/shard_map/ppermute | solution.py:392
  42.4 4.7 %copy-start = (bf16[3584,1792]{1,0:T(8,128)(2,1)S(1)}, bf16[3584,1792]{1,0:T(8,128)(2,1)}, u32[]{:S(2)}) copy-start(bf16[3584,1792]{1,0:T(8,128)(2,1)} %refs_5_.2) | copy-start | bytes 38535172
  47.0 4.7 %copy-start.2 = (bf16[3584,1792]{1,0:T(8,128)(2,1)S(1)}, bf16[3584,1792]{1,0:T(8,128)(2,1)}, u32[]{:S(2)}) copy-start(bf16[3584,1792]{1,0:T(8,128)(2,1)} %refs_6_.4) | copy-start | bytes 38535172
  51.7 1.2 copy-start.10
  52.9 49.5 %copy-start.1 = (bf16[3584,1792]{1,0:T(8,128)(2,1)S(1)}, bf16[3584,1792]{1,0:T(8,128)(2,1)}, u32[]{:S(2)}) copy-start(bf16[3584,1792]{1,0:T(8,128)(2,1)} %refs_5_.2) | copy-start | bytes 38535172
  52.9 49.6 %copy-start.3 = (bf16[3584,1792]{1,0:T(8,128)(2,1)S(1)}, bf16[3584,1792]{1,0:T(8,128)(2,1)}, u32[]{:S(2)}) copy-start(bf16[3584,1792]{1,0:T(8,128)(2,1)} %refs_6_.4) | copy-start | bytes 38535172
  56.4 46.0 %copy-start.7 = (bf16[64,7296]{1,0:T(8,128)(2,1)}, bf16[64,7296]{1,0:T(8,128)(2,1)S(1)}, u32[]{:S(2)}) copy-start(bf16[64,7296]{1,0:T(8,128)(2,1)S(1)} %collective-permute-done.2.refs_3_) | copy-start | bytes 2801668
  56.5 31.1 %collective-permute-start.7 = (bf16[64,7296]{1,0:T(8,128)(2,1)S(1)}, bf16[64,7296]{1,0:T(8,128)(2,1)S(1)}, u32[]{:S(2)}, u32[]{:S(2)}) collective-permute-start(bf16[64,7296]{1,0:T(8,128)(2,1)S(1)} %collective-permute-done.1.refs_1_), channel_id=1, source_target_pairs={{2,4},{4,6},{3,5},{5,7},{10,12},{12,14},{11,13},{13,15},{18,20},{2... | collective-permute-start | bytes 2801672 | tf_op jit(solution)/shard_map/ppermute | solution.py:391
  61.6 30.4 %collective-permute-start.9 = (bf16[64,7296]{1,0:T(8,128)(2,1)S(1)}, bf16[64,7296]{1,0:T(8,128)(2,1)S(1)}, u32[]{:S(2)}, u32[]{:S(2)}) collective-permute-start(bf16[64,7296]{1,0:T(8,128)(2,1)S(1)} %collective-permute-done.2.refs_3_), channel_id=1, source_target_pairs={{2,0},{4,2},{3,1},{5,3},{10,8},{12,10},{11,9},{13,11},{18,16},{20,... | collective-permute-start | bytes 2801672 | tf_op jit(solution)/shard_map/ppermute | solution.py:392
  63.6 11.6 %collective-permute-start.5 = (bf16[128,1792]{1,0:T(8,128)(2,1)S(1)}, bf16[128,1792]{1,0:T(8,128)(2,1)S(1)}, u32[]{:S(2)}, u32[]{:S(2)}) collective-permute-start(bf16[128,1792]{1,0:T(8,128)(2,1)S(1)} %project.5.own_ref), channel_id=1, source_target_pairs={{1,0},{3,2},{4,5},{6,7},{9,8},{11,10},{12,13},{14,15},{17,16},{19,... | collective-permute-start | bytes 1376264 | tf_op jit(solution)/shard_map/ppermute | solution.py:349
  67.4 62.2 %collective-permute-start.12 = (bf16[64,7168]{1,0:T(8,128)(2,1)}, bf16[64,7168]{1,0:T(8,128)(2,1)S(1)}, u32[]{:S(2)}, u32[]{:S(2)}) collective-permute-start(bf16[64,7168]{1,0:T(8,128)(2,1)} %collective-permute-done.6.refs_0_), channel_id=1, source_target_pairs={{4,6},{5,7},{12,14},{13,15},{20,22},{21,23},{28,30},{29,31}} | collective-permute-start | bytes 2752520 | tf_op jit(solution)/shard_map/ppermute | solution.py:391
  71.9 59.9 %collective-permute-start.13 = (bf16[64,7168]{1,0:T(8,128)(2,1)}, bf16[64,7168]{1,0:T(8,128)(2,1)S(1)}, u32[]{:S(2)}, u32[]{:S(2)}) collective-permute-start(bf16[64,7168]{1,0:T(8,128)(2,1)} %collective-permute-done.8.refs_1_), channel_id=1, source_target_pairs={{2,0},{3,1},{10,8},{11,9},{18,16},{19,17},{26,24},{27,25}} | collective-permute-start | bytes 2752520 | tf_op jit(solution)/shard_map/ppermute | solution.py:392
  75.2 37.0 %collective-permute-start.14 = (f32[128,128]{1,0:T(8,128)S(1)}, f32[128,128]{1,0:T(8,128)S(1)}, u32[]{:S(2)}, u32[]{:S(2)}) collective-permute-start(f32[128,128]{1,0:T(8,128)S(1)} %get-tuple-element.91.refs_1_), channel_id=1, source_target_pairs={{0,6},{6,0},{1,7},{7,1},{8,14},{14,8},{9,15},{15,9},{16,22},{22,16... | collective-permute-start | bytes 196616 | tf_op jit(solution)/shard_map/ppermute | solution.py:394
  87.6 63.2 %collective-permute-start.16 = (bf16[64,7296]{1,0:T(8,128)(2,1)S(1)}, bf16[64,7296]{1,0:T(8,128)(2,1)S(1)}, u32[]{:S(2)}, u32[]{:S(2)}) collective-permute-start(bf16[64,7296]{1,0:T(8,128)(2,1)S(1)} %collective-permute-done.7.refs_2_), channel_id=1, source_target_pairs={{4,6},{5,7},{12,14},{13,15},{20,22},{21,23},{28,30},{29,31}} | collective-permute-start | bytes 2801672 | tf_op jit(solution)/shard_map/ppermute | solution.py:391
  92.0 59.5 %collective-permute-start.17 = (bf16[64,7296]{1,0:T(8,128)(2,1)S(1)}, bf16[64,7296]{1,0:T(8,128)(2,1)S(1)}, u32[]{:S(2)}, u32[]{:S(2)}) collective-permute-start(bf16[64,7296]{1,0:T(8,128)(2,1)S(1)} %collective-permute-done.9.refs_3_), channel_id=1, source_target_pairs={{2,0},{3,1},{10,8},{11,9},{18,16},{19,17},{26,24},{27,25}} | collective-permute-start | bytes 2801672 | tf_op jit(solution)/shard_map/ppermute | solution.py:392
  96.7 3.2 %copy-start.4 = (bf16[1792,2112]{0,1:T(8,128)(2,1)S(1)}, bf16[1792,2112]{0,1:T(8,128)(2,1)}, u32[]{:S(2)}) copy-start(bf16[1792,2112]{0,1:T(8,128)(2,1)} %param.17) | copy-start | bytes 22708228
  102.4 1.2 copy-start.8
  103.6 23.2 %slice-start = ((s8[7569408]{0:T(1024)(128)(4,1)}), s8[4194304]{0:T(1024)(128)(4,1)S(1)}, s32[]{:S(2)}) async-start(s8[7569408]{0:T(1024)(128)(4,1)} %bitcast.3), calls=%async_computation | async-start | bytes 8388608
  112.2 11.2 %collective-permute-start.10 = (bf16[128,1792]{1,0:T(8,128)(2,1)S(1)}, bf16[128,1792]{1,0:T(8,128)(2,1)S(1)}, u32[]{:S(2)}, u32[]{:S(2)}) collective-permute-start(bf16[128,1792]{1,0:T(8,128)(2,1)S(1)} %get-tuple-element.82), channel_id=1, source_target_pairs={{1,0},{3,2},{2,3},{5,4},{4,5},{6,7},{9,8},{11,10},{10,11},{13,12},... | collective-permute-start | bytes 1376264 | tf_op jit(solution)/shard_map/ppermute | solution.py:349
  115.6 11.2 %slice-start.1 = ((s8[7569408]{0:T(1024)(128)(4,1)}), s8[3375104]{0:T(1024)(128)(4,1)S(1)}, s32[]{:S(2)}) async-start(s8[7569408]{0:T(1024)(128)(4,1)} %bitcast.3), calls=%async_computation.1 | async-start | bytes 6750208
  123.4 12.8 %collective-permute-start.11 = (bf16[128,1792]{1,0:T(8,128)(2,1)S(1)}, bf16[128,1792]{1,0:T(8,128)(2,1)S(1)}, u32[]{:S(2)}, u32[]{:S(2)}) collective-permute-start(bf16[128,1792]{1,0:T(8,128)(2,1)S(1)} %project.7.own_ref), channel_id=1, source_target_pairs={{0,1},{2,3},{5,4},{7,6},{8,9},{10,11},{13,12},{15,14},{16,17},{18,... | collective-permute-start | bytes 1376264 | tf_op jit(solution)/shard_map/ppermute | solution.py:349
  129.7 19.8 %collective-permute-start.19 = (bf16[64,2176]{1,0:T(8,128)(2,1)S(1)}, bf16[64,2176]{1,0:T(8,128)(2,1)S(1)}, u32[]{:S(2)}, u32[]{:S(2)}) collective-permute-start(bf16[64,2176]{1,0:T(8,128)(2,1)S(1)} %get-tuple-element.98), channel_id=1, source_target_pairs={{0,2},{2,4},{4,6},{5,7},{7,1},{8,10},{10,12},{12,14},{13,15},{15,9... | collective-permute-start | bytes 835592 | tf_op jit(solution)/shard_map/ppermute | solution.py:432
  135.5 21.0 %collective-permute-start.15 = (bf16[64,1792]{1,0:T(8,128)(2,1)S(1)}, bf16[64,1792]{1,0:T(8,128)(2,1)S(1)}, u32[]{:S(2)}, u32[]{:S(2)}) collective-permute-start(bf16[64,1792]{1,0:T(8,128)(2,1)S(1)} %project.8.own_ref), channel_id=1, source_target_pairs={{0,1},{7,6},{8,9},{15,14},{16,17},{23,22},{24,25},{31,30}} | collective-permute-start | bytes 688136 | tf_op jit(solution)/shard_map/ppermute | solution.py:349
  136.2 23.4 %collective-permute-start.20 = (bf16[64,2176]{1,0:T(8,128)(2,1)S(1)}, bf16[64,2176]{1,0:T(8,128)(2,1)S(1)}, u32[]{:S(2)}, u32[]{:S(2)}) collective-permute-start(bf16[64,2176]{1,0:T(8,128)(2,1)S(1)} %get-tuple-element.99), channel_id=1, source_target_pairs={{0,4},{2,6},{5,1},{7,3},{8,12},{10,14},{13,9},{15,11},{16,20},{18,... | collective-permute-start | bytes 835592 | tf_op jit(solution)/shard_map/ppermute | solution.py:432
  149.5 10.8 %collective-permute-start.21 = (bf16[64,2176]{1,0:T(8,128)(2,1)S(1)}, bf16[64,2176]{1,0:T(8,128)(2,1)S(1)}, u32[]{:S(2)}, u32[]{:S(2)}) collective-permute-start(bf16[64,2176]{1,0:T(8,128)(2,1)S(1)} %get-tuple-element.100), channel_id=1, source_target_pairs={{0,6},{2,0},{3,1},{5,3},{7,5},{8,14},{10,8},{11,9},{13,11},{15,13}... | collective-permute-start | bytes 835592 | tf_op jit(solution)/shard_map/ppermute | solution.py:432
  150.8 9.5 %collective-permute-start.22 = (bf16[64,2176]{1,0:T(8,128)(2,1)S(1)}, bf16[64,2176]{1,0:T(8,128)(2,1)S(1)}, u32[]{:S(2)}, u32[]{:S(2)}) collective-permute-start(bf16[64,2176]{1,0:T(8,128)(2,1)S(1)} %get-tuple-element.95.refs_1_), channel_id=1, source_target_pairs={{3,5},{4,0},{6,4},{11,13},{12,8},{14,12},{19,21},{20,16},{22,20},{... | collective-permute-start | bytes 835592 | tf_op jit(solution)/shard_map/ppermute | solution.py:365
  151.5 19.7 %collective-permute-start.23 = (bf16[64,2176]{1,0:T(8,128)(2,1)S(1)}, bf16[64,2176]{1,0:T(8,128)(2,1)S(1)}, u32[]{:S(2)}, u32[]{:S(2)}) collective-permute-start(bf16[64,2176]{1,0:T(8,128)(2,1)S(1)} %get-tuple-element.96.refs_2_), channel_id=1, source_target_pairs={{1,3},{3,7},{4,2},{9,11},{11,15},{12,10},{17,19},{19,23},{20,18},{... | collective-permute-start | bytes 835592 | tf_op jit(solution)/shard_map/ppermute | solution.py:365
  156.5 26.4 %copy-start.11 = (f32[512]{0:T(512)S(1)}, f32[512]{0:T(512)}, u32[]{:S(2)}) copy-start(f32[512]{0:T(512)} %param.19) | copy-start | bytes 6148
  156.6 14.6 %collective-permute-start.18 = (bf16[64,1792]{1,0:T(8,128)(2,1)S(1)}, bf16[64,1792]{1,0:T(8,128)(2,1)S(1)}, u32[]{:S(2)}, u32[]{:S(2)}) collective-permute-start(bf16[64,1792]{1,0:T(8,128)(2,1)S(1)} %project.9.own_ref), channel_id=1, source_target_pairs={{0,1},{7,6},{8,9},{15,14},{16,17},{23,22},{24,25},{31,30}} | collective-permute-start | bytes 688136 | tf_op jit(solution)/shard_map/ppermute | solution.py:349
  159.6 16.8 %collective-permute-start.24 = (bf16[64,2176]{1,0:T(8,128)(2,1)S(1)}, bf16[64,2176]{1,0:T(8,128)(2,1)S(1)}, u32[]{:S(2)}, u32[]{:S(2)}) collective-permute-start(bf16[64,2176]{1,0:T(8,128)(2,1)S(1)} %get-tuple-element.103), channel_id=1, source_target_pairs={{1,5},{6,0},{9,13},{14,8},{17,21},{22,16},{25,29},{30,24}} | collective-permute-start | bytes 835592 | tf_op jit(solution)/shard_map/ppermute | solution.py:365
  173.6 9.3 %collective-permute-start.25 = (bf16[64,2176]{1,0:T(8,128)(2,1)S(1)}, bf16[64,2176]{1,0:T(8,128)(2,1)S(1)}, u32[]{:S(2)}, u32[]{:S(2)}) collective-permute-start(bf16[64,2176]{1,0:T(8,128)(2,1)S(1)} %get-tuple-element.104), channel_id=1, source_target_pairs={{1,7},{6,2},{9,15},{14,10},{17,23},{22,18},{25,31},{30,26}} | collective-permute-start | bytes 835592 | tf_op jit(solution)/shard_map/ppermute | solution.py:365

commit v3 on v2

--- a/solution.py
+++ b/solution.py
@@ -59,8 +59,6 @@
 
 VMEM = pl.BlockSpec(memory_space=pltpu.VMEM)
 NO_COST = pl.CostEstimate(flops=0, bytes_accessed=0, transcendentals=0)
-SOME_COST = pl.CostEstimate(flops=0, bytes_accessed=15_000_000, transcendentals=0)
-MORE_COST = pl.CostEstimate(flops=0, bytes_accessed=100_000_000, transcendentals=0)
 
 
 def kernel(body, name, inputs, outputs, scratch=(), cost=NO_COST):
@@ -76,33 +74,44 @@
     )(*inputs)
 
 
-def enter(hidden, embed, cuts):
+def half_rows(half, rows, swaps):
+    return pl.ds(pl.multiple_of((half + (1 - 2 * half) * swaps) * rows, rows), rows)
+
+
+def enter(hidden, embed, swaps):
     rows, depth = hidden.shape
-
-    def body(hidden_ref, embed_ref, *outs):
-        sums = []
-        for column, ref in enumerate((hidden_ref, embed_ref)):
-            for (low, high), out in zip(cuts[:-1], outs, strict=False):
-                out[:, column * depth : (column + 1) * depth] = ref[low:high, :]
-            wide = ref[...].astype(jnp.float32)
-            sums.append(jnp.sum(wide * wide, axis=1, keepdims=True))
-        lane = lax.broadcasted_iota(jnp.int32, (rows, LANES), 1)
-        outs[-1][...] = jnp.where(lane == 0, sums[0], jnp.where(lane == 1, sums[1], 0.0))
-
-    outputs = [((high - low, 2 * depth), jnp.bfloat16) for low, high in cuts[:-1]]
-    *pieces, sums = kernel(body, "enter", [hidden, embed], outputs + [((rows, LANES), jnp.float32)])
-    return pieces, sums
-
-
-def pack(hidden, embed, sums, other_sums, low):
+    height = rows // 2
+
+    def body(hidden_ref, embed_ref, piece_ref, sums_ref):
+        swapped = swaps()
+        for half in range(2):
+            sums = []
+            for column, ref in enumerate((hidden_ref, embed_ref)):
+                part = ref[half_rows(half, height, swapped), :]
+                if half == 0:
+                    piece_ref[:, column * depth : (column + 1) * depth] = part
+                wide = part.astype(jnp.float32)
+                sums.append(jnp.sum(wide * wide, axis=1, keepdims=True))
+            lane = lax.broadcasted_iota(jnp.int32, (height, LANES), 1)
+            sums_ref[half * height : (half + 1) * height, :] = jnp.where(
+                lane == 0, sums[0], jnp.where(lane == 1, sums[1], 0.0)
+            )
+        piece_ref[:, 2 * depth :] = jnp.zeros((height, LANES), jnp.bfloat16)
+
+    outputs = [((height, 2 * depth + LANES), jnp.bfloat16), ((rows, LANES), jnp.float32)]
+    return kernel(body, "enter", [hidden, embed], outputs)
+
+
+def pack(hidden, embed, sums, other_sums, swaps):
     rows, depth = hidden.shape
-    height = rows - low
+    height = rows // 2
 
     def body(hidden_ref, embed_ref, sums_ref, other_ref, piece_ref, total_ref):
         total = sums_ref[...] + other_ref[...]
         total_ref[...] = total
-        piece_ref[:, :depth] = hidden_ref[low:, :]
-        piece_ref[:, depth : 2 * depth] = embed_ref[low:, :]
+        second = half_rows(1, height, swaps())
+        piece_ref[:, :depth] = hidden_ref[second, :]
+        piece_ref[:, depth : 2 * depth] = embed_ref[second, :]
         lane = lax.broadcasted_iota(jnp.int32, (height, LANES), 1)
         spare = jnp.zeros((height, LANES), jnp.float32)
         at = 0
@@ -197,6 +206,26 @@
     return result if own_first is not None else result[0]
 
 
+def warm(arrays, weights):
+    def body(*refs):
+        refs[-1][...] = refs[0][:8, :LANES]
+
+    return kernel(body, "warm", [*arrays, *[resident(w) for w in weights]], [((8, LANES), arrays[0].dtype)])[0]
+
+
+def choose(first, second, takes_first):
+    def body(first_ref, second_ref, out):
+        @pl.when(takes_first())
+        def _():
+            out[...] = first_ref[...]
+
+        @pl.when(jnp.logical_not(takes_first()))
+        def _():
+            out[...] = second_ref[...]
+
+    return kernel(body, "choose", [first, second], [(first.shape, first.dtype)])[0]
+
+
 def latent_partial(own, received, gain, w_latent, cuts, known=(), route=()):
     rows, width = own.shape
     lat = w_latent.shape[0]
@@ -222,57 +251,67 @@
         spare = jnp.where(column == 0, high_half, jnp.where(column == 1, total - high_half, 0.0))
         last = jnp.concatenate([last, spare], axis=1).astype(jnp.bfloat16)
 
-        def put(ref, part):
+        def put(ref, at, part):
             if part < len(known):
-                ref[...] = known_refs[part][...]
+                ref[at : at + known[part].shape[0], :] = known_refs[part][...]
             else:
                 low, high = cuts[part - len(known)]
-                ref[:, :edge] = main[low:high, :]
-                ref[:, edge:] = last[low:high, :]
+                ref[at : at + high - low, :edge] = main[low:high, :]
+                ref[at : at + high - low, edge:] = last[low:high, :]
 
         if not route:
             for part, ref in enumerate(lat_refs):
-                put(ref, part)
-        else:
-            lat_refs[0][...] = jnp.zeros_like(lat_refs[0])
-            for when, ref in zip(route, lat_refs, strict=True):
+                put(ref, 0, part)
+        for whens, ref in zip(route, lat_refs, strict=False):
+            for block, when in enumerate(whens):
                 for part in range(len(known) + len(cuts)):
-                    pl.when(when(part))(lambda ref=ref, part=part: put(ref, part))
+                    pl.when(when() == part)(
+                        lambda ref=ref, block=block, part=part: put(ref, block * height, part)
+                    )
 
     sizes = [high - low for low, high in cuts]
-    outputs = [((rows, width), jnp.bfloat16)]
-    outputs += [((size, padded), jnp.bfloat16) for size in ([sizes[0]] * len(route) if route else sizes)]
+    height = sizes[0]
+    if route:
+        sizes = [height * len(whens) for whens in route]
+    outputs = [((rows, width), jnp.bfloat16)] + [((size, padded), jnp.bfloat16) for size in sizes]
     mtp, *parts = kernel(body, "latent_partial", [own, received, gain, resident(w_latent), *known], outputs)
     return mtp, parts
 
 
-def add_early(choices, arrays, rows):
-    shape = (rows, choices[0][1].shape[1])
-
-    def body(*refs):
-        total = refs[-1]
-        value = jnp.zeros(shape, jnp.float32)
-        for (when, _), ref in zip(choices, refs, strict=False):
-            part = ref[...].astype(jnp.float32)
-            value = value + (part if when is None else jnp.where(when(), part, 0.0))
-        total[...] = value
-        for (at, array), ref in zip(arrays, refs[len(choices) : -1], strict=True):
-            total[at : at + array.shape[0], :] += ref[...].astype(jnp.float32)
-
-    inputs = [array for _, array in choices] + [array for _, array in arrays]
-    return kernel(body, "add_early", inputs, [(shape, jnp.float32)])[0]
-
-
-def place_rows(choices, blocks, shape):
-    height = shape[0] // blocks
+def add_parts(inner, outer, pairs, single, far, is_end):
+    rows, width = inner.shape
+
+    def body(inner_ref, outer_ref, first_ref, second_ref, single_ref, far_ref, base_ref, owed_ref):
+        outer_sum = outer_ref[...].astype(jnp.float32) + far_ref[...].astype(jnp.float32)
+        inner_sum = inner_ref[...].astype(jnp.float32) + single_ref[...].astype(jnp.float32)
+        for ref in (first_ref, second_ref):
+            inner_sum = inner_sum + ref[:rows, :].astype(jnp.float32)
+            outer_sum = outer_sum + ref[rows:, :].astype(jnp.float32)
+        base_ref[...] = jnp.where(is_end(), outer_sum, inner_sum)
+        owed_ref[...] = outer_sum.astype(jnp.bfloat16)
+
+    return kernel(
+        body,
+        "add_parts",
+        [inner, outer, *pairs, single, far],
+        [((rows, width), jnp.float32), ((rows, width), jnp.bfloat16)],
+    )
+
+
+def place_rows(choices, shape, swaps):
+    height = shape[0] // 4
 
     def body(*refs):
         out = refs[-1]
-        for (block, row, when, array), ref in zip(choices, refs, strict=False):
+        swapped = swaps()
+        for (shard, first, when, array), ref in zip(choices, refs, strict=False):
 
             @pl.when(when())
-            def _(block=block, row=row, array=array, ref=ref):
-                out[block * height + row : block * height + row + array.shape[0], :] = ref[...]
+            def _(shard=shard, first=first, array=array, ref=ref):
+                for at in range(array.shape[0] // height):
+                    half = first + at
+                    row = (2 * shard + half + (1 - 2 * half) * swapped) * height
+                    out[pl.ds(pl.multiple_of(row, height), height), :] = ref[at * height : (at + 1) * height, :]
 
     return kernel(body, "place_rows", [choice[-1] for choice in choices], [(shape, jnp.bfloat16)])[0]
 
@@ -310,18 +349,6 @@
     )
 
 
-def rounds_of(pairs):
-    lists = []
-    for source, target in pairs:
-        for chosen in lists:
-            if all(source != s and target != t for s, t in chosen):
-                chosen.append((source, target))
-                break
-        else:
-            lists.append([(source, target)])
-    return lists
-
-
 def shards_line(
     hidden_in, embed_in, hidden_gain, embed_gain, w_hidden, w_embed, attn_gain, w_latent, q_gain, kv_gain
 ):
@@ -329,7 +356,6 @@
     last = line - 1
     shard = hidden_in.shape[0]
     rows_out = shard // 2
-    cuts = cuts_of(shard)
     halves = ((0, rows_out), (rows_out, shard))
 
     def me():
@@ -354,105 +380,125 @@
     def senders_of(k):
         return [(d, owner(s)) for d in range(line) for s in shard_of(k, d)]
 
-    def send_latent(k, low, value):
-        pairs = []
-        for d in range(line):
-            for s in shard_of(k, d):
-                target = (s % 2) * 2 + low // rows_out
-                if target != d:
-                    pairs.append((device(d, owner(s)), device(target, owner(s))))
-        return [
-            (low % rows_out, lax.ppermute(value, ("dp", "mp"), chosen)) for chosen in rounds_of(pairs)
-        ]
-
-    pieces, sums = enter(hidden_in, embed_in, cuts)
+    def upper():
+        return jnp.where(me() >= line // 2, 1, 0)
+
+    first_piece, sums = enter(hidden_in, embed_in, upper)
     tokens = lax.axis_size("mp") * line * rows_out
     tables = rope_tables(
         w_latent.shape[1] - Q_LAT - KV_LAT, jnp.arange(tokens, dtype=jnp.int32) % LENGTH
     )
     small = [gain[None, :] for gain in (hidden_gain, embed_gain, attn_gain, q_gain, kv_gain)] + list(tables)
-    (w_hidden, w_embed, w_latent), small = lax.optimization_barrier(((w_hidden, w_embed, w_latent.T), small))
+    w_latent = w_latent.T
     hidden_gain, embed_gain, attn_gain, q_gain, kv_gain, cosine, sine_grid = small
     weights = (hidden_gain, embed_gain, w_hidden, w_embed)
 
     other_sums = lax.ppermute(sums, "mp", [(0, 1), (1, 0)])
-    piece, sums = pack(hidden_in, embed_in, sums, other_sums, cuts[-1][0])
-    pieces.append(piece)
-    ahead = [pieces]
-    back = [pieces]
-    for k in range(1, line):
-        if k == 2:
-            ahead[1][0], back[1][0], sums = lax.optimization_barrier((ahead[1][0], back[1][0], sums))
-            groups = [([piece], sums, low) for piece, (low, _) in zip(pieces, cuts, strict=True)]
-            got_own = project(groups, weights, cost=SOME_COST)
-            ahead[1][-1], back[1][-1], got_own, sums = lax.optimization_barrier(
-                (ahead[1][-1], back[1][-1], got_own, sums)
-            )
-        ahead.append([lax.ppermute(x, "dp", [(i, i + 1) for i in range(k - 1, last)]) for x in ahead[-1]])
-        back.append([lax.ppermute(x, "dp", [(i + 1, i) for i in range(0, line - k)]) for x in back[-1]])
+    second_piece, sums = pack(hidden_in, embed_in, sums, other_sums, upper)
+    pieces = [first_piece, second_piece]
+    token = warm([sums, hidden_gain, embed_gain, attn_gain, q_gain, kv_gain, cosine, sine_grid], [w_hidden, w_embed])
+    sums_three = lax.ppermute(sums, "dp", [(0, last), (last, 0)])
+
+    def go_ahead(x, k):
+        return lax.ppermute(x, "dp", [(i, i + 1) for i in range(k - 1, last)])
+
+    def go_back(x, k):
+        return lax.ppermute(x, "dp", [(i + 1, i) for i in range(0, line - k)])
+
+    ahead_one = [go_ahead(x, 1) for x in pieces]
+    back_one = [go_back(x, 1) for x in pieces]
+    ahead_one[0], back_one[0], token = lax.optimization_barrier((ahead_one[0], back_one[0], token))
+    ahead_two = [go_ahead(ahead_one[0], 2)]
+    back_two = [go_back(back_one[0], 2)]
+    sums = after(sums, token, ahead_one[0], back_one[0])
+    groups = [([piece], sums, low) for piece, (low, _) in zip(pieces, halves, strict=True)]
+    got_own = project(groups, weights)
+    ahead_one[1], back_one[1], got_own, sums_three = lax.optimization_barrier(
+        (ahead_one[1], back_one[1], got_own, sums_three)
+    )
+    ahead_two.append(go_ahead(ahead_one[1], 2))
+    back_two.append(go_back(back_one[1], 2))
     mtp_own, lat_own = latent_partial(got_own, to_owner(got_own, senders_of(0)), attn_gain, w_latent, halves)
-    sums_three = lax.ppermute(sums, "dp", [(0, last), (last, 0)])
+
+    def from_ahead():
+        return me() >= line // 2
+
+    ahead_two[0], back_two[0], lat_own = lax.optimization_barrier((ahead_two[0], back_two[0], lat_own))
+    two = [choose(ahead_two[0], back_two[0], from_ahead)]
+    ends_on = [(line - 2, last), (1, 0)]
+    three = [lax.ppermute(two[0], "dp", ends_on)]
 
     def ahead_is_own():
         near = jnp.where(me() >= 1, me() - 1, me() + 1)
         owned = jnp.where(near >= line // 2, 1, 0) == mine()
         return jnp.where(me() >= 1, owned, jnp.logical_not(owned))
 
-    def routed(offset):
-        def when(part):
-            to = me() + offset
-            to = jnp.where(to >= line, to - line, to)
-            upper = jnp.where(to >= line // 2, 1, 0)
-            step = jnp.abs(me() - (2 * mine() + upper))
-            return jnp.logical_and(step == part // 2, to - upper * (line // 2) == part % 2)
-
-        return when
-
-    one = lax.optimization_barrier((ahead[1], back[1], ahead[2], back[2], lat_own))
-    groups = [([x], [one[0][-1]], low) for x, (low, _) in zip(one[0], cuts, strict=True)]
-    groups += [([x], [one[1][-1]], low) for x, (low, _) in zip(one[1], cuts, strict=True)]
-    got, other = project(groups, weights, own_first=ahead_is_own)
-    mtp_one, (lat_base, *lat_routed) = latent_partial(
-        got,
-        to_owner(other, senders_of(1)),
+    one = lax.optimization_barrier((ahead_one, back_one, two[0]))
+    groups = [([x], [one[0][-1]], low) for x, (low, _) in zip(one[0], halves, strict=True)]
+    groups += [([x], [one[1][-1]], low) for x, (low, _) in zip(one[1], halves, strict=True)]
+    got_one, other_one = project(groups, weights, own_first=ahead_is_own)
+    received_one = to_owner(other_one, senders_of(1))
+    ahead_two[1], back_two[1], received_one = lax.optimization_barrier(
+        (ahead_two[1], back_two[1], received_one)
+    )
+    two.append(choose(ahead_two[1], back_two[1], from_ahead))
+    three.append(lax.ppermute(two[1], "dp", ends_on))
+    mtp_one, lat_one = latent_partial(got_one, received_one, attn_gain, w_latent, halves)
+
+    got_two = project([([x], [two[-1]], low) for x, (low, _) in zip(two, halves, strict=True)], weights)
+    received_two = to_owner(got_two, senders_of(2))
+    sums_three = after(sums_three, got_two)
+    got_three = [project([([three[0]], sums_three, 0)], weights)]
+    received_two = after(received_two, got_three[0])
+
+    def part_for(half, place):
+        return 2 * jnp.abs(me() - (2 * mine() + half)) + jnp.where(mine() == 1, 1 - place, place)
+
+    mtp_two, (inner, outer, away) = latent_partial(
+        got_two,
+        received_two,
         attn_gain,
         w_latent,
         halves,
-        known=one[4],
-        route=[routed(offset) for offset in range(line)],
-    )
-    early = []
-    for offset, part in enumerate(lat_routed, 1):
-        pairs = []
-        for m in range(2):
-            for d in range(line):
-                to = (d + offset) % line
-                if abs(d - (2 * m + to // 2)) <= 1:
-                    pairs.append((device(d, m), device(to, m)))
-        early.append((0, lax.ppermute(part, ("dp", "mp"), pairs)))
-
-    two = lax.optimization_barrier((ahead[2], back[2], got))
-    groups = [([x, y], [two[0][-1], two[1][-1]], low) for x, y, (low, _) in zip(*two[:2], cuts, strict=True)]
-    got = project(groups, weights)
-    mtp_two, lat_two = latent_partial(got, to_owner(got, senders_of(2)), attn_gain, w_latent, halves)
-    early_two = []
-    for (low, _), part in zip(halves, lat_two, strict=True):
-        early_two += send_latent(2, low, part)
-
-    mtp_three = []
-    late = []
-    sums_three = after(sums_three, got, lat_base)
-    for x, y, (low, high) in zip(ahead[3], back[3], cuts, strict=True):
-        ends = high == shard
-        got = project([([x, y], sums_three, low)], weights, cost=MORE_COST if ends else SOME_COST)
-        received = to_owner(got, senders_of(3))
-        if ends:
-            received = after(received, early, early_two)
-        mtp, (lat,) = latent_partial(got, received, attn_gain, w_latent, ((0, high - low),))
-        mtp_three.append(mtp)
-        late += send_latent(3, low, lat)
-        sums_three = after(sums_three, got, lat_two)
-    early += early_two
+        known=[*lat_own, *lat_one],
+        route=[
+            [lambda: part_for(upper(), 1 - upper())],
+            [lambda: part_for(upper(), upper())],
+            [lambda: part_for(1 - upper(), upper()), lambda: part_for(1 - upper(), 1 - upper())],
+        ],
+    )
+
+    def send(value, pairs):
+        pairs = [(device(d, m), device(to, m)) for m, d, to in pairs]
+        return lax.ppermute(value, ("dp", "mp"), pairs)
+
+    both = range(2)
+    crossing = [
+        send(away, [(0, 0, 2), (1, 3, 1)]),
+        send(away, [(m, d, to) for m in both for d, to in ((1, 2), (2, 1))]),
+    ]
+    single = send(inner, [(m, d, to) for m in both for d, to in ((0, 1), (3, 2))])
+
+    to_middle = [(0, last, 1), (1, 0, 2)]
+    whole = ((0, rows_out),)
+    mtp, (lat,) = latent_partial(
+        got_three[0], to_owner(got_three[0], senders_of(3)), attn_gain, w_latent, whole
+    )
+    mtp_three = [mtp]
+    far = send(lat, to_middle)
+    sums_three = after(sums_three, got_three[0], inner, lat)
+    got_three.append(project([([three[1]], sums_three, rows_out)], weights))
+    mtp, (lat,) = latent_partial(
+        got_three[1], to_owner(got_three[1], senders_of(3)), attn_gain, w_latent, whole
+    )
+    mtp_three.append(mtp)
+
+    def is_end():
+        return jnp.logical_or(me() == 0, me() == last)
+
+    base, owed = add_parts(inner, outer, crossing, single, far, is_end)
+    owed = send(owed, [(m, d, to) for m in both for d, to in ((1, 0), (2, last))])
+    late = [(0, owed), (0, send(lat, to_middle))]
 
     def distance(offset):
         return jnp.abs(me() - (2 * mine() + offset))
@@ -461,22 +507,14 @@
     for offset in range(2):
         for k, mtp in enumerate((mtp_own, mtp_one, mtp_two)):
             choices.append((offset, 0, lambda offset=offset, k=k: distance(offset) == k, mtp))
-        for (low, _), mtp in zip(cuts, mtp_three, strict=True):
-            choices.append((offset, low, lambda offset=offset: distance(offset) == last, mtp))
-    mtp_hidden = place_rows(choices, 2, (2 * shard, w_hidden.shape[1]))
-
-    choices = [(None, lat_base)]
-    for half, part in enumerate(lat_two):
-        choices.append((lambda half=half: routed(0)(2 * 2 + half), part))
-    base = add_early(choices, early, rows_out)
+        for half, mtp in enumerate(mtp_three):
+            choices.append((offset, half, lambda offset=offset: distance(offset) == last, mtp))
+    mtp_hidden = place_rows(choices, (2 * shard, w_hidden.shape[1]), mine)
+
     q_latent, kv_latent, key_rope = finish(
         base, late, q_gain, kv_gain, cosine, sine_grid, lambda: (mine() * line + me()) * rows_out
     )
     return (mtp_hidden, q_latent, kv_latent, key_rope)
-
-
-def cuts_of(shard):
-    return ((0, shard // 2), (shard // 2, shard))
 
 
 def shards_any(

time: 185 us -> 159 us (0.86)
  waiting for transfers between devices: 65.3 us -> 48 us
  starting transfers between devices: 55.8 us -> 51 us
  local copies, waits for them, and re-layouts: 20 us -> 16.3 us
    ppermute x19 -> x16, waiting for transfers between devices: 60.1 us -> 30.2 us  [the longest x6 12.8 us: send(): return lax.ppermute(value, ('dp', 'mp'), pairs)]
    ppermute x5, waiting for transfers between devices: 2.45 us -> 15.1 us  [to_owner(): return lax.ppermute(value, ('dp', 'mp'), pairs)]
    ppermute x5, starting transfers between devices: 9.51 us -> 6.45 us  [to_owner(): return lax.ppermute(value, ('dp', 'mp'), pairs)]
    unnamed x28 -> x36, local copies, waits for them, and re-layouts: 17.2 us -> 14.9 us
    ppermute x19 -> x16, starting transfers between devices: 44 us -> 42.3 us  [the longest x4 16.5 us: go_ahead(): return lax.ppermute(x, 'dp', [(i, i + 1) for i in range(k - 1, last)])]
    pallas_call x15 -> x17, Pallas kernels: 40.6 us -> 40.3 us  [kernel(): pl.pallas_call(body, in_specs=[VMEM] * len(inputs), out_specs=[VMEM] * le...]
  transfers between devices with their start and end apart: 26 -> 23, of which waited for: 11 -> 11; matrix products, arithmetic and copies ran while one was open for 2% -> 2% of each run, Pallas kernels for 21% -> 25%
where the time goes in v3:
time: 159 us; the launch traced here: 158 us
  starting transfers between devices  51 us (32%)
  waiting for transfers between devices  48 us (30%)
  Pallas kernels  40.3 us (25%)
  local copies, waits for them, and re-layouts  16.3 us (10%)
    pallas_call x17, Pallas kernels, kernel(): pl.pallas_call(body, in_specs=[VMEM] * len(inputs), out_specs=[VMEM] * le...  40.3 us
    ppermute x4, starting transfers between devices, go_ahead(): return lax.ppermute(x, 'dp', [(i, i + 1) for i in range(k - 1, last)])  16.5 us
    ppermute x5, waiting for transfers between devices, to_owner(): return lax.ppermute(value, ('dp', 'mp'), pairs)  15.1 us
    unnamed x36, local copies, waits for them, and re-layouts  14.9 us
    ppermute x6, starting transfers between devices, send(): return lax.ppermute(value, ('dp', 'mp'), pairs)  13.2 us
    ppermute x6, waiting for transfers between devices, send(): return lax.ppermute(value, ('dp', 'mp'), pairs)  12.8 us
    ppermute x4, starting transfers between devices, go_back(): return lax.ppermute(x, 'dp', [(i + 1, i) for i in range(0, line - k)])  9.59 us
    ppermute x4, waiting for transfers between devices, go_ahead(): return lax.ppermute(x, 'dp', [(i, i + 1) for i in range(k - 1, last)])  8.31 us
  transfers between devices with their start and end apart: 23, of which 11 were waited for; matrix products, arithmetic and copies ran while one was open for 2% of the time, Pallas kernels for 25%

profile of v3, /device:TPU:8, one launch (start us, length us, event | category | flops | bytes accessed | tf_op | source)
XLA Modules:
  0.0 157.8 jit_solution(4822054648201346026)
XLA Ops:
  0.6 1.2 copy-done.3
  1.8 1.2 copy-done.4
  3.5 3.5 %collective-permute-start.3 = (bf16[64,7296]{1,0:T(8,128)(2,1)S(1)}, bf16[64,7296]{1,0:T(8,128)(2,1)S(1)}, u32[]{:S(2)}, u32[]{:S(2)}) collective-permute-start(bf16[64,7296]{1,0:T(8,128)(2,1)S(1)} %get-tuple-element.52.refs_0_), channel_id=1, source_target_pairs={{0,2},{2,4},{4,6},{1,3},{3,5},{5,7},{8,10},{10,12},{12,14},{9,11},... | collective-permute-start | bytes 2801672 | tf_op jit(solution)/shard_map/ppermute | solution.py:403
  6.9 2.4 %collective-permute-start.4 = (bf16[64,7296]{1,0:T(8,128)(2,1)S(1)}, bf16[64,7296]{1,0:T(8,128)(2,1)}, u32[]{:S(2)}, u32[]{:S(2)}) collective-permute-start(bf16[64,7296]{1,0:T(8,128)(2,1)S(1)} %get-tuple-element.52.refs_0_), channel_id=1, source_target_pairs={{2,0},{4,2},{6,4},{3,1},{5,3},{7,5},{10,8},{12,10},{14,12},{11,9},... | collective-permute-start | bytes 2801672 | tf_op jit(solution)/shard_map/ppermute | solution.py:406
  9.4 1.6 %collective-permute-start = (f32[128,128]{1,0:T(8,128)S(1)}, f32[128,128]{1,0:T(8,128)S(1)}, u32[]{:S(2)}, u32[]{:S(2)}) collective-permute-start(f32[128,128]{1,0:T(8,128)S(1)} %get-tuple-element.50.sums_ref), channel_id=1, source_target_pairs={{0,1},{1,0},{2,3},{3,2},{4,5},{5,4},{6,7},{7,6},{8,9},{9,8},{10,11... | collective-permute-start | bytes 196616 | tf_op jit(solution)/shard_map/ppermute | solution.py:396
  10.9 2.7 %collective-permute-done.other_ref = f32[128,128]{1,0:T(8,128)S(1)} collective-permute-done((f32[128,128]{1,0:T(8,128)S(1)}, f32[128,128]{1,0:T(8,128)S(1)}, u32[]{:S(2)}, u32[]{:S(2)}) %collective-permute-start) | collective-permute-done | bytes 65568 | tf_op jit(solution)/shard_map/ppermute | solution.py:396
  13.8 3.4 %collective-permute-start.1 = (bf16[64,7296]{1,0:T(8,128)(2,1)S(1)}, bf16[64,7296]{1,0:T(8,128)(2,1)}, u32[]{:S(2)}, u32[]{:S(2)}) collective-permute-start(bf16[64,7296]{1,0:T(8,128)(2,1)S(1)} %get-tuple-element.51.refs_2_), channel_id=1, source_target_pairs={{0,2},{2,4},{4,6},{1,3},{3,5},{5,7},{8,10},{10,12},{12,14},{9,11},... | collective-permute-start | bytes 2801672 | tf_op jit(solution)/shard_map/ppermute | solution.py:403
  17.3 3.4 %collective-permute-start.2 = (bf16[64,7296]{1,0:T(8,128)(2,1)S(1)}, bf16[64,7296]{1,0:T(8,128)(2,1)}, u32[]{:S(2)}, u32[]{:S(2)}) collective-permute-start(bf16[64,7296]{1,0:T(8,128)(2,1)S(1)} %get-tuple-element.51.refs_2_), channel_id=1, source_target_pairs={{2,0},{4,2},{6,4},{3,1},{5,3},{7,5},{10,8},{12,10},{14,12},{11,9},... | collective-permute-start | bytes 2801672 | tf_op jit(solution)/shard_map/ppermute | solution.py:406
  20.6 8.3 %collective-permute-done.3.refs_0_ = bf16[64,7296]{1,0:T(8,128)(2,1)S(1)} collective-permute-done((bf16[64,7296]{1,0:T(8,128)(2,1)S(1)}, bf16[64,7296]{1,0:T(8,128)(2,1)S(1)}, u32[]{:S(2)}, u32[]{:S(2)}) %collective-permute-start.3) | collective-permute-done | bytes 933920 | tf_op jit(solution)/shard_map/ppermute | solution.py:403
  28.9 3.6 %collective-permute-done.4.refs_2_ = bf16[64,7296]{1,0:T(8,128)(2,1)} collective-permute-done((bf16[64,7296]{1,0:T(8,128)(2,1)S(1)}, bf16[64,7296]{1,0:T(8,128)(2,1)}, u32[]{:S(2)}, u32[]{:S(2)}) %collective-permute-start.4) | collective-permute-done | bytes 933920 | tf_op jit(solution)/shard_map/ppermute | solution.py:406
  32.6 4.4 %collective-permute-start.7 = (bf16[64,7296]{1,0:T(8,128)(2,1)S(1)}, bf16[64,7296]{1,0:T(8,128)(2,1)}, u32[]{:S(2)}, u32[]{:S(2)}) collective-permute-start(bf16[64,7296]{1,0:T(8,128)(2,1)S(1)} %collective-permute-done.3.refs_0_), channel_id=1, source_target_pairs={{2,4},{4,6},{3,5},{5,7},{10,12},{12,14},{11,13},{13,15},{18,20},{2... | collective-permute-start | bytes 2801672 | tf_op jit(solution)/shard_map/ppermute | solution.py:403
  37.0 1.9 %collective-permute-start.8 = (bf16[64,7296]{1,0:T(8,128)(2,1)}, bf16[64,7296]{1,0:T(8,128)(2,1)}, u32[]{:S(2)}, u32[]{:S(2)}) collective-permute-start(bf16[64,7296]{1,0:T(8,128)(2,1)} %collective-permute-done.4.refs_2_), channel_id=1, source_target_pairs={{2,0},{4,2},{3,1},{5,3},{10,8},{12,10},{11,9},{13,11},{18,16},{20,... | collective-permute-start | bytes 2801672 | tf_op jit(solution)/shard_map/ppermute | solution.py:406
  41.0 4.6 %copy-done = bf16[3584,1792]{1,0:T(8,128)(2,1)S(1)} copy-done((bf16[3584,1792]{1,0:T(8,128)(2,1)S(1)}, bf16[3584,1792]{1,0:T(8,128)(2,1)}, u32[]{:S(2)}) %copy-start) | copy-done | bytes 12845080
  45.7 4.6 %copy-done.1 = bf16[3584,1792]{1,0:T(8,128)(2,1)S(1)} copy-done((bf16[3584,1792]{1,0:T(8,128)(2,1)S(1)}, bf16[3584,1792]{1,0:T(8,128)(2,1)}, u32[]{:S(2)}) %copy-start.1) | copy-done | bytes 12845080
  50.4 3.5 %project.5.own_ref = bf16[128,1792]{1,0:T(8,128)(2,1)S(1)} custom-call(bf16[64,7296]{1,0:T(8,128)(2,1)S(1)} %get-tuple-element.52.refs_0_, f32[128,128]{1,0:T(8,128)S(1)} %get-tuple-element.56.refs_1_, bf16[64,7296]{1,0:T(8,128)(2,1)S(1)} %get-tuple-element.51.refs_2_, f32[1,3584]{1,0:T(1,128)S(1)} %broadcast_in_dim.17.refs_3_.refs_4_.refs_2_, ...), custom_call_target="tpu_custom_call" | custom-call | tf_op jit(solution)/shard_map/project/pallas_call | solution.py:65
  54.0 5.2 %collective-permute-start.9 = (bf16[64,7296]{1,0:T(8,128)(2,1)}, bf16[64,7296]{1,0:T(8,128)(2,1)S(1)}, u32[]{:S(2)}, u32[]{:S(2)}) collective-permute-start(bf16[64,7296]{1,0:T(8,128)(2,1)} %collective-permute-done.1.refs_1_), channel_id=1, source_target_pairs={{2,4},{4,6},{3,5},{5,7},{10,12},{12,14},{11,13},{13,15},{18,20},{2... | collective-permute-start | bytes 2801672 | tf_op jit(solution)/shard_map/ppermute | solution.py:403
  59.1 1.9 %collective-permute-start.10 = (bf16[64,7296]{1,0:T(8,128)(2,1)}, bf16[64,7296]{1,0:T(8,128)(2,1)S(1)}, u32[]{:S(2)}, u32[]{:S(2)}) collective-permute-start(bf16[64,7296]{1,0:T(8,128)(2,1)} %collective-permute-done.2.refs_3_), channel_id=1, source_target_pairs={{2,0},{4,2},{3,1},{5,3},{10,8},{12,10},{11,9},{13,11},{18,16},{20,... | collective-permute-start | bytes 2801672 | tf_op jit(solution)/shard_map/ppermute | solution.py:406
  61.1 1.3 collective-permute-start.6
  62.4 9.3 %collective-permute-done.6.received_ref = bf16[128,1792]{1,0:T(8,128)(2,1)S(1)} collective-permute-done((bf16[128,1792]{1,0:T(8,128)(2,1)S(1)}, bf16[128,1792]{1,0:T(8,128)(2,1)S(1)}, u32[]{:S(2)}, u32[]{:S(2)}) %collective-permute-start.6) | collective-permute-done | bytes 458784 | tf_op jit(solution)/shard_map/ppermute | solution.py:375
  71.7 3.1 %copy-done.2 = bf16[1792,2112]{0,1:T(8,128)(2,1)S(1)} copy-done((bf16[1792,2112]{0,1:T(8,128)(2,1)S(1)}, bf16[1792,2112]{0,1:T(8,128)(2,1)}, u32[]{:S(2)}) %copy-start.2) | copy-done | bytes 7569432
  74.9 2.6 %latent_partial.5 = (bf16[128,1792]{1,0:T(8,128)(2,1)S(1)}, bf16[64,2176]{1,0:T(8,128)(2,1)S(1)}, bf16[64,2176]{1,0:T(8,128)(2,1)S(1)}) custom-call(bf16[128,1792]{1,0:T(8,128)(2,1)S(1)} %project.5.own_ref, bf16[128,1792]{1,0:T(8,128)(2,1)S(1)} %collective-permute-done.6.received_ref, f32[1,1792]{1,0:T(1,128)S(1)} %broadcast_in_dim.19.gain_ref, ...), custom_call_target="tpu_custom_call" | custom-call | tf_op jit(solution)/shard_map/latent_partial/pallas_call | solution.py:65
  77.5 1.5 choose.2.refs_0_
  79.1 8.7 %project.6 = (bf16[128,1792]{1,0:T(8,128)(2,1)S(1)}, bf16[128,1792]{1,0:T(8,128)(2,1)S(1)}) custom-call(bf16[64,7296]{1,0:T(8,128)(2,1)S(1)} %collective-permute-done.3.refs_0_, bf16[64,7296]{1,0:T(8,128)(2,1)} %collective-permute-done.1.refs_1_, bf16[64,7296]{1,0:T(8,128)(2,1)} %collective-permute-done.4.refs_2_, ...), custom_call_target="tpu_custom_call" | custom-call | tf_op jit(solution)/shard_map/project/pallas_call | solution.py:65
  87.8 1.9 %collective-permute-start.11 = (bf16[128,1792]{1,0:T(8,128)(2,1)S(1)}, bf16[128,1792]{1,0:T(8,128)(2,1)S(1)}, u32[]{:S(2)}, u32[]{:S(2)}) collective-permute-start(bf16[128,1792]{1,0:T(8,128)(2,1)S(1)} %get-tuple-element.70), channel_id=1, source_target_pairs={{1,0},{3,2},{2,3},{5,4},{4,5},{6,7},{9,8},{11,10},{10,11},{13,12},... | collective-permute-start | bytes 1376264 | tf_op jit(solution)/shard_map/ppermute | solution.py:375
  89.7 1.3 collective-permute-start.13
  91.1 1.3 collective-permute-done.10.second_ref
  92.4 5.8 %collective-permute-done.11.received_ref = bf16[128,1792]{1,0:T(8,128)(2,1)S(1)} collective-permute-done((bf16[128,1792]{1,0:T(8,128)(2,1)S(1)}, bf16[128,1792]{1,0:T(8,128)(2,1)S(1)}, u32[]{:S(2)}, u32[]{:S(2)}) %collective-permute-start.11) | collective-permute-done | bytes 458784 | tf_op jit(solution)/shard_map/ppermute | solution.py:375
  98.3 1.7 %collective-permute-start.15 = (bf16[64,7296]{1,0:T(8,128)(2,1)S(1)}, bf16[64,7296]{1,0:T(8,128)(2,1)S(1)}, u32[]{:S(2)}, u32[]{:S(2)}) collective-permute-start(bf16[64,7296]{1,0:T(8,128)(2,1)S(1)} %choose.3.refs_1_), channel_id=1, source_target_pairs={{4,6},{2,0},{5,7},{3,1},{12,14},{10,8},{13,15},{11,9},{20,22},{18,... | collective-permute-start | bytes 2801672 | tf_op jit(solution)/shard_map/ppermute | solution.py:445
  100.0 3.7 %project.7.own_ref = bf16[128,1792]{1,0:T(8,128)(2,1)S(1)} custom-call(bf16[64,7296]{1,0:T(8,128)(2,1)S(1)} %choose.2.refs_0_, bf16[64,7296]{1,0:T(8,128)(2,1)S(1)} %choose.3.refs_1_, f32[1,3584]{1,0:T(1,128)S(1)} %broadcast_in_dim.17.refs_3_.refs_4_.refs_2_, f32[1,3584]{1,0:T(1,128)S(1)} %broadcast_in_dim.18.refs_4_.refs_5_.refs_3_, ...), custom_call_target="tpu_custom_call" | custom-call | tf_op jit(solution)/shard_map/project/pallas_call | solution.py:65
  103.6 1.9 %collective-permute-start.12 = (bf16[128,1792]{1,0:T(8,128)(2,1)S(1)}, bf16[128,1792]{1,0:T(8,128)(2,1)S(1)}, u32[]{:S(2)}, u32[]{:S(2)}) collective-permute-start(bf16[128,1792]{1,0:T(8,128)(2,1)S(1)} %project.7.own_ref), channel_id=1, source_target_pairs={{0,1},{2,3},{5,4},{7,6},{8,9},{10,11},{13,12},{15,14},{16,17},{18,... | collective-permute-start | bytes 1376264 | tf_op jit(solution)/shard_map/ppermute | solution.py:375
  105.5 2.6 %latent_partial.6 = (bf16[128,1792]{1,0:T(8,128)(2,1)S(1)}, bf16[64,2176]{1,0:T(8,128)(2,1)S(1)}, bf16[64,2176]{1,0:T(8,128)(2,1)S(1)}) custom-call(bf16[128,1792]{1,0:T(8,128)(2,1)S(1)} %get-tuple-element.69.own_ref, bf16[128,1792]{1,0:T(8,128)(2,1)S(1)} %collective-permute-done.11.received_ref, f32[1,1792]{1,0:T(1,128)S(1)} %broadcast_in_dim.19.gain_ref, ...), custom_call_target="tpu_custom_call" | custom-call | tf_op jit(solution)/shard_map/latent_partial/pallas_call | solution.py:65
  108.1 4.1 %collective-permute-done.13.refs_0_ = bf16[64,7296]{1,0:T(8,128)(2,1)S(1)} collective-permute-done((bf16[64,7296]{1,0:T(8,128)(2,1)S(1)}, bf16[64,7296]{1,0:T(8,128)(2,1)S(1)}, u32[]{:S(2)}, u32[]{:S(2)}) %collective-permute-start.13) | collective-permute-done | bytes 933920 | tf_op jit(solution)/shard_map/ppermute | solution.py:429
  112.2 3.6 %project.8.own_ref = bf16[64,1792]{1,0:T(8,128)(2,1)S(1)} custom-call(bf16[64,7296]{1,0:T(8,128)(2,1)S(1)} %collective-permute-done.13.refs_0_, f32[128,128]{1,0:T(8,128)S(1)} %collective-permute-done.5.refs_1_, f32[1,3584]{1,0:T(1,128)S(1)} %broadcast_in_dim.17.refs_3_.refs_4_.refs_2_, f32[1,3584]{1,0:T(1,128)S(1)} %broadcast_in_dim.18.refs_4_.refs_5_.refs_3_, ...), custom_call_target="tpu_custom_call" | custom-call | tf_op jit(solution)/shard_map/project/pallas_call | solution.py:65
  115.8 2.8 %latent_partial.7 = (bf16[128,1792]{1,0:T(8,128)(2,1)S(1)}, bf16[64,2176]{1,0:T(8,128)(2,1)S(1)}, bf16[64,2176]{1,0:T(8,128)(2,1)S(1)}, bf16[128,2176]{1,0:T(8,128)(2,1)S(1)}) custom-call(bf16[128,1792]{1,0:T(8,128)(2,1)S(1)} %project.7.own_ref, bf16[128,1792]{1,0:T(8,128)(2,1)S(1)} %collective-permute-done.12.received_ref, ...), custom_call_target="tpu_custom_call" | custom-call | tf_op jit(solution)/shard_map/latent_partial/pallas_call | solution.py:65
  119.3 5.8 %collective-permute-start.18 = (bf16[128,2176]{1,0:T(8,128)(2,1)S(1)}, bf16[128,2176]{1,0:T(8,128)(2,1)S(1)}, u32[]{:S(2)}, u32[]{:S(2)}) collective-permute-start(bf16[128,2176]{1,0:T(8,128)(2,1)S(1)} %get-tuple-element.89), channel_id=1, source_target_pairs={{2,4},{4,2},{3,5},{5,3},{10,12},{12,10},{11,13},{13,11},{18,20},{2... | collective-permute-start | bytes 1671176 | tf_op jit(solution)/shard_map/ppermute | solution.py:473
  125.8 1.3 collective-permute-start.19
  127.1 2.4 %latent_partial.8 = (bf16[64,1792]{1,0:T(8,128)(2,1)S(1)}, bf16[64,2176]{1,0:T(8,128)(2,1)S(1)}) custom-call(bf16[64,1792]{1,0:T(8,128)(2,1)S(1)} %project.8.own_ref, bf16[64,1792]{1,0:T(8,128)(2,1)S(1)} %collective-permute-done.14.received_ref, f32[1,1792]{1,0:T(1,128)S(1)} %broadcast_in_dim.19.gain_ref, bf16[2112,1792]{1,0:T(8,128)(2,1)S(1)} %bitcast.11), custom_call_target="tpu_custom_call" | custom-call | tf_op jit(solution)/shard_map/latent_partial/pallas_call | solution.py:65
  129.5 1.5 collective-permute-start.20
  131.1 3.6 %project.9.own_ref = bf16[64,1792]{1,0:T(8,128)(2,1)S(1)} custom-call(bf16[64,7296]{1,0:T(8,128)(2,1)S(1)} %collective-permute-done.15.refs_0_, f32[128,128]{1,0:T(8,128)S(1)} %collective-permute-done.5.refs_1_, f32[1,3584]{1,0:T(1,128)S(1)} %broadcast_in_dim.17.refs_3_.refs_4_.refs_2_, f32[1,3584]{1,0:T(1,128)S(1)} %broadcast_in_dim.18.refs_4_.refs_5_.refs_3_, ...), custom_call_target="tpu_custom_call" | custom-call | tf_op jit(solution)/shard_map/project/pallas_call | solution.py:65
  135.3 2.5 %collective-permute-done.19.single_ref = bf16[64,2176]{1,0:T(8,128)(2,1)S(1)} collective-permute-done((bf16[64,2176]{1,0:T(8,128)(2,1)S(1)}, bf16[64,2176]{1,0:T(8,128)(2,1)S(1)}, u32[]{:S(2)}, u32[]{:S(2)}) %collective-permute-start.19) | collective-permute-done | bytes 278560 | tf_op jit(solution)/shard_map/ppermute | solution.py:473
  137.9 3.5 %collective-permute-done.20.far_ref = bf16[64,2176]{1,0:T(8,128)(2,1)S(1)} collective-permute-done((bf16[64,2176]{1,0:T(8,128)(2,1)S(1)}, bf16[64,2176]{1,0:T(8,128)(2,1)S(1)}, u32[]{:S(2)}, u32[]{:S(2)}) %collective-permute-start.20) | collective-permute-done | bytes 278560 | tf_op jit(solution)/shard_map/ppermute | solution.py:473
  142.5 2.6 %collective-permute-start.21 = (bf16[64,2176]{1,0:T(8,128)(2,1)S(1)}, bf16[64,2176]{1,0:T(8,128)(2,1)S(1)}, u32[]{:S(2)}, u32[]{:S(2)}) collective-permute-start(bf16[64,2176]{1,0:T(8,128)(2,1)S(1)} %get-tuple-element.91), channel_id=1, source_target_pairs={{2,0},{4,6},{3,1},{5,7},{10,8},{12,14},{11,9},{13,15},{18,16},{20,... | collective-permute-start | bytes 835592 | tf_op jit(solution)/shard_map/ppermute | solution.py:473
  145.1 2.4 %latent_partial.9 = (bf16[64,1792]{1,0:T(8,128)(2,1)S(1)}, bf16[64,2176]{1,0:T(8,128)(2,1)S(1)}) custom-call(bf16[64,1792]{1,0:T(8,128)(2,1)S(1)} %project.9.own_ref, bf16[64,1792]{1,0:T(8,128)(2,1)S(1)} %collective-permute-done.16.received_ref, f32[1,1792]{1,0:T(1,128)S(1)} %broadcast_in_dim.19.gain_ref, bf16[2112,1792]{1,0:T(8,128)(2,1)S(1)} %bitcast.12), custom_call_target="tpu_custom_call" | custom-call | tf_op jit(solution)/shard_map/latent_partial/pallas_call | solution.py:65
  147.5 1.3 collective-permute-start.22
  148.8 1.0 multiply_sine_fusion
  149.8 1.0 place_rows.1
  150.8 6.0 %collective-permute-done.22.refs_1_ = bf16[64,2176]{1,0:T(8,128)(2,1)S(1)} collective-permute-done((bf16[64,2176]{1,0:T(8,128)(2,1)S(1)}, bf16[64,2176]{1,0:T(8,128)(2,1)S(1)}, u32[]{:S(2)}, u32[]{:S(2)}) %collective-permute-start.22) | collective-permute-done | bytes 278560 | tf_op jit(solution)/shard_map/ppermute | solution.py:473
  156.8 1.0 finish.1
  (61 shorter events, 6.1 us)
Async XLA Ops:
  0.6 1.2 copy-start.3
  1.8 1.2 copy-start.4
  3.5 25.5 %collective-permute-start.3 = (bf16[64,7296]{1,0:T(8,128)(2,1)S(1)}, bf16[64,7296]{1,0:T(8,128)(2,1)S(1)}, u32[]{:S(2)}, u32[]{:S(2)}) collective-permute-start(bf16[64,7296]{1,0:T(8,128)(2,1)S(1)} %get-tuple-element.52.refs_0_), channel_id=1, source_target_pairs={{0,2},{2,4},{4,6},{1,3},{3,5},{5,7},{8,10},{10,12},{12,14},{9,11},... | collective-permute-start | bytes 2801672 | tf_op jit(solution)/shard_map/ppermute | solution.py:403
  6.9 25.6 %collective-permute-start.4 = (bf16[64,7296]{1,0:T(8,128)(2,1)S(1)}, bf16[64,7296]{1,0:T(8,128)(2,1)}, u32[]{:S(2)}, u32[]{:S(2)}) collective-permute-start(bf16[64,7296]{1,0:T(8,128)(2,1)S(1)} %get-tuple-element.52.refs_0_), channel_id=1, source_target_pairs={{2,0},{4,2},{6,4},{3,1},{5,3},{7,5},{10,8},{12,10},{14,12},{11,9},... | collective-permute-start | bytes 2801672 | tf_op jit(solution)/shard_map/ppermute | solution.py:406
  9.4 4.3 %collective-permute-start = (f32[128,128]{1,0:T(8,128)S(1)}, f32[128,128]{1,0:T(8,128)S(1)}, u32[]{:S(2)}, u32[]{:S(2)}) collective-permute-start(f32[128,128]{1,0:T(8,128)S(1)} %get-tuple-element.50.sums_ref), channel_id=1, source_target_pairs={{0,1},{1,0},{2,3},{3,2},{4,5},{5,4},{6,7},{7,6},{8,9},{9,8},{10,11... | collective-permute-start | bytes 196616 | tf_op jit(solution)/shard_map/ppermute | solution.py:396
  13.8 40.1 %collective-permute-start.1 = (bf16[64,7296]{1,0:T(8,128)(2,1)S(1)}, bf16[64,7296]{1,0:T(8,128)(2,1)}, u32[]{:S(2)}, u32[]{:S(2)}) collective-permute-start(bf16[64,7296]{1,0:T(8,128)(2,1)S(1)} %get-tuple-element.51.refs_2_), channel_id=1, source_target_pairs={{0,2},{2,4},{4,6},{1,3},{3,5},{5,7},{8,10},{10,12},{12,14},{9,11},... | collective-permute-start | bytes 2801672 | tf_op jit(solution)/shard_map/ppermute | solution.py:403
  17.3 36.7 %collective-permute-start.2 = (bf16[64,7296]{1,0:T(8,128)(2,1)S(1)}, bf16[64,7296]{1,0:T(8,128)(2,1)}, u32[]{:S(2)}, u32[]{:S(2)}) collective-permute-start(bf16[64,7296]{1,0:T(8,128)(2,1)S(1)} %get-tuple-element.51.refs_2_), channel_id=1, source_target_pairs={{2,0},{4,2},{6,4},{3,1},{5,3},{7,5},{10,8},{12,10},{14,12},{11,9},... | collective-permute-start | bytes 2801672 | tf_op jit(solution)/shard_map/ppermute | solution.py:406
  32.6 44.9 %collective-permute-start.7 = (bf16[64,7296]{1,0:T(8,128)(2,1)S(1)}, bf16[64,7296]{1,0:T(8,128)(2,1)}, u32[]{:S(2)}, u32[]{:S(2)}) collective-permute-start(bf16[64,7296]{1,0:T(8,128)(2,1)S(1)} %collective-permute-done.3.refs_0_), channel_id=1, source_target_pairs={{2,4},{4,6},{3,5},{5,7},{10,12},{12,14},{11,13},{13,15},{18,20},{2... | collective-permute-start | bytes 2801672 | tf_op jit(solution)/shard_map/ppermute | solution.py:403
  37.0 40.5 %collective-permute-start.8 = (bf16[64,7296]{1,0:T(8,128)(2,1)}, bf16[64,7296]{1,0:T(8,128)(2,1)}, u32[]{:S(2)}, u32[]{:S(2)}) collective-permute-start(bf16[64,7296]{1,0:T(8,128)(2,1)} %collective-permute-done.4.refs_2_), channel_id=1, source_target_pairs={{2,0},{4,2},{3,1},{5,3},{10,8},{12,10},{11,9},{13,11},{18,16},{20,... | collective-permute-start | bytes 2801672 | tf_op jit(solution)/shard_map/ppermute | solution.py:406
  38.9 15.0 %collective-permute-start.5 = (f32[128,128]{1,0:T(8,128)S(1)}, f32[128,128]{1,0:T(8,128)S(1)}, u32[]{:S(2)}, u32[]{:S(2)}) collective-permute-start(f32[128,128]{1,0:T(8,128)S(1)} %get-tuple-element.56.refs_1_), channel_id=1, source_target_pairs={{0,6},{6,0},{1,7},{7,1},{8,14},{14,8},{9,15},{15,9},{16,22},{22,16... | collective-permute-start | bytes 196616 | tf_op jit(solution)/shard_map/ppermute | solution.py:400
  41.0 4.7 %copy-start = (bf16[3584,1792]{1,0:T(8,128)(2,1)S(1)}, bf16[3584,1792]{1,0:T(8,128)(2,1)}, u32[]{:S(2)}) copy-start(bf16[3584,1792]{1,0:T(8,128)(2,1)} %refs_4_.5) | copy-start | bytes 38535172
  45.7 4.7 %copy-start.1 = (bf16[3584,1792]{1,0:T(8,128)(2,1)S(1)}, bf16[3584,1792]{1,0:T(8,128)(2,1)}, u32[]{:S(2)}) copy-start(bf16[3584,1792]{1,0:T(8,128)(2,1)} %refs_5_.7) | copy-start | bytes 38535172
  50.3 12.0 %copy-start.7 = (f32[1792]{0:T(1024)S(1)}, f32[1792]{0:T(1024)}, u32[]{:S(2)}) copy-start(f32[1792]{0:T(1024)} %param.16) | copy-start | bytes 21508
  50.3 28.7 %slice-start = ((s8[12845056]{0:T(1024)(128)(4,1)}), s8[4194304]{0:T(1024)(128)(4,1)S(1)}, s32[]{:S(2)}) async-start(s8[12845056]{0:T(1024)(128)(4,1)} %bitcast.2), calls=%async_computation | async-start | bytes 8388608
  50.3 28.7 %slice-start.1 = ((s8[12845056]{0:T(1024)(128)(4,1)}), s8[4194304]{0:T(1024)(128)(4,1)S(1)}, s32[]{:S(2)}) async-start(s8[12845056]{0:T(1024)(128)(4,1)} %bitcast.2), calls=%async_computation.1 | async-start | bytes 8388608
  50.3 28.7 %slice-start.2 = ((s8[12845056]{0:T(1024)(128)(4,1)}), s8[4194304]{0:T(1024)(128)(4,1)S(1)}, s32[]{:S(2)}) async-start(s8[12845056]{0:T(1024)(128)(4,1)} %bitcast.2), calls=%async_computation.2 | async-start | bytes 8388608
  50.3 28.7 %slice-start.4 = ((s8[12845056]{0:T(1024)(128)(4,1)}), s8[4194304]{0:T(1024)(128)(4,1)S(1)}, s32[]{:S(2)}) async-start(s8[12845056]{0:T(1024)(128)(4,1)} %bitcast.4), calls=%async_computation.4 | async-start | bytes 8388608
  50.4 28.7 %slice-start.5 = ((s8[12845056]{0:T(1024)(128)(4,1)}), s8[4194304]{0:T(1024)(128)(4,1)S(1)}, s32[]{:S(2)}) async-start(s8[12845056]{0:T(1024)(128)(4,1)} %bitcast.4), calls=%async_computation.5 | async-start | bytes 8388608
  50.4 28.7 %slice-start.6 = ((s8[12845056]{0:T(1024)(128)(4,1)}), s8[4194304]{0:T(1024)(128)(4,1)S(1)}, s32[]{:S(2)}) async-start(s8[12845056]{0:T(1024)(128)(4,1)} %bitcast.4), calls=%async_computation.6 | async-start | bytes 8388608
  54.0 37.1 %collective-permute-start.9 = (bf16[64,7296]{1,0:T(8,128)(2,1)}, bf16[64,7296]{1,0:T(8,128)(2,1)S(1)}, u32[]{:S(2)}, u32[]{:S(2)}) collective-permute-start(bf16[64,7296]{1,0:T(8,128)(2,1)} %collective-permute-done.1.refs_1_), channel_id=1, source_target_pairs={{2,4},{4,6},{3,5},{5,7},{10,12},{12,14},{11,13},{13,15},{18,20},{2... | collective-permute-start | bytes 2801672 | tf_op jit(solution)/shard_map/ppermute | solution.py:403
  59.1 33.3 %collective-permute-start.10 = (bf16[64,7296]{1,0:T(8,128)(2,1)}, bf16[64,7296]{1,0:T(8,128)(2,1)S(1)}, u32[]{:S(2)}, u32[]{:S(2)}) collective-permute-start(bf16[64,7296]{1,0:T(8,128)(2,1)} %collective-permute-done.2.refs_3_), channel_id=1, source_target_pairs={{2,0},{4,2},{3,1},{5,3},{10,8},{12,10},{11,9},{13,11},{18,16},{20,... | collective-permute-start | bytes 2801672 | tf_op jit(solution)/shard_map/ppermute | solution.py:406
  61.1 10.7 %collective-permute-start.6 = (bf16[128,1792]{1,0:T(8,128)(2,1)S(1)}, bf16[128,1792]{1,0:T(8,128)(2,1)S(1)}, u32[]{:S(2)}, u32[]{:S(2)}) collective-permute-start(bf16[128,1792]{1,0:T(8,128)(2,1)S(1)} %project.5.own_ref), channel_id=1, source_target_pairs={{1,0},{3,2},{4,5},{6,7},{9,8},{11,10},{12,13},{14,15},{17,16},{19,... | collective-permute-start | bytes 1376264 | tf_op jit(solution)/shard_map/ppermute | solution.py:375
  71.7 3.1 %copy-start.2 = (bf16[1792,2112]{0,1:T(8,128)(2,1)S(1)}, bf16[1792,2112]{0,1:T(8,128)(2,1)}, u32[]{:S(2)}) copy-start(bf16[1792,2112]{0,1:T(8,128)(2,1)} %param.17) | copy-start | bytes 22708228
  74.9 4.2 %slice-start.3 = ((s8[12845056]{0:T(1024)(128)(4,1)}), s8[262144]{0:T(1024)(128)(4,1)S(1)}, s32[]{:S(2)}) async-start(s8[12845056]{0:T(1024)(128)(4,1)} %bitcast.2), calls=%async_computation.3 | async-start | bytes 524288
  74.9 4.2 %slice-start.7 = ((s8[12845056]{0:T(1024)(128)(4,1)}), s8[262144]{0:T(1024)(128)(4,1)S(1)}, s32[]{:S(2)}) async-start(s8[12845056]{0:T(1024)(128)(4,1)} %bitcast.4), calls=%async_computation.7 | async-start | bytes 524288
  87.8 10.4 %collective-permute-start.11 = (bf16[128,1792]{1,0:T(8,128)(2,1)S(1)}, bf16[128,1792]{1,0:T(8,128)(2,1)S(1)}, u32[]{:S(2)}, u32[]{:S(2)}) collective-permute-start(bf16[128,1792]{1,0:T(8,128)(2,1)S(1)} %get-tuple-element.70), channel_id=1, source_target_pairs={{1,0},{3,2},{2,3},{5,4},{4,5},{6,7},{9,8},{11,10},{10,11},{13,12},... | collective-permute-start | bytes 1376264 | tf_op jit(solution)/shard_map/ppermute | solution.py:375
  89.7 22.4 %collective-permute-start.13 = (bf16[64,7296]{1,0:T(8,128)(2,1)S(1)}, bf16[64,7296]{1,0:T(8,128)(2,1)S(1)}, u32[]{:S(2)}, u32[]{:S(2)}) collective-permute-start(bf16[64,7296]{1,0:T(8,128)(2,1)S(1)} %choose.2.refs_0_), channel_id=1, source_target_pairs={{4,6},{2,0},{5,7},{3,1},{12,14},{10,8},{13,15},{11,9},{20,22},{18,... | collective-permute-start | bytes 2801672 | tf_op jit(solution)/shard_map/ppermute | solution.py:429
  98.2 7.3 %slice-start.8 = ((s8[7569408]{0:T(1024)(128)(4,1)}), s8[4194304]{0:T(1024)(128)(4,1)S(1)}, s32[]{:S(2)}) async-start(s8[7569408]{0:T(1024)(128)(4,1)} %bitcast.7), calls=%async_computation.8 | async-start | bytes 8388608
  98.3 7.3 %slice-start.9 = ((s8[7569408]{0:T(1024)(128)(4,1)}), s8[3375104]{0:T(1024)(128)(4,1)S(1)}, s32[]{:S(2)}) async-start(s8[7569408]{0:T(1024)(128)(4,1)} %bitcast.7), calls=%async_computation.9 | async-start | bytes 6750208
  98.3 32.8 %collective-permute-start.15 = (bf16[64,7296]{1,0:T(8,128)(2,1)S(1)}, bf16[64,7296]{1,0:T(8,128)(2,1)S(1)}, u32[]{:S(2)}, u32[]{:S(2)}) collective-permute-start(bf16[64,7296]{1,0:T(8,128)(2,1)S(1)} %choose.3.refs_1_), channel_id=1, source_target_pairs={{4,6},{2,0},{5,7},{3,1},{12,14},{10,8},{13,15},{11,9},{20,22},{18,... | collective-permute-start | bytes 2801672 | tf_op jit(solution)/shard_map/ppermute | solution.py:445
  103.6 12.2 %collective-permute-start.12 = (bf16[128,1792]{1,0:T(8,128)(2,1)S(1)}, bf16[128,1792]{1,0:T(8,128)(2,1)S(1)}, u32[]{:S(2)}, u32[]{:S(2)}) collective-permute-start(bf16[128,1792]{1,0:T(8,128)(2,1)S(1)} %project.7.own_ref), channel_id=1, source_target_pairs={{0,1},{2,3},{5,4},{7,6},{8,9},{10,11},{13,12},{15,14},{16,17},{18,... | collective-permute-start | bytes 1376264 | tf_op jit(solution)/shard_map/ppermute | solution.py:375
  118.6 22.8 %collective-permute-start.17 = (bf16[128,2176]{1,0:T(8,128)(2,1)S(1)}, bf16[128,2176]{1,0:T(8,128)(2,1)S(1)}, u32[]{:S(2)}, u32[]{:S(2)}) collective-permute-start(bf16[128,2176]{1,0:T(8,128)(2,1)S(1)} %get-tuple-element.89), channel_id=1, source_target_pairs={{0,4},{7,3},{8,12},{15,11},{16,20},{23,19},{24,28},{31,27}} | collective-permute-start | bytes 1671176 | tf_op jit(solution)/shard_map/ppermute | solution.py:473
  119.3 22.9 %collective-permute-start.18 = (bf16[128,2176]{1,0:T(8,128)(2,1)S(1)}, bf16[128,2176]{1,0:T(8,128)(2,1)S(1)}, u32[]{:S(2)}, u32[]{:S(2)}) collective-permute-start(bf16[128,2176]{1,0:T(8,128)(2,1)S(1)} %get-tuple-element.89), channel_id=1, source_target_pairs={{2,4},{4,2},{3,5},{5,3},{10,12},{12,10},{11,13},{13,11},{18,20},{2... | collective-permute-start | bytes 1671176 | tf_op jit(solution)/shard_map/ppermute | solution.py:473
  125.1 2.0 %collective-permute-start.14 = (bf16[64,1792]{1,0:T(8,128)(2,1)S(1)}, bf16[64,1792]{1,0:T(8,128)(2,1)S(1)}, u32[]{:S(2)}, u32[]{:S(2)}) collective-permute-start(bf16[64,1792]{1,0:T(8,128)(2,1)S(1)} %project.8.own_ref), channel_id=1, source_target_pairs={{0,1},{7,6},{8,9},{15,14},{16,17},{23,22},{24,25},{31,30}} | collective-permute-start | bytes 688136 | tf_op jit(solution)/shard_map/ppermute | solution.py:375
  125.8 12.0 %collective-permute-start.19 = (bf16[64,2176]{1,0:T(8,128)(2,1)S(1)}, bf16[64,2176]{1,0:T(8,128)(2,1)S(1)}, u32[]{:S(2)}, u32[]{:S(2)}) collective-permute-start(bf16[64,2176]{1,0:T(8,128)(2,1)S(1)} %get-tuple-element.84.inner_ref), channel_id=1, source_target_pairs={{0,2},{6,4},{1,3},{7,5},{8,10},{14,12},{9,11},{15,13},{16,18},{22,... | collective-permute-start | bytes 835592 | tf_op jit(solution)/shard_map/ppermute | solution.py:473
  129.5 19.3 %copy-start.6 = (f32[1536]{0:T(1024)S(1)}, f32[1536]{0:T(1024)}, u32[]{:S(2)}) copy-start(f32[1536]{0:T(1024)} %param.18) | copy-start | bytes 18436
  129.5 11.8 %collective-permute-start.20 = (bf16[64,2176]{1,0:T(8,128)(2,1)S(1)}, bf16[64,2176]{1,0:T(8,128)(2,1)S(1)}, u32[]{:S(2)}, u32[]{:S(2)}) collective-permute-start(bf16[64,2176]{1,0:T(8,128)(2,1)S(1)} %get-tuple-element.85), channel_id=1, source_target_pairs={{6,2},{1,5},{14,10},{9,13},{22,18},{17,21},{30,26},{25,29}} | collective-permute-start | bytes 835592 | tf_op jit(solution)/shard_map/ppermute | solution.py:473
  134.6 22.2 %copy-start.5 = (f32[512]{0:T(512)S(1)}, f32[512]{0:T(512)}, u32[]{:S(2)}) copy-start(f32[512]{0:T(512)} %param.19) | copy-start | bytes 6148
  134.6 10.4 %collective-permute-start.16 = (bf16[64,1792]{1,0:T(8,128)(2,1)S(1)}, bf16[64,1792]{1,0:T(8,128)(2,1)S(1)}, u32[]{:S(2)}, u32[]{:S(2)}) collective-permute-start(bf16[64,1792]{1,0:T(8,128)(2,1)S(1)} %project.9.own_ref), channel_id=1, source_target_pairs={{0,1},{7,6},{8,9},{15,14},{16,17},{23,22},{24,25},{31,30}} | collective-permute-start | bytes 688136 | tf_op jit(solution)/shard_map/ppermute | solution.py:375
  142.5 8.4 %collective-permute-start.21 = (bf16[64,2176]{1,0:T(8,128)(2,1)S(1)}, bf16[64,2176]{1,0:T(8,128)(2,1)S(1)}, u32[]{:S(2)}, u32[]{:S(2)}) collective-permute-start(bf16[64,2176]{1,0:T(8,128)(2,1)S(1)} %get-tuple-element.91), channel_id=1, source_target_pairs={{2,0},{4,6},{3,1},{5,7},{10,8},{12,14},{11,9},{13,15},{18,16},{20,... | collective-permute-start | bytes 835592 | tf_op jit(solution)/shard_map/ppermute | solution.py:473
  147.5 9.3 %collective-permute-start.22 = (bf16[64,2176]{1,0:T(8,128)(2,1)S(1)}, bf16[64,2176]{1,0:T(8,128)(2,1)S(1)}, u32[]{:S(2)}, u32[]{:S(2)}) collective-permute-start(bf16[64,2176]{1,0:T(8,128)(2,1)S(1)} %get-tuple-element.92), channel_id=1, source_target_pairs={{6,2},{1,5},{14,10},{9,13},{22,18},{17,21},{30,26},{25,29}} | collective-permute-start | bytes 835592 | tf_op jit(solution)/shard_map/ppermute | solution.py:473

commit v4 on v3

--- a/solution.py
+++ b/solution.py
@@ -13,7 +13,7 @@
 LENGTH = 2048
 LANES = 128
 TERMS = 3
-VMEM_BYTES = 9 * 1024 * 1024
+VMEM_BYTES = 6 * 1024 * 1024
 
 epsilon = 1e-06
 
@@ -61,7 +61,7 @@
 NO_COST = pl.CostEstimate(flops=0, bytes_accessed=0, transcendentals=0)
 
 
-def kernel(body, name, inputs, outputs, scratch=(), cost=NO_COST):
+def kernel(body, name, inputs, outputs, scratch=()):
     return pl.pallas_call(
         body,
         in_specs=[VMEM] * len(inputs),
@@ -69,7 +69,7 @@
         out_shape=[jax.ShapeDtypeStruct(shape, kind) for shape, kind in outputs],
         scratch_shapes=list(scratch),
         compiler_params=pltpu.CompilerParams(vmem_limit_bytes=VMEM_BYTES),
-        cost_estimate=cost,
+        cost_estimate=NO_COST,
         name=name,
     )(*inputs)
 
@@ -129,88 +129,73 @@
     return kernel(body, "pack", [hidden, embed, sums, other_sums], outputs)
 
 
-def project(groups, weights, own_first=None, cost=NO_COST):
+def project(groups, weights, other_groups=None, takes_first=None, keeps_first=None, needed=None):
     hidden_gain, embed_gain, w_hidden, w_embed = weights
     depth, width = w_hidden.shape
-    packed = [isinstance(group[1], list) for group in groups]
-    inputs = []
-    for arrays, sums, _ in groups:
-        inputs += [*arrays, *(sums if isinstance(sums, list) else [sums])]
+    variants = [groups] if other_groups is None else [groups, other_groups]
     distinct = []
-    for array in inputs:
-        if all(array is not other for other in distinct):
-            distinct.append(array)
+    for variant in variants:
+        for array, sums, _ in variant:
+            for value in (array, sums):
+                if all(value is not other for other in distinct):
+                    distinct.append(value)
     place = {id(array): at for at, array in enumerate(distinct)}
-    sizes = [group[0][0].shape[0] for group in groups]
-    total = sum(sizes)
+    total = sum(group[0].shape[0] for group in groups)
     padded = max(total, LANES)
 
-    def squares_of(refs, low, size):
-        height = refs[0].shape[0]
-        parts = []
-        for start in range(low, low + size, height):
-            spare = sum(ref[:, 2 * depth :].astype(jnp.float32) for ref in refs)
-            at = start // height * 2 * TERMS
-            parts.append(
-                [
-                    sum(spare[:, first + t : first + t + 1] for t in range(TERMS))
-                    for first in (at, at + TERMS)
-                ]
-            )
-        return [jnp.concatenate(column, axis=0) for column in zip(*parts, strict=True)]
+    def squares_of(ref, low, size):
+        if ref.dtype == jnp.float32:
+            return [ref[low : low + size, column : column + 1] for column in range(2)]
+        spare = ref[:, 2 * depth :].astype(jnp.float32)
+        at = low // size * 2 * TERMS
+        return [
+            sum(spare[:, first + t : first + t + 1] for t in range(TERMS)) for first in (at, at + TERMS)
+        ]
 
     def body(*refs):
         sources = refs[: len(distinct)]
         hgain_ref, egain_ref, wh_ref, we_ref, *outs, normed = refs[len(distinct) :]
-        at = 0
-        for (arrays, sums, low), size, is_packed in zip(groups, sizes, packed, strict=True):
-            arrays = [sources[place[id(array)]] for array in arrays]
-            if is_packed:
-                squares = squares_of([sources[place[id(array)]] for array in sums], low, size)
+
+        def norm(variant):
+            at = 0
+            for array, sums, low in variant:
+                size = array.shape[0]
+                squares = squares_of(sources[place[id(sums)]], low, size)
+                for column, gain_ref in enumerate((hgain_ref, egain_ref)):
+                    part = pl.ds(column * depth, depth)
+                    value = sources[place[id(array)]][:, part].astype(jnp.float32)
+                    normed[at : at + size, part] = (
+                        value * inverse_rms(squares[column], D) * gain_ref[...]
+                    ).astype(jnp.bfloat16)
+                at += size
+
+        def run():
+            if other_groups is None:
+                norm(groups)
             else:
-                known = sources[place[id(sums)]]
-                squares = [known[low : low + size, column : column + 1] for column in range(2)]
-            for column, gain_ref in enumerate((hgain_ref, egain_ref)):
-                part = pl.ds(column * depth, depth)
-                value = arrays[0][:, part].astype(jnp.float32)
-                for other in arrays[1:]:
-                    value = value + other[:, part].astype(jnp.float32)
-                normed[at : at + size, part] = (
-                    value * inverse_rms(squares[column], D) * gain_ref[...]
-                ).astype(jnp.bfloat16)
-            at += size
-        result = (
-            jnp.dot(normed[:, :depth], wh_ref[...], preferred_element_type=jnp.float32)
-            + jnp.dot(normed[:, depth:], we_ref[...], preferred_element_type=jnp.float32)
-        ).astype(jnp.bfloat16)
-        if own_first is not None:
-            first = result[: total // 2, :]
-            second = result[total // 2 : total, :]
-            keep = own_first()
-            outs[0][...] = jnp.where(keep, first, second)
-            outs[1][...] = jnp.where(keep, second, first)
-        else:
-            outs[0][...] = result[:total, :]
-
-    outputs = [((total, width), jnp.bfloat16)]
-    if own_first is not None:
-        outputs = [((total // 2, width), jnp.bfloat16)] * 2
+                pl.when(takes_first())(lambda: norm(groups))
+                pl.when(jnp.logical_not(takes_first()))(lambda: norm(other_groups))
+            result = jnp.dot(normed[:, :depth], wh_ref[...], preferred_element_type=jnp.float32)
+            result = result + jnp.dot(normed[:, depth:], we_ref[...], preferred_element_type=jnp.float32)
+            result = result[:total, :].astype(jnp.bfloat16)
+            if keeps_first is None:
+                outs[0][...] = result
+            else:
+                parts = (result[: total // 2, :], result[total // 2 :, :])
+                outs[0][...] = jnp.where(keeps_first(), parts[0], parts[1])
+                outs[1][...] = jnp.where(keeps_first(), parts[1], parts[0])
+
+        run() if needed is None else pl.when(needed())(run)
+
+    sizes = [total] if keeps_first is None else [total // 2] * 2
     result = kernel(
         body,
         "project",
         [*distinct, hidden_gain, embed_gain, resident(w_hidden), resident(w_embed)],
-        outputs,
+        [((size, width), jnp.bfloat16) for size in sizes],
         [pltpu.VMEM((padded, 2 * depth), jnp.bfloat16)],
-        cost,
-    )
-    return result if own_first is not None else result[0]
-
-
-def warm(arrays, weights):
-    def body(*refs):
-        refs[-1][...] = refs[0][:8, :LANES]
-
-    return kernel(body, "warm", [*arrays, *[resident(w) for w in weights]], [((8, LANES), arrays[0].dtype)])[0]
+    )
+    return result[0] if keeps_first is None else result
 
 
 def choose(first, second, takes_first):
@@ -226,13 +211,13 @@
     return kernel(body, "choose", [first, second], [(first.shape, first.dtype)])[0]
 
 
-def latent_partial(own, received, gain, w_latent, cuts, known=(), route=()):
+def latent_partial(own, received, gain, w_latent, cuts, known=(), route=(), needed=None):
     rows, width = own.shape
     lat = w_latent.shape[0]
     padded = -(-(lat + 2) // LANES) * LANES
     edge = padded - LANES
 
-    def body(own_ref, received_ref, gain_ref, w_ref, *refs):
+    def run(own_ref, received_ref, gain_ref, w_ref, *refs):
         known_refs, mtp_ref, lat_refs = refs[: len(known)], refs[len(known)], refs[len(known) + 1 :]
         mtp = (own_ref[...].astype(jnp.float32) + received_ref[...].astype(jnp.float32)).astype(
             jnp.bfloat16
@@ -269,6 +254,9 @@
                         lambda ref=ref, block=block, part=part: put(ref, block * height, part)
                     )
 
+    def body(*refs):
+        run(*refs) if needed is None else pl.when(needed())(lambda: run(*refs))
+
     sizes = [high - low for low, high in cuts]
     height = sizes[0]
     if route:
@@ -288,13 +276,14 @@
             inner_sum = inner_sum + ref[:rows, :].astype(jnp.float32)
             outer_sum = outer_sum + ref[rows:, :].astype(jnp.float32)
         base_ref[...] = jnp.where(is_end(), outer_sum, inner_sum)
-        owed_ref[...] = outer_sum.astype(jnp.bfloat16)
+        owed_ref[:, :width] = outer_sum.astype(jnp.bfloat16)
+        owed_ref[:, width:] = jnp.zeros((rows, LANES), jnp.bfloat16)
 
     return kernel(
         body,
         "add_parts",
         [inner, outer, *pairs, single, far],
-        [((rows, width), jnp.float32), ((rows, width), jnp.bfloat16)],
+        [((rows, width), jnp.float32), ((rows, width + LANES), jnp.bfloat16)],
     )
 
 
@@ -302,18 +291,27 @@
     height = shape[0] // 4
 
     def body(*refs):
-        out = refs[-1]
+        *refs, out = refs
         swapped = swaps()
-        for (shard, first, when, array), ref in zip(choices, refs, strict=False):
+        for shard, first, when, array in choices:
+            terms = [refs.pop(0) for _ in (array if isinstance(array, tuple) else (array,))]
+            array = array[0] if isinstance(array, tuple) else array
 
             @pl.when(when())
-            def _(shard=shard, first=first, array=array, ref=ref):
-                for at in range(array.shape[0] // height):
-                    half = first + at
-                    row = (2 * shard + half + (1 - 2 * half) * swapped) * height
-                    out[pl.ds(pl.multiple_of(row, height), height), :] = ref[at * height : (at + 1) * height, :]
-
-    return kernel(body, "place_rows", [choice[-1] for choice in choices], [(shape, jnp.bfloat16)])[0]
+            def _(shard=shard, first=first, array=array, terms=terms):
+                size = min(array.shape[0], height)
+                for at in range(array.shape[0] // size):
+                    half, within = (first + at, 0) if isinstance(first, int) else (1, first())
+                    row = (2 * shard + half + (1 - 2 * half) * swapped) * height + within
+                    value = terms[0][at * size : (at + 1) * size, :]
+                    if len(terms) > 1:
+                        value = value.astype(jnp.float32) + terms[1][...].astype(jnp.float32)
+                    out[pl.ds(pl.multiple_of(row, size), size), :] = value.astype(jnp.bfloat16)
+
+    inputs = []
+    for choice in choices:
+        inputs += choice[-1] if isinstance(choice[-1], tuple) else [choice[-1]]
+    return kernel(body, "place_rows", inputs, [(shape, jnp.bfloat16)])[0]
 
 
 def finish(base, late, q_gain, kv_gain, cosine, sine_grid, first_row):
@@ -326,7 +324,8 @@
         qg_ref, kg_ref, cos_ref, sin_ref, q_ref, kv_ref, rope_ref, total = refs[len(late) :]
         total[...] = base_ref[...]
         for (at, array), ref in zip(late, late_refs, strict=True):
-            total[at : at + array.shape[0], :] += ref[...].astype(jnp.float32)
+            size = array.shape[0]
+            total[pl.ds(pl.multiple_of(at(), size), size), :] += ref[:, : total.shape[1]].astype(jnp.float32)
         whole = total[...]
         squares = whole[:, lat + rope : lat + rope + 1] + whole[:, lat + rope + 1 : lat + rope + 2]
         latent = whole * inverse_rms(squares, D)
@@ -396,7 +395,6 @@
     other_sums = lax.ppermute(sums, "mp", [(0, 1), (1, 0)])
     second_piece, sums = pack(hidden_in, embed_in, sums, other_sums, upper)
     pieces = [first_piece, second_piece]
-    token = warm([sums, hidden_gain, embed_gain, attn_gain, q_gain, kv_gain, cosine, sine_grid], [w_hidden, w_embed])
     sums_three = lax.ppermute(sums, "dp", [(0, last), (last, 0)])
 
     def go_ahead(x, k):
@@ -407,49 +405,54 @@
 
     ahead_one = [go_ahead(x, 1) for x in pieces]
     back_one = [go_back(x, 1) for x in pieces]
-    ahead_one[0], back_one[0], token = lax.optimization_barrier((ahead_one[0], back_one[0], token))
     ahead_two = [go_ahead(ahead_one[0], 2)]
     back_two = [go_back(back_one[0], 2)]
-    sums = after(sums, token, ahead_one[0], back_one[0])
-    groups = [([piece], sums, low) for piece, (low, _) in zip(pieces, halves, strict=True)]
+    ahead_one[0], back_one[0], sums = lax.optimization_barrier((ahead_one[0], back_one[0], sums))
+    groups = [(piece, sums, low) for piece, (low, _) in zip(pieces, halves, strict=True)]
     got_own = project(groups, weights)
     ahead_one[1], back_one[1], got_own, sums_three = lax.optimization_barrier(
         (ahead_one[1], back_one[1], got_own, sums_three)
     )
     ahead_two.append(go_ahead(ahead_one[1], 2))
     back_two.append(go_back(back_one[1], 2))
-    mtp_own, lat_own = latent_partial(got_own, to_owner(got_own, senders_of(0)), attn_gain, w_latent, halves)
+    received_own = to_owner(got_own, senders_of(0))
+    mtp_own, lat_own = latent_partial(got_own, received_own, attn_gain, w_latent, halves)
 
     def from_ahead():
         return me() >= line // 2
-
-    ahead_two[0], back_two[0], lat_own = lax.optimization_barrier((ahead_two[0], back_two[0], lat_own))
-    two = [choose(ahead_two[0], back_two[0], from_ahead)]
-    ends_on = [(line - 2, last), (1, 0)]
-    three = [lax.ppermute(two[0], "dp", ends_on)]
 
     def ahead_is_own():
         near = jnp.where(me() >= 1, me() - 1, me() + 1)
         owned = jnp.where(near >= line // 2, 1, 0) == mine()
         return jnp.where(me() >= 1, owned, jnp.logical_not(owned))
 
-    one = lax.optimization_barrier((ahead_one, back_one, two[0]))
-    groups = [([x], [one[0][-1]], low) for x, (low, _) in zip(one[0], halves, strict=True)]
-    groups += [([x], [one[1][-1]], low) for x, (low, _) in zip(one[1], halves, strict=True)]
-    got_one, other_one = project(groups, weights, own_first=ahead_is_own)
-    received_one = to_owner(other_one, senders_of(1))
-    ahead_two[1], back_two[1], received_one = lax.optimization_barrier(
-        (ahead_two[1], back_two[1], received_one)
+    def ahead_is_other():
+        return jnp.logical_not(ahead_is_own())
+
+    groups_ahead = [(x, ahead_one[1], low) for x, (low, _) in zip(ahead_one, halves, strict=True)]
+    groups_back = [(x, back_one[1], low) for x, (low, _) in zip(back_one, halves, strict=True)]
+    received_one = to_owner(project(groups_ahead, weights, groups_back, ahead_is_other), senders_of(1))
+    got_one = project(groups_ahead, weights, groups_back, ahead_is_own)
+    ahead_two[0], back_two[0], received_one = lax.optimization_barrier(
+        (ahead_two[0], back_two[0], received_one)
+    )
+    two = [choose(ahead_two[0], back_two[0], from_ahead)]
+    ends_on = [(line - 2, last), (1, 0)]
+    three = [lax.ppermute(two[0], "dp", ends_on)]
+    mtp_one, lat_one = latent_partial(got_one, received_one, attn_gain, w_latent, halves)
+    ahead_two[1], back_two[1], lat_one, lat_own = lax.optimization_barrier(
+        (ahead_two[1], back_two[1], lat_one, lat_own)
     )
     two.append(choose(ahead_two[1], back_two[1], from_ahead))
     three.append(lax.ppermute(two[1], "dp", ends_on))
-    mtp_one, lat_one = latent_partial(got_one, received_one, attn_gain, w_latent, halves)
-
-    got_two = project([([x], [two[-1]], low) for x, (low, _) in zip(two, halves, strict=True)], weights)
+
+    def is_end():
+        return jnp.logical_or(me() == 0, me() == last)
+
+    got_two = project([(x, two[1], low) for x, (low, _) in zip(two, halves, strict=True)], weights)
     received_two = to_owner(got_two, senders_of(2))
     sums_three = after(sums_three, got_two)
-    got_three = [project([([three[0]], sums_three, 0)], weights)]
-    received_two = after(received_two, got_three[0])
+    got_three = [project([(three[0], sums_three, 0)], weights, needed=is_end)]
 
     def part_for(half, place):
         return 2 * jnp.abs(me() - (2 * mine() + half)) + jnp.where(mine() == 1, 1 - place, place)
@@ -482,23 +485,30 @@
     to_middle = [(0, last, 1), (1, 0, 2)]
     whole = ((0, rows_out),)
     mtp, (lat,) = latent_partial(
-        got_three[0], to_owner(got_three[0], senders_of(3)), attn_gain, w_latent, whole
+        got_three[0], to_owner(got_three[0], senders_of(3)), attn_gain, w_latent, whole, needed=is_end
     )
     mtp_three = [mtp]
     far = send(lat, to_middle)
     sums_three = after(sums_three, got_three[0], inner, lat)
-    got_three.append(project([([three[1]], sums_three, rows_out)], weights))
-    mtp, (lat,) = latent_partial(
-        got_three[1], to_owner(got_three[1], senders_of(3)), attn_gain, w_latent, whole
-    )
-    mtp_three.append(mtp)
-
-    def is_end():
-        return jnp.logical_or(me() == 0, me() == last)
+    part = rows_out // 2
+    kept, given = project([(three[1], sums_three, rows_out)], weights, keeps_first=lambda: mine() == 0, needed=is_end)
+    ends = (0, last)
+    received = lax.ppermute(
+        given, ("dp", "mp"), [(device(d, m), device(d, 1 - m)) for d in ends for m in range(2)]
+    )
+    mtp, (lat,) = latent_partial(kept, received, attn_gain, w_latent, ((0, part),), needed=is_end)
+    mtp_three += [mtp, (given, to_owner(kept, [(last, 0), (0, 1)]))]
+    late = [
+        (lambda: part * mine(), send(lat, to_middle)),
+        (
+            lambda: part * (1 - mine()),
+            lax.ppermute(lat, ("dp", "mp"), [(device(last, 1), device(1, 0)), (device(0, 0), device(2, 1))]),
+        ),
+    ]
 
     base, owed = add_parts(inner, outer, crossing, single, far, is_end)
     owed = send(owed, [(m, d, to) for m in both for d, to in ((1, 0), (2, last))])
-    late = [(0, owed), (0, send(lat, to_middle))]
+    late = [(lambda: 0, owed), *late]
 
     def distance(offset):
         return jnp.abs(me() - (2 * mine() + offset))
@@ -507,7 +517,7 @@
     for offset in range(2):
         for k, mtp in enumerate((mtp_own, mtp_one, mtp_two)):
             choices.append((offset, 0, lambda offset=offset, k=k: distance(offset) == k, mtp))
-        for half, mtp in enumerate(mtp_three):
+        for half, mtp in zip((0, lambda: part * mine(), lambda: part * (1 - mine())), mtp_three, strict=True):
             choices.append((offset, half, lambda offset=offset: distance(offset) == last, mtp))
     mtp_hidden = place_rows(choices, (2 * shard, w_hidden.shape[1]), mine)
 

time: 159 us -> 155 us (0.975)
  Pallas kernels: 40.3 us -> 28.4 us
  waiting for transfers between devices: 48 us -> 57.4 us
  local copies, waits for them, and re-layouts: 16.3 us -> 13.2 us
  starting transfers between devices: 51 us -> 53 us
    pallas_call x17 -> x18, Pallas kernels: 40.3 us -> 28.4 us  [kernel(): pl.pallas_call(body, in_specs=[VMEM] * len(inputs), out_specs=[VMEM] * le...]
    ppermute x1, waiting for transfers between devices: 0.01 us -> 9.8 us  [shards_line(): three.append(lax.ppermute(two[1], 'dp', ends_on))]
    ppermute x1, waiting for transfers between devices: 4.06 us -> 0.01 us  [shards_line(): three = [lax.ppermute(two[0], 'dp', ends_on)]]
    ppermute x4, starting transfers between devices: 16.5 us -> 13 us  [go_ahead(): return lax.ppermute(x, 'dp', [(i, i + 1) for i in range(k - 1, last)])]
    unnamed x36 -> x22, local copies, waits for them, and re-layouts: 14.9 us -> 11.7 us
    ppermute x5, starting transfers between devices: 6.45 us -> 9.51 us  [to_owner(): return lax.ppermute(value, ('dp', 'mp'), pairs)]
    ppermute x5, waiting for transfers between devices: 15.1 us -> 17.7 us  [to_owner(): return lax.ppermute(value, ('dp', 'mp'), pairs)]
    ppermute x1, starting transfers between devices: 1.67 us -> 3.93 us  [shards_line(): three.append(lax.ppermute(two[1], 'dp', ends_on))]
  transfers between devices with their start and end apart: 23 -> 25, of which waited for: 11 -> 13; matrix products, arithmetic and copies ran while one was open for 2% -> 2% of each run, Pallas kernels for 25% -> 17%
where the time goes in v4:
time: 155 us; the launch traced here: 154 us
  waiting for transfers between devices  57.4 us (37%)
  starting transfers between devices  53 us (34%)
  Pallas kernels  28.4 us (18%)
  local copies, waits for them, and re-layouts  13.2 us (9%)
    pallas_call x18, Pallas kernels, kernel(): pl.pallas_call(body, in_specs=[VMEM] * len(inputs), out_specs=[VMEM] * le...  28.4 us
    ppermute x5, waiting for transfers between devices, to_owner(): return lax.ppermute(value, ('dp', 'mp'), pairs)  17.7 us
    ppermute x4, starting transfers between devices, go_ahead(): return lax.ppermute(x, 'dp', [(i, i + 1) for i in range(k - 1, last)])  13 us
    unnamed x22, local copies, waits for them, and re-layouts  11.7 us
    ppermute x6, starting transfers between devices, send(): return lax.ppermute(value, ('dp', 'mp'), pairs)  11.3 us
    ppermute x6, waiting for transfers between devices, send(): return lax.ppermute(value, ('dp', 'mp'), pairs)  11.2 us
    ppermute x1, waiting for transfers between devices, shards_line(): three.append(lax.ppermute(two[1], 'dp', ends_on))  9.8 us
    ppermute x5, starting transfers between devices, to_owner(): return lax.ppermute(value, ('dp', 'mp'), pairs)  9.51 us
  transfers between devices with their start and end apart: 25, of which 13 were waited for; matrix products, arithmetic and copies ran while one was open for 2% of the time, Pallas kernels for 17%

profile of v4, /device:TPU:8, one launch (start us, length us, event | category | flops | bytes accessed | tf_op | source)
XLA Modules:
  0.0 154.1 jit_solution(11840017042179358660)
XLA Ops:
  0.6 1.2 copy-done.4
  1.8 1.2 copy-done.5
  3.5 3.5 %collective-permute-start.3 = (bf16[64,7296]{1,0:T(8,128)(2,1)S(1)}, bf16[64,7296]{1,0:T(8,128)(2,1)S(1)}, u32[]{:S(2)}, u32[]{:S(2)}) collective-permute-start(bf16[64,7296]{1,0:T(8,128)(2,1)S(1)} %get-tuple-element.49.refs_0_), channel_id=1, source_target_pairs={{0,2},{2,4},{4,6},{1,3},{3,5},{5,7},{8,10},{10,12},{12,14},{9,11},... | collective-permute-start | bytes 2801672 | tf_op jit(solution)/shard_map/ppermute | solution.py:401
  6.9 2.4 %collective-permute-start.4 = (bf16[64,7296]{1,0:T(8,128)(2,1)S(1)}, bf16[64,7296]{1,0:T(8,128)(2,1)S(1)}, u32[]{:S(2)}, u32[]{:S(2)}) collective-permute-start(bf16[64,7296]{1,0:T(8,128)(2,1)S(1)} %get-tuple-element.49.refs_0_), channel_id=1, source_target_pairs={{2,0},{4,2},{6,4},{3,1},{5,3},{7,5},{10,8},{12,10},{14,12},{11,9},... | collective-permute-start | bytes 2801672 | tf_op jit(solution)/shard_map/ppermute | solution.py:404
  9.4 1.6 %collective-permute-start = (f32[128,128]{1,0:T(8,128)S(1)}, f32[128,128]{1,0:T(8,128)S(1)}, u32[]{:S(2)}, u32[]{:S(2)}) collective-permute-start(f32[128,128]{1,0:T(8,128)S(1)} %get-tuple-element.47.sums_ref), channel_id=1, source_target_pairs={{0,1},{1,0},{2,3},{3,2},{4,5},{5,4},{6,7},{7,6},{8,9},{9,8},{10,11... | collective-permute-start | bytes 196616 | tf_op jit(solution)/shard_map/ppermute | solution.py:395
  10.9 2.7 %collective-permute-done.other_ref = f32[128,128]{1,0:T(8,128)S(1)} collective-permute-done((f32[128,128]{1,0:T(8,128)S(1)}, f32[128,128]{1,0:T(8,128)S(1)}, u32[]{:S(2)}, u32[]{:S(2)}) %collective-permute-start) | collective-permute-done | bytes 65568 | tf_op jit(solution)/shard_map/ppermute | solution.py:395
  13.8 3.4 %collective-permute-start.1 = (bf16[64,7296]{1,0:T(8,128)(2,1)S(1)}, bf16[64,7296]{1,0:T(8,128)(2,1)S(1)}, u32[]{:S(2)}, u32[]{:S(2)}) collective-permute-start(bf16[64,7296]{1,0:T(8,128)(2,1)S(1)} %get-tuple-element.48.refs_2_), channel_id=1, source_target_pairs={{0,2},{2,4},{4,6},{1,3},{3,5},{5,7},{8,10},{10,12},{12,14},{9,11},... | collective-permute-start | bytes 2801672 | tf_op jit(solution)/shard_map/ppermute | solution.py:401
  17.3 2.5 %collective-permute-start.2 = (bf16[64,7296]{1,0:T(8,128)(2,1)S(1)}, bf16[64,7296]{1,0:T(8,128)(2,1)S(1)}, u32[]{:S(2)}, u32[]{:S(2)}) collective-permute-start(bf16[64,7296]{1,0:T(8,128)(2,1)S(1)} %get-tuple-element.48.refs_2_), channel_id=1, source_target_pairs={{2,0},{4,2},{6,4},{3,1},{5,3},{7,5},{10,8},{12,10},{14,12},{11,9},... | collective-permute-start | bytes 2801672 | tf_op jit(solution)/shard_map/ppermute | solution.py:404
  19.7 9.2 %collective-permute-done.3.refs_0_ = bf16[64,7296]{1,0:T(8,128)(2,1)S(1)} collective-permute-done((bf16[64,7296]{1,0:T(8,128)(2,1)S(1)}, bf16[64,7296]{1,0:T(8,128)(2,1)S(1)}, u32[]{:S(2)}, u32[]{:S(2)}) %collective-permute-start.3) | collective-permute-done | bytes 933920 | tf_op jit(solution)/shard_map/ppermute | solution.py:401
  28.9 4.4 %collective-permute-start.7 = (bf16[64,7296]{1,0:T(8,128)(2,1)S(1)}, bf16[64,7296]{1,0:T(8,128)(2,1)}, u32[]{:S(2)}, u32[]{:S(2)}) collective-permute-start(bf16[64,7296]{1,0:T(8,128)(2,1)S(1)} %collective-permute-done.3.refs_0_), channel_id=1, source_target_pairs={{2,4},{4,6},{3,5},{5,7},{10,12},{12,14},{11,13},{13,15},{18,20},{2... | collective-permute-start | bytes 2801672 | tf_op jit(solution)/shard_map/ppermute | solution.py:401
  33.4 1.9 %collective-permute-start.8 = (bf16[64,7296]{1,0:T(8,128)(2,1)S(1)}, bf16[64,7296]{1,0:T(8,128)(2,1)}, u32[]{:S(2)}, u32[]{:S(2)}) collective-permute-start(bf16[64,7296]{1,0:T(8,128)(2,1)S(1)} %collective-permute-done.4.refs_2_), channel_id=1, source_target_pairs={{2,0},{4,2},{3,1},{5,3},{10,8},{12,10},{11,9},{13,11},{18,16},{20,... | collective-permute-start | bytes 2801672 | tf_op jit(solution)/shard_map/ppermute | solution.py:404
  37.4 4.6 %copy-done = bf16[3584,1792]{1,0:T(8,128)(2,1)S(1)} copy-done((bf16[3584,1792]{1,0:T(8,128)(2,1)S(1)}, bf16[3584,1792]{1,0:T(8,128)(2,1)}, u32[]{:S(2)}) %copy-start) | copy-done | bytes 12845080
  42.1 4.6 %copy-done.2 = bf16[3584,1792]{1,0:T(8,128)(2,1)S(1)} copy-done((bf16[3584,1792]{1,0:T(8,128)(2,1)S(1)}, bf16[3584,1792]{1,0:T(8,128)(2,1)}, u32[]{:S(2)}) %copy-start.2) | copy-done | bytes 12845080
  46.7 3.5 %project.6.refs_0_ = bf16[128,1792]{1,0:T(8,128)(2,1)S(1)} custom-call(bf16[64,7296]{1,0:T(8,128)(2,1)S(1)} %get-tuple-element.49.refs_0_, f32[128,128]{1,0:T(8,128)S(1)} %get-tuple-element.51.refs_1_, bf16[64,7296]{1,0:T(8,128)(2,1)S(1)} %get-tuple-element.48.refs_2_, f32[1,3584]{1,0:T(1,128)S(1)} %broadcast_in_dim.17.refs_3_.refs_4_.refs_2_, ...), custom_call_target="tpu_custom_call" | custom-call | tf_op jit(solution)/shard_map/project/pallas_call | solution.py:65
  50.3 3.6 %collective-permute-done.2.refs_3_ = bf16[64,7296]{1,0:T(8,128)(2,1)S(1)} collective-permute-done((bf16[64,7296]{1,0:T(8,128)(2,1)S(1)}, bf16[64,7296]{1,0:T(8,128)(2,1)S(1)}, u32[]{:S(2)}, u32[]{:S(2)}) %collective-permute-start.2) | collective-permute-done | bytes 933920 | tf_op jit(solution)/shard_map/ppermute | solution.py:404
  53.9 1.6 %collective-permute-start.10 = (bf16[64,7296]{1,0:T(8,128)(2,1)S(1)}, bf16[64,7296]{1,0:T(8,128)(2,1)S(1)}, u32[]{:S(2)}, u32[]{:S(2)}) collective-permute-start(bf16[64,7296]{1,0:T(8,128)(2,1)S(1)} %collective-permute-done.1.refs_1_), channel_id=1, source_target_pairs={{2,4},{4,6},{3,5},{5,7},{10,12},{12,14},{11,13},{13,15},{18,20},{2... | collective-permute-start | bytes 2801672 | tf_op jit(solution)/shard_map/ppermute | solution.py:401
  55.5 2.4 %collective-permute-start.11 = (bf16[64,7296]{1,0:T(8,128)(2,1)S(1)}, bf16[64,7296]{1,0:T(8,128)(2,1)S(1)}, u32[]{:S(2)}, u32[]{:S(2)}) collective-permute-start(bf16[64,7296]{1,0:T(8,128)(2,1)S(1)} %collective-permute-done.2.refs_3_), channel_id=1, source_target_pairs={{2,0},{4,2},{3,1},{5,3},{10,8},{12,10},{11,9},{13,11},{18,16},{20,... | collective-permute-start | bytes 2801672 | tf_op jit(solution)/shard_map/ppermute | solution.py:404
  58.0 4.1 %project.8 = bf16[128,1792]{1,0:T(8,128)(2,1)S(1)} custom-call(bf16[64,7296]{1,0:T(8,128)(2,1)S(1)} %collective-permute-done.3.refs_0_, bf16[64,7296]{1,0:T(8,128)(2,1)S(1)} %collective-permute-done.1.refs_1_, bf16[64,7296]{1,0:T(8,128)(2,1)S(1)} %collective-permute-done.4.refs_2_, bf16[64,7296]{1,0:T(8,128)(2,1)S(1)} %collective-permute-done.2.refs_3_, ...), custom_call_target="tpu_custom_call" | custom-call | tf_op jit(solution)/shard_map/project/pallas_call | solution.py:65
  62.0 3.4 %collective-permute-start.9 = (bf16[128,1792]{1,0:T(8,128)(2,1)S(1)}, bf16[128,1792]{1,0:T(8,128)(2,1)S(1)}, u32[]{:S(2)}, u32[]{:S(2)}) collective-permute-start(bf16[128,1792]{1,0:T(8,128)(2,1)S(1)} %project.8), channel_id=1, source_target_pairs={{1,0},{3,2},{2,3},{5,4},{4,5},{6,7},{9,8},{11,10},{10,11},{13,12},... | collective-permute-start | bytes 1376264 | tf_op jit(solution)/shard_map/ppermute | solution.py:374
  65.5 8.7 %collective-permute-done.9.refs_1_ = bf16[128,1792]{1,0:T(8,128)(2,1)S(1)} collective-permute-done((bf16[128,1792]{1,0:T(8,128)(2,1)S(1)}, bf16[128,1792]{1,0:T(8,128)(2,1)S(1)}, u32[]{:S(2)}, u32[]{:S(2)}) %collective-permute-start.9) | collective-permute-done | bytes 458784 | tf_op jit(solution)/shard_map/ppermute | solution.py:374
  74.1 1.3 collective-permute-start.6
  75.5 1.7 %choose.2.refs_0_ = bf16[64,7296]{1,0:T(8,128)(2,1)S(1)} custom-call(bf16[64,7296]{1,0:T(8,128)(2,1)} %collective-permute-done.7.first_ref, bf16[64,7296]{1,0:T(8,128)(2,1)} %collective-permute-done.8.second_ref), custom_call_target="tpu_custom_call" | custom-call | tf_op jit(solution)/shard_map/choose/pallas_call | solution.py:65
  77.1 1.8 %collective-permute-start.13 = (bf16[64,7296]{1,0:T(8,128)(2,1)S(1)}, bf16[64,7296]{1,0:T(8,128)(2,1)S(1)}, u32[]{:S(2)}, u32[]{:S(2)}) collective-permute-start(bf16[64,7296]{1,0:T(8,128)(2,1)S(1)} %choose.2.refs_0_), channel_id=1, source_target_pairs={{4,6},{2,0},{5,7},{3,1},{12,14},{10,8},{13,15},{11,9},{20,22},{18,... | collective-permute-start | bytes 2801672 | tf_op jit(solution)/shard_map/ppermute | solution.py:441
  79.0 4.2 %project.7.refs_0_ = bf16[128,1792]{1,0:T(8,128)(2,1)S(1)} custom-call(bf16[64,7296]{1,0:T(8,128)(2,1)S(1)} %collective-permute-done.3.refs_0_, bf16[64,7296]{1,0:T(8,128)(2,1)S(1)} %collective-permute-done.1.refs_1_, bf16[64,7296]{1,0:T(8,128)(2,1)S(1)} %collective-permute-done.4.refs_2_, bf16[64,7296]{1,0:T(8,128)(2,1)S(1)} %collective-permute-done.2.refs_3_, ...), custom_call_target="tpu_custom_call" | custom-call | tf_op jit(solution)/shard_map/project/pallas_call | solution.py:65
  83.2 2.2 %collective-permute-done.6.refs_1_ = bf16[128,1792]{1,0:T(8,128)(2,1)S(1)} collective-permute-done((bf16[128,1792]{1,0:T(8,128)(2,1)S(1)}, bf16[128,1792]{1,0:T(8,128)(2,1)S(1)}, u32[]{:S(2)}, u32[]{:S(2)}) %collective-permute-start.6) | collective-permute-done | bytes 458784 | tf_op jit(solution)/shard_map/ppermute | solution.py:374
  85.4 2.6 %latent_partial.5 = (bf16[128,1792]{1,0:T(8,128)(2,1)S(1)}, bf16[64,2176]{1,0:T(8,128)(2,1)S(1)}, bf16[64,2176]{1,0:T(8,128)(2,1)S(1)}) custom-call(bf16[128,1792]{1,0:T(8,128)(2,1)S(1)} %project.6.refs_0_, bf16[128,1792]{1,0:T(8,128)(2,1)S(1)} %collective-permute-done.6.refs_1_, f32[1,1792]{1,0:T(1,128)S(1)} %broadcast_in_dim.19.refs_2_, ...), custom_call_target="tpu_custom_call" | custom-call | tf_op jit(solution)/shard_map/latent_partial/pallas_call | solution.py:65
  88.0 2.6 %latent_partial.6 = (bf16[128,1792]{1,0:T(8,128)(2,1)S(1)}, bf16[64,2176]{1,0:T(8,128)(2,1)S(1)}, bf16[64,2176]{1,0:T(8,128)(2,1)S(1)}) custom-call(bf16[128,1792]{1,0:T(8,128)(2,1)S(1)} %project.7.refs_0_, bf16[128,1792]{1,0:T(8,128)(2,1)S(1)} %collective-permute-done.9.refs_1_, f32[1,1792]{1,0:T(1,128)S(1)} %broadcast_in_dim.19.refs_2_, ...), custom_call_target="tpu_custom_call" | custom-call | tf_op jit(solution)/shard_map/latent_partial/pallas_call | solution.py:65
  90.6 1.8 %collective-permute-done.11.second_ref = bf16[64,7296]{1,0:T(8,128)(2,1)S(1)} collective-permute-done((bf16[64,7296]{1,0:T(8,128)(2,1)S(1)}, bf16[64,7296]{1,0:T(8,128)(2,1)S(1)}, u32[]{:S(2)}, u32[]{:S(2)}) %collective-permute-start.11) | collective-permute-done | bytes 933920 | tf_op jit(solution)/shard_map/ppermute | solution.py:404
  92.5 3.9 %collective-permute-start.15 = (bf16[64,7296]{1,0:T(8,128)(2,1)S(1)}, bf16[64,7296]{1,0:T(8,128)(2,1)S(1)}, u32[]{:S(2)}, u32[]{:S(2)}) collective-permute-start(bf16[64,7296]{1,0:T(8,128)(2,1)S(1)} %choose.3.refs_1_), channel_id=1, source_target_pairs={{4,6},{2,0},{5,7},{3,1},{12,14},{10,8},{13,15},{11,9},{20,22},{18,... | collective-permute-start | bytes 2801672 | tf_op jit(solution)/shard_map/ppermute | solution.py:447
  96.4 3.7 %project.9.refs_0_ = bf16[128,1792]{1,0:T(8,128)(2,1)S(1)} custom-call(bf16[64,7296]{1,0:T(8,128)(2,1)S(1)} %choose.2.refs_0_, bf16[64,7296]{1,0:T(8,128)(2,1)S(1)} %choose.3.refs_1_, f32[1,3584]{1,0:T(1,128)S(1)} %broadcast_in_dim.17.refs_3_.refs_4_.refs_2_, f32[1,3584]{1,0:T(1,128)S(1)} %broadcast_in_dim.18.refs_4_.refs_5_.refs_3_, ...), custom_call_target="tpu_custom_call" | custom-call | tf_op jit(solution)/shard_map/project/pallas_call | solution.py:65
  100.1 3.5 %collective-permute-start.12 = (bf16[128,1792]{1,0:T(8,128)(2,1)S(1)}, bf16[128,1792]{1,0:T(8,128)(2,1)S(1)}, u32[]{:S(2)}, u32[]{:S(2)}) collective-permute-start(bf16[128,1792]{1,0:T(8,128)(2,1)S(1)} %project.9.refs_0_), channel_id=1, source_target_pairs={{0,1},{2,3},{5,4},{7,6},{8,9},{10,11},{13,12},{15,14},{16,17},{18,... | collective-permute-start | bytes 1376264 | tf_op jit(solution)/shard_map/ppermute | solution.py:374
  103.6 6.8 %collective-permute-done.12.refs_1_ = bf16[128,1792]{1,0:T(8,128)(2,1)S(1)} collective-permute-done((bf16[128,1792]{1,0:T(8,128)(2,1)S(1)}, bf16[128,1792]{1,0:T(8,128)(2,1)S(1)}, u32[]{:S(2)}, u32[]{:S(2)}) %collective-permute-start.12) | collective-permute-done | bytes 458784 | tf_op jit(solution)/shard_map/ppermute | solution.py:374
  110.4 2.8 %latent_partial.7 = (bf16[128,1792]{1,0:T(8,128)(2,1)S(1)}, bf16[64,2176]{1,0:T(8,128)(2,1)S(1)}, bf16[64,2176]{1,0:T(8,128)(2,1)S(1)}, bf16[128,2176]{1,0:T(8,128)(2,1)S(1)}) custom-call(bf16[128,1792]{1,0:T(8,128)(2,1)S(1)} %project.9.refs_0_, bf16[128,1792]{1,0:T(8,128)(2,1)S(1)} %collective-permute-done.12.refs_1_, ...), custom_call_target="tpu_custom_call" | custom-call | tf_op jit(solution)/shard_map/latent_partial/pallas_call | solution.py:65
  113.8 3.2 %collective-permute-start.19 = (bf16[128,2176]{1,0:T(8,128)(2,1)S(1)}, bf16[128,2176]{1,0:T(8,128)(2,1)S(1)}, u32[]{:S(2)}, u32[]{:S(2)}) collective-permute-start(bf16[128,2176]{1,0:T(8,128)(2,1)S(1)} %get-tuple-element.83), channel_id=1, source_target_pairs={{2,4},{4,2},{3,5},{5,3},{10,12},{12,10},{11,13},{13,11},{18,20},{2... | collective-permute-start | bytes 1671176 | tf_op jit(solution)/shard_map/ppermute | solution.py:476
  118.0 1.3 collective-permute-start.20
  119.4 1.3 collective-permute-start.21
  120.7 9.8 %collective-permute-done.15.refs_0_ = bf16[64,7296]{1,0:T(8,128)(2,1)S(1)} collective-permute-done((bf16[64,7296]{1,0:T(8,128)(2,1)S(1)}, bf16[64,7296]{1,0:T(8,128)(2,1)S(1)}, u32[]{:S(2)}, u32[]{:S(2)}) %collective-permute-start.15) | collective-permute-done | bytes 933920 | tf_op jit(solution)/shard_map/ppermute | solution.py:447
  131.3 1.1 collective-permute-done.20.single_ref
  132.4 4.9 %collective-permute-done.19.second_ref = bf16[128,2176]{1,0:T(8,128)(2,1)S(1)} collective-permute-done((bf16[128,2176]{1,0:T(8,128)(2,1)S(1)}, bf16[128,2176]{1,0:T(8,128)(2,1)S(1)}, u32[]{:S(2)}, u32[]{:S(2)}) %collective-permute-start.19) | collective-permute-done | bytes 557088 | tf_op jit(solution)/shard_map/ppermute | solution.py:476
  137.3 1.2 collective-permute-done.21.far_ref
  138.8 3.5 %collective-permute-start.22 = (bf16[64,2304]{1,0:T(8,128)(2,1)S(1)}, bf16[64,2304]{1,0:T(8,128)(2,1)S(1)}, u32[]{:S(2)}, u32[]{:S(2)}) collective-permute-start(bf16[64,2304]{1,0:T(8,128)(2,1)S(1)} %get-tuple-element.85), channel_id=1, source_target_pairs={{2,0},{4,6},{3,1},{5,7},{10,8},{12,14},{11,9},{13,15},{18,16},{20,... | collective-permute-start | bytes 884744 | tf_op jit(solution)/shard_map/ppermute | solution.py:476
  143.0 1.3 collective-permute-start.23
  144.3 1.3 collective-permute-start.24
  145.6 1.0 multiply_sine_fusion
  146.6 1.0 place_rows.1
  147.7 3.9 %collective-permute-done.23.refs_1_ = bf16[32,2176]{1,0:T(8,128)(2,1)S(1)} collective-permute-done((bf16[32,2176]{1,0:T(8,128)(2,1)S(1)}, bf16[32,2176]{1,0:T(8,128)(2,1)S(1)}, u32[]{:S(2)}, u32[]{:S(2)}) %collective-permute-start.23) | collective-permute-done | bytes 139296 | tf_op jit(solution)/shard_map/ppermute | solution.py:476
  151.6 1.5 collective-permute-done.24.refs_2_
  153.1 1.1 finish.1
  (50 shorter events, 6.3 us)
Async XLA Ops:
  0.6 1.2 copy-start.4
  1.8 1.2 copy-start.5
  3.5 25.5 %collective-permute-start.3 = (bf16[64,7296]{1,0:T(8,128)(2,1)S(1)}, bf16[64,7296]{1,0:T(8,128)(2,1)S(1)}, u32[]{:S(2)}, u32[]{:S(2)}) collective-permute-start(bf16[64,7296]{1,0:T(8,128)(2,1)S(1)} %get-tuple-element.49.refs_0_), channel_id=1, source_target_pairs={{0,2},{2,4},{4,6},{1,3},{3,5},{5,7},{8,10},{10,12},{12,14},{9,11},... | collective-permute-start | bytes 2801672 | tf_op jit(solution)/shard_map/ppermute | solution.py:401
  6.9 26.4 %collective-permute-start.4 = (bf16[64,7296]{1,0:T(8,128)(2,1)S(1)}, bf16[64,7296]{1,0:T(8,128)(2,1)S(1)}, u32[]{:S(2)}, u32[]{:S(2)}) collective-permute-start(bf16[64,7296]{1,0:T(8,128)(2,1)S(1)} %get-tuple-element.49.refs_0_), channel_id=1, source_target_pairs={{2,0},{4,2},{6,4},{3,1},{5,3},{7,5},{10,8},{12,10},{14,12},{11,9},... | collective-permute-start | bytes 2801672 | tf_op jit(solution)/shard_map/ppermute | solution.py:404
  9.4 4.3 %collective-permute-start = (f32[128,128]{1,0:T(8,128)S(1)}, f32[128,128]{1,0:T(8,128)S(1)}, u32[]{:S(2)}, u32[]{:S(2)}) collective-permute-start(f32[128,128]{1,0:T(8,128)S(1)} %get-tuple-element.47.sums_ref), channel_id=1, source_target_pairs={{0,1},{1,0},{2,3},{3,2},{4,5},{5,4},{6,7},{7,6},{8,9},{9,8},{10,11... | collective-permute-start | bytes 196616 | tf_op jit(solution)/shard_map/ppermute | solution.py:395
  13.8 36.5 %collective-permute-start.1 = (bf16[64,7296]{1,0:T(8,128)(2,1)S(1)}, bf16[64,7296]{1,0:T(8,128)(2,1)S(1)}, u32[]{:S(2)}, u32[]{:S(2)}) collective-permute-start(bf16[64,7296]{1,0:T(8,128)(2,1)S(1)} %get-tuple-element.48.refs_2_), channel_id=1, source_target_pairs={{0,2},{2,4},{4,6},{1,3},{3,5},{5,7},{8,10},{10,12},{12,14},{9,11},... | collective-permute-start | bytes 2801672 | tf_op jit(solution)/shard_map/ppermute | solution.py:401
  17.3 36.6 %collective-permute-start.2 = (bf16[64,7296]{1,0:T(8,128)(2,1)S(1)}, bf16[64,7296]{1,0:T(8,128)(2,1)S(1)}, u32[]{:S(2)}, u32[]{:S(2)}) collective-permute-start(bf16[64,7296]{1,0:T(8,128)(2,1)S(1)} %get-tuple-element.48.refs_2_), channel_id=1, source_target_pairs={{2,0},{4,2},{6,4},{3,1},{5,3},{7,5},{10,8},{12,10},{14,12},{11,9},... | collective-permute-start | bytes 2801672 | tf_op jit(solution)/shard_map/ppermute | solution.py:404
  28.9 46.5 %collective-permute-start.7 = (bf16[64,7296]{1,0:T(8,128)(2,1)S(1)}, bf16[64,7296]{1,0:T(8,128)(2,1)}, u32[]{:S(2)}, u32[]{:S(2)}) collective-permute-start(bf16[64,7296]{1,0:T(8,128)(2,1)S(1)} %collective-permute-done.3.refs_0_), channel_id=1, source_target_pairs={{2,4},{4,6},{3,5},{5,7},{10,12},{12,14},{11,13},{13,15},{18,20},{2... | collective-permute-start | bytes 2801672 | tf_op jit(solution)/shard_map/ppermute | solution.py:401
  33.4 42.1 %collective-permute-start.8 = (bf16[64,7296]{1,0:T(8,128)(2,1)S(1)}, bf16[64,7296]{1,0:T(8,128)(2,1)}, u32[]{:S(2)}, u32[]{:S(2)}) collective-permute-start(bf16[64,7296]{1,0:T(8,128)(2,1)S(1)} %collective-permute-done.4.refs_2_), channel_id=1, source_target_pairs={{2,0},{4,2},{3,1},{5,3},{10,8},{12,10},{11,9},{13,11},{18,16},{20,... | collective-permute-start | bytes 2801672 | tf_op jit(solution)/shard_map/ppermute | solution.py:404
  35.3 15.0 %collective-permute-start.5 = (f32[128,128]{1,0:T(8,128)S(1)}, f32[128,128]{1,0:T(8,128)S(1)}, u32[]{:S(2)}, u32[]{:S(2)}) collective-permute-start(f32[128,128]{1,0:T(8,128)S(1)} %get-tuple-element.51.refs_1_), channel_id=1, source_target_pairs={{0,6},{6,0},{1,7},{7,1},{8,14},{14,8},{9,15},{15,9},{16,22},{22,16... | collective-permute-start | bytes 196616 | tf_op jit(solution)/shard_map/ppermute | solution.py:398
  37.4 4.7 %copy-start = (bf16[3584,1792]{1,0:T(8,128)(2,1)S(1)}, bf16[3584,1792]{1,0:T(8,128)(2,1)}, u32[]{:S(2)}) copy-start(bf16[3584,1792]{1,0:T(8,128)(2,1)} %refs_4_.5) | copy-start | bytes 38535172
  42.1 4.7 %copy-start.2 = (bf16[3584,1792]{1,0:T(8,128)(2,1)S(1)}, bf16[3584,1792]{1,0:T(8,128)(2,1)}, u32[]{:S(2)}) copy-start(bf16[3584,1792]{1,0:T(8,128)(2,1)} %refs_5_.7) | copy-start | bytes 38535172
  46.7 11.2 %copy-start.1 = (bf16[3584,1792]{1,0:T(8,128)(2,1)S(1)}, bf16[3584,1792]{1,0:T(8,128)(2,1)}, u32[]{:S(2)}) copy-start(bf16[3584,1792]{1,0:T(8,128)(2,1)} %refs_4_.5) | copy-start | bytes 38535172
  46.7 11.2 %copy-start.3 = (bf16[3584,1792]{1,0:T(8,128)(2,1)S(1)}, bf16[3584,1792]{1,0:T(8,128)(2,1)}, u32[]{:S(2)}) copy-start(bf16[3584,1792]{1,0:T(8,128)(2,1)} %refs_5_.7) | copy-start | bytes 38535172
  50.3 28.6 %copy-start.8 = (f32[1792]{0:T(1024)S(1)}, f32[1792]{0:T(1024)}, u32[]{:S(2)}) copy-start(f32[1792]{0:T(1024)} %param.16) | copy-start | bytes 21508
  53.9 36.7 %collective-permute-start.10 = (bf16[64,7296]{1,0:T(8,128)(2,1)S(1)}, bf16[64,7296]{1,0:T(8,128)(2,1)S(1)}, u32[]{:S(2)}, u32[]{:S(2)}) collective-permute-start(bf16[64,7296]{1,0:T(8,128)(2,1)S(1)} %collective-permute-done.1.refs_1_), channel_id=1, source_target_pairs={{2,4},{4,6},{3,5},{5,7},{10,12},{12,14},{11,13},{13,15},{18,20},{2... | collective-permute-start | bytes 2801672 | tf_op jit(solution)/shard_map/ppermute | solution.py:401
  55.5 36.9 %collective-permute-start.11 = (bf16[64,7296]{1,0:T(8,128)(2,1)S(1)}, bf16[64,7296]{1,0:T(8,128)(2,1)S(1)}, u32[]{:S(2)}, u32[]{:S(2)}) collective-permute-start(bf16[64,7296]{1,0:T(8,128)(2,1)S(1)} %collective-permute-done.2.refs_3_), channel_id=1, source_target_pairs={{2,0},{4,2},{3,1},{5,3},{10,8},{12,10},{11,9},{13,11},{18,16},{20,... | collective-permute-start | bytes 2801672 | tf_op jit(solution)/shard_map/ppermute | solution.py:404
  62.0 12.1 %collective-permute-start.9 = (bf16[128,1792]{1,0:T(8,128)(2,1)S(1)}, bf16[128,1792]{1,0:T(8,128)(2,1)S(1)}, u32[]{:S(2)}, u32[]{:S(2)}) collective-permute-start(bf16[128,1792]{1,0:T(8,128)(2,1)S(1)} %project.8), channel_id=1, source_target_pairs={{1,0},{3,2},{2,3},{5,4},{4,5},{6,7},{9,8},{11,10},{10,11},{13,12},... | collective-permute-start | bytes 1376264 | tf_op jit(solution)/shard_map/ppermute | solution.py:374
  74.1 11.3 %collective-permute-start.6 = (bf16[128,1792]{1,0:T(8,128)(2,1)S(1)}, bf16[128,1792]{1,0:T(8,128)(2,1)S(1)}, u32[]{:S(2)}, u32[]{:S(2)}) collective-permute-start(bf16[128,1792]{1,0:T(8,128)(2,1)S(1)} %project.6.refs_0_), channel_id=1, source_target_pairs={{1,0},{3,2},{4,5},{6,7},{9,8},{11,10},{12,13},{14,15},{17,16},{19,... | collective-permute-start | bytes 1376264 | tf_op jit(solution)/shard_map/ppermute | solution.py:374
  75.4 10.0 %slice-start = ((s8[7569408]{0:T(1024)(128)(4,1)}), s8[4194304]{0:T(1024)(128)(4,1)S(1)}, s32[]{:S(2)}) async-start(s8[7569408]{0:T(1024)(128)(4,1)} %bitcast.2), calls=%async_computation | async-start | bytes 8388608
  77.1 40.0 %collective-permute-start.13 = (bf16[64,7296]{1,0:T(8,128)(2,1)S(1)}, bf16[64,7296]{1,0:T(8,128)(2,1)S(1)}, u32[]{:S(2)}, u32[]{:S(2)}) collective-permute-start(bf16[64,7296]{1,0:T(8,128)(2,1)S(1)} %choose.2.refs_0_), channel_id=1, source_target_pairs={{4,6},{2,0},{5,7},{3,1},{12,14},{10,8},{13,15},{11,9},{20,22},{18,... | collective-permute-start | bytes 2801672 | tf_op jit(solution)/shard_map/ppermute | solution.py:441
  78.9 6.5 %slice-start.1 = ((s8[7569408]{0:T(1024)(128)(4,1)}), s8[3375104]{0:T(1024)(128)(4,1)S(1)}, s32[]{:S(2)}) async-start(s8[7569408]{0:T(1024)(128)(4,1)} %bitcast.2), calls=%async_computation.1 | async-start | bytes 6750208
  92.5 38.0 %collective-permute-start.15 = (bf16[64,7296]{1,0:T(8,128)(2,1)S(1)}, bf16[64,7296]{1,0:T(8,128)(2,1)S(1)}, u32[]{:S(2)}, u32[]{:S(2)}) collective-permute-start(bf16[64,7296]{1,0:T(8,128)(2,1)S(1)} %choose.3.refs_1_), channel_id=1, source_target_pairs={{4,6},{2,0},{5,7},{3,1},{12,14},{10,8},{13,15},{11,9},{20,22},{18,... | collective-permute-start | bytes 2801672 | tf_op jit(solution)/shard_map/ppermute | solution.py:447
  100.1 10.3 %collective-permute-start.12 = (bf16[128,1792]{1,0:T(8,128)(2,1)S(1)}, bf16[128,1792]{1,0:T(8,128)(2,1)S(1)}, u32[]{:S(2)}, u32[]{:S(2)}) collective-permute-start(bf16[128,1792]{1,0:T(8,128)(2,1)S(1)} %project.9.refs_0_), channel_id=1, source_target_pairs={{0,1},{2,3},{5,4},{7,6},{8,9},{10,11},{13,12},{15,14},{16,17},{18,... | collective-permute-start | bytes 1376264 | tf_op jit(solution)/shard_map/ppermute | solution.py:374
  113.1 19.2 %collective-permute-start.18 = (bf16[128,2176]{1,0:T(8,128)(2,1)S(1)}, bf16[128,2176]{1,0:T(8,128)(2,1)S(1)}, u32[]{:S(2)}, u32[]{:S(2)}) collective-permute-start(bf16[128,2176]{1,0:T(8,128)(2,1)S(1)} %get-tuple-element.83), channel_id=1, source_target_pairs={{0,4},{7,3},{8,12},{15,11},{16,20},{23,19},{24,28},{31,27}} | collective-permute-start | bytes 1671176 | tf_op jit(solution)/shard_map/ppermute | solution.py:476
  113.8 23.4 %collective-permute-start.19 = (bf16[128,2176]{1,0:T(8,128)(2,1)S(1)}, bf16[128,2176]{1,0:T(8,128)(2,1)S(1)}, u32[]{:S(2)}, u32[]{:S(2)}) collective-permute-start(bf16[128,2176]{1,0:T(8,128)(2,1)S(1)} %get-tuple-element.83), channel_id=1, source_target_pairs={{2,4},{4,2},{3,5},{5,3},{10,12},{12,10},{11,13},{13,11},{18,20},{2... | collective-permute-start | bytes 1671176 | tf_op jit(solution)/shard_map/ppermute | solution.py:476
  117.3 2.0 %collective-permute-start.14 = (bf16[64,1792]{1,0:T(8,128)(2,1)S(1)}, bf16[64,1792]{1,0:T(8,128)(2,1)S(1)}, u32[]{:S(2)}, u32[]{:S(2)}) collective-permute-start(bf16[64,1792]{1,0:T(8,128)(2,1)S(1)} %project.10.refs_0_), channel_id=1, source_target_pairs={{0,1},{7,6},{8,9},{15,14},{16,17},{23,22},{24,25},{31,30}} | collective-permute-start | bytes 688136 | tf_op jit(solution)/shard_map/ppermute | solution.py:374
  118.0 14.3 %collective-permute-start.20 = (bf16[64,2176]{1,0:T(8,128)(2,1)S(1)}, bf16[64,2176]{1,0:T(8,128)(2,1)S(1)}, u32[]{:S(2)}, u32[]{:S(2)}) collective-permute-start(bf16[64,2176]{1,0:T(8,128)(2,1)S(1)} %get-tuple-element.76.inner_ref), channel_id=1, source_target_pairs={{0,2},{6,4},{1,3},{7,5},{8,10},{14,12},{9,11},{15,13},{16,18},{22,... | collective-permute-start | bytes 835592 | tf_op jit(solution)/shard_map/ppermute | solution.py:476
  119.4 27.2 %copy-start.7 = (f32[1536]{0:T(1024)S(1)}, f32[1536]{0:T(1024)}, u32[]{:S(2)}) copy-start(f32[1536]{0:T(1024)} %param.18) | copy-start | bytes 18436
  119.4 19.1 %collective-permute-start.21 = (bf16[64,2176]{1,0:T(8,128)(2,1)S(1)}, bf16[64,2176]{1,0:T(8,128)(2,1)S(1)}, u32[]{:S(2)}, u32[]{:S(2)}) collective-permute-start(bf16[64,2176]{1,0:T(8,128)(2,1)S(1)} %get-tuple-element.77), channel_id=1, source_target_pairs={{6,2},{1,5},{14,10},{9,13},{22,18},{17,21},{30,26},{25,29}} | collective-permute-start | bytes 835592 | tf_op jit(solution)/shard_map/ppermute | solution.py:476
  130.5 22.6 %copy-start.6 = (f32[512]{0:T(512)S(1)}, f32[512]{0:T(512)}, u32[]{:S(2)}) copy-start(f32[512]{0:T(512)} %param.19) | copy-start | bytes 6148
  130.5 12.5 %collective-permute-start.16 = (bf16[32,1792]{1,0:T(8,128)(2,1)S(1)}, bf16[32,1792]{1,0:T(8,128)(2,1)S(1)}, u32[]{:S(2)}, u32[]{:S(2)}) collective-permute-start(bf16[32,1792]{1,0:T(8,128)(2,1)S(1)} %get-tuple-element.80.refs_5_.refs_12_), channel_id=1, source_target_pairs={{0,1},{1,0},{6,7},{7,6},{8,9},{9,8},{14,15},{15,14},{16,17},{17,16... | collective-permute-start | bytes 344072 | tf_op jit(solution)/shard_map/ppermute | solution.py:496
  138.8 14.2 %collective-permute-start.22 = (bf16[64,2304]{1,0:T(8,128)(2,1)S(1)}, bf16[64,2304]{1,0:T(8,128)(2,1)S(1)}, u32[]{:S(2)}, u32[]{:S(2)}) collective-permute-start(bf16[64,2304]{1,0:T(8,128)(2,1)S(1)} %get-tuple-element.85), channel_id=1, source_target_pairs={{2,0},{4,6},{3,1},{5,7},{10,8},{12,14},{11,9},{13,15},{18,16},{20,... | collective-permute-start | bytes 884744 | tf_op jit(solution)/shard_map/ppermute | solution.py:476
  142.3 4.3 %collective-permute-start.17 = (bf16[32,1792]{1,0:T(8,128)(2,1)S(1)}, bf16[32,1792]{1,0:T(8,128)(2,1)S(1)}, u32[]{:S(2)}, u32[]{:S(2)}) collective-permute-start(bf16[32,1792]{1,0:T(8,128)(2,1)S(1)} %get-tuple-element.79.refs_0_), channel_id=1, source_target_pairs={{7,6},{0,1},{15,14},{8,9},{23,22},{16,17},{31,30},{24,25}} | collective-permute-start | bytes 344072 | tf_op jit(solution)/shard_map/ppermute | solution.py:374
  143.0 8.6 %collective-permute-start.23 = (bf16[32,2176]{1,0:T(8,128)(2,1)S(1)}, bf16[32,2176]{1,0:T(8,128)(2,1)S(1)}, u32[]{:S(2)}, u32[]{:S(2)}) collective-permute-start(bf16[32,2176]{1,0:T(8,128)(2,1)S(1)} %get-tuple-element.86), channel_id=1, source_target_pairs={{6,2},{1,5},{14,10},{9,13},{22,18},{17,21},{30,26},{25,29}} | collective-permute-start | bytes 417800 | tf_op jit(solution)/shard_map/ppermute | solution.py:476
  144.3 8.7 %collective-permute-start.24 = (bf16[32,2176]{1,0:T(8,128)(2,1)S(1)}, bf16[32,2176]{1,0:T(8,128)(2,1)S(1)}, u32[]{:S(2)}, u32[]{:S(2)}) collective-permute-start(bf16[32,2176]{1,0:T(8,128)(2,1)S(1)} %get-tuple-element.86), channel_id=1, source_target_pairs={{7,2},{0,5},{15,10},{8,13},{23,18},{16,21},{31,26},{24,29}} | collective-permute-start | bytes 417800 | tf_op jit(solution)/shard_map/ppermute | solution.py:505

commit v5 on v4

--- a/solution.py
+++ b/solution.py
@@ -14,6 +14,7 @@
 LANES = 128
 TERMS = 3
 VMEM_BYTES = 6 * 1024 * 1024
+ENTER_BYTES = 56 * 1024 * 1024
 
 epsilon = 1e-06
 
@@ -61,14 +62,14 @@
 NO_COST = pl.CostEstimate(flops=0, bytes_accessed=0, transcendentals=0)
 
 
-def kernel(body, name, inputs, outputs, scratch=()):
+def kernel(body, name, inputs, outputs, scratch=(), place=VMEM, vmem=VMEM_BYTES):
     return pl.pallas_call(
         body,
-        in_specs=[VMEM] * len(inputs),
+        in_specs=[place] * len(inputs),
         out_specs=[VMEM] * len(outputs),
         out_shape=[jax.ShapeDtypeStruct(shape, kind) for shape, kind in outputs],
         scratch_shapes=list(scratch),
-        compiler_params=pltpu.CompilerParams(vmem_limit_bytes=VMEM_BYTES),
+        compiler_params=pltpu.CompilerParams(vmem_limit_bytes=vmem),
         cost_estimate=NO_COST,
         name=name,
     )(*inputs)
@@ -82,24 +83,45 @@
     rows, depth = hidden.shape
     height = rows // 2
 
-    def body(hidden_ref, embed_ref, piece_ref, sums_ref):
+    def body(hidden_ref, embed_ref, piece_ref, sems):
+        part = half_rows(0, height, swaps())
+        copies = [
+            pltpu.make_async_copy(
+                ref.at[part, :], piece_ref.at[:, pl.ds(column * depth, depth)], sems.at[column]
+            )
+            for column, ref in enumerate((hidden_ref, embed_ref))
+        ]
+        for copy in copies:
+            copy.start()
+        for copy in copies:
+            copy.wait()
+
+    return kernel(
+        body,
+        "enter",
+        [hidden, embed],
+        [((height, 2 * depth), jnp.bfloat16)],
+        [pltpu.SemaphoreType.DMA((2,))],
+        place=pl.BlockSpec(memory_space=pl.ANY),
+        vmem=ENTER_BYTES,
+    )[0]
+
+
+def add_squares(hidden, embed, swaps):
+    rows = hidden.shape[0]
+    height = rows // 2
+
+    def body(hidden_ref, embed_ref, sums_ref):
         swapped = swaps()
+        lane = lax.broadcasted_iota(jnp.int32, (height, LANES), 1)
         for half in range(2):
-            sums = []
+            total = jnp.zeros((height, LANES), jnp.float32)
             for column, ref in enumerate((hidden_ref, embed_ref)):
-                part = ref[half_rows(half, height, swapped), :]
-                if half == 0:
-                    piece_ref[:, column * depth : (column + 1) * depth] = part
-                wide = part.astype(jnp.float32)
-                sums.append(jnp.sum(wide * wide, axis=1, keepdims=True))
-            lane = lax.broadcasted_iota(jnp.int32, (height, LANES), 1)
-            sums_ref[half * height : (half + 1) * height, :] = jnp.where(
-                lane == 0, sums[0], jnp.where(lane == 1, sums[1], 0.0)
-            )
-        piece_ref[:, 2 * depth :] = jnp.zeros((height, LANES), jnp.bfloat16)
-
-    outputs = [((height, 2 * depth + LANES), jnp.bfloat16), ((rows, LANES), jnp.float32)]
-    return kernel(body, "enter", [hidden, embed], outputs)
+                wide = ref[half_rows(half, height, swapped), :].astype(jnp.float32)
+                total = jnp.where(lane == column, jnp.sum(wide * wide, axis=1, keepdims=True), total)
+            sums_ref[half * height : (half + 1) * height, :] = total
+
+    return kernel(body, "add_squares", [hidden, embed], [((rows, LANES), jnp.float32)])[0]
 
 
 def pack(hidden, embed, sums, other_sums, swaps):
@@ -196,19 +218,6 @@
         [pltpu.VMEM((padded, 2 * depth), jnp.bfloat16)],
     )
     return result[0] if keeps_first is None else result
-
-
-def choose(first, second, takes_first):
-    def body(first_ref, second_ref, out):
-        @pl.when(takes_first())
-        def _():
-            out[...] = first_ref[...]
-
-        @pl.when(jnp.logical_not(takes_first()))
-        def _():
-            out[...] = second_ref[...]
-
-    return kernel(body, "choose", [first, second], [(first.shape, first.dtype)])[0]
 
 
 def latent_partial(own, received, gain, w_latent, cuts, known=(), route=(), needed=None):
@@ -382,7 +391,8 @@
     def upper():
         return jnp.where(me() >= line // 2, 1, 0)
 
-    first_piece, sums = enter(hidden_in, embed_in, upper)
+    first_piece = enter(hidden_in, embed_in, upper)
+    sums = add_squares(hidden_in, embed_in, upper)
     tokens = lax.axis_size("mp") * line * rows_out
     tables = rope_tables(
         w_latent.shape[1] - Q_LAT - KV_LAT, jnp.arange(tokens, dtype=jnp.int32) % LENGTH
@@ -397,62 +407,54 @@
     pieces = [first_piece, second_piece]
     sums_three = lax.ppermute(sums, "dp", [(0, last), (last, 0)])
 
-    def go_ahead(x, k):
-        return lax.ppermute(x, "dp", [(i, i + 1) for i in range(k - 1, last)])
-
-    def go_back(x, k):
-        return lax.ppermute(x, "dp", [(i + 1, i) for i in range(0, line - k)])
-
-    ahead_one = [go_ahead(x, 1) for x in pieces]
-    back_one = [go_back(x, 1) for x in pieces]
-    ahead_two = [go_ahead(ahead_one[0], 2)]
-    back_two = [go_back(back_one[0], 2)]
-    ahead_one[0], back_one[0], sums = lax.optimization_barrier((ahead_one[0], back_one[0], sums))
+    pairs_on = [(0, 1), (1, 0), (2, 3), (3, 2)]
+    middle_on = [(1, 2), (2, 1)]
+    ends_on = [(2, 3), (1, 0)]
+    pair_one = [lax.ppermute(x, "dp", pairs_on) for x in pieces]
+    cross_one = [lax.ppermute(x, "dp", middle_on) for x in pieces]
+    ends_two = [lax.ppermute(cross_one[0], "dp", ends_on)]
+    middle_two = [lax.ppermute(pair_one[0], "dp", middle_on)]
+    pair_one[0], cross_one[0], sums = lax.optimization_barrier((pair_one[0], cross_one[0], sums))
     groups = [(piece, sums, low) for piece, (low, _) in zip(pieces, halves, strict=True)]
     got_own = project(groups, weights)
-    ahead_one[1], back_one[1], got_own, sums_three = lax.optimization_barrier(
-        (ahead_one[1], back_one[1], got_own, sums_three)
-    )
-    ahead_two.append(go_ahead(ahead_one[1], 2))
-    back_two.append(go_back(back_one[1], 2))
+    pair_one[1], cross_one[1], got_own, sums_three = lax.optimization_barrier(
+        (pair_one[1], cross_one[1], got_own, sums_three)
+    )
+    ends_two.append(lax.ppermute(cross_one[1], "dp", ends_on))
+    middle_two.append(lax.ppermute(pair_one[1], "dp", middle_on))
     received_own = to_owner(got_own, senders_of(0))
     mtp_own, lat_own = latent_partial(got_own, received_own, attn_gain, w_latent, halves)
 
-    def from_ahead():
-        return me() >= line // 2
-
-    def ahead_is_own():
-        near = jnp.where(me() >= 1, me() - 1, me() + 1)
-        owned = jnp.where(near >= line // 2, 1, 0) == mine()
-        return jnp.where(me() >= 1, owned, jnp.logical_not(owned))
-
-    def ahead_is_other():
-        return jnp.logical_not(ahead_is_own())
-
-    groups_ahead = [(x, ahead_one[1], low) for x, (low, _) in zip(ahead_one, halves, strict=True)]
-    groups_back = [(x, back_one[1], low) for x, (low, _) in zip(back_one, halves, strict=True)]
-    received_one = to_owner(project(groups_ahead, weights, groups_back, ahead_is_other), senders_of(1))
-    got_one = project(groups_ahead, weights, groups_back, ahead_is_own)
-    ahead_two[0], back_two[0], received_one = lax.optimization_barrier(
-        (ahead_two[0], back_two[0], received_one)
-    )
-    two = [choose(ahead_two[0], back_two[0], from_ahead)]
-    ends_on = [(line - 2, last), (1, 0)]
-    three = [lax.ppermute(two[0], "dp", ends_on)]
+    def pair_is_own():
+        return upper() == mine()
+
+    def pair_is_other():
+        return upper() != mine()
+
+    groups_pair = [(x, pair_one[1], low) for x, (low, _) in zip(pair_one, halves, strict=True)]
+    groups_cross = [(x, cross_one[1], low) for x, (low, _) in zip(cross_one, halves, strict=True)]
+    received_one = to_owner(project(groups_pair, weights, groups_cross, pair_is_other), senders_of(1))
+    got_one = project(groups_pair, weights, groups_cross, pair_is_own)
+    middle_two[0], ends_two[0], received_one = lax.optimization_barrier(
+        (middle_two[0], ends_two[0], received_one)
+    )
+    three = [lax.ppermute(middle_two[0], "dp", ends_on)]
     mtp_one, lat_one = latent_partial(got_one, received_one, attn_gain, w_latent, halves)
-    ahead_two[1], back_two[1], lat_one, lat_own = lax.optimization_barrier(
-        (ahead_two[1], back_two[1], lat_one, lat_own)
-    )
-    two.append(choose(ahead_two[1], back_two[1], from_ahead))
-    three.append(lax.ppermute(two[1], "dp", ends_on))
+    middle_two[1], ends_two[1], lat_one, lat_own = lax.optimization_barrier(
+        (middle_two[1], ends_two[1], lat_one, lat_own)
+    )
+    three.append(lax.ppermute(middle_two[1], "dp", ends_on))
 
     def is_end():
         return jnp.logical_or(me() == 0, me() == last)
 
-    got_two = project([(x, two[1], low) for x, (low, _) in zip(two, halves, strict=True)], weights)
+    groups_ends = [(x, ends_two[1], low) for x, (low, _) in zip(ends_two, halves, strict=True)]
+    groups_middle = [(x, middle_two[1], low) for x, (low, _) in zip(middle_two, halves, strict=True)]
+    got_two = project(groups_ends, weights, groups_middle, is_end)
     received_two = to_owner(got_two, senders_of(2))
     sums_three = after(sums_three, got_two)
     got_three = [project([(three[0], sums_three, 0)], weights, needed=is_end)]
+    received_two = after(received_two, got_three[0])
 
     def part_for(half, place):
         return 2 * jnp.abs(me() - (2 * mine() + half)) + jnp.where(mine() == 1, 1 - place, place)

time: 155 us -> 151 us (0.974)
  starting transfers between devices: 53 us -> 42.8 us
  local copies, waits for them, and re-layouts: 13.2 us -> 19 us
    ppermute x10, starting transfers between devices: 27.9 us -> 19.9 us  [the longest x2 6.96 us: shards_line(): cross_one = [lax.ppermute(x, 'dp', middle_on) for x in pieces]]
    unnamed x22 -> x32, local copies, waits for them, and re-layouts: 11.7 us -> 17.5 us
    ppermute x5, waiting for transfers between devices: 17.7 us -> 13.7 us  [to_owner(): return lax.ppermute(value, ('dp', 'mp'), pairs)]
    ppermute x6, waiting for transfers between devices: 11.2 us -> 14.7 us  [send(): return lax.ppermute(value, ('dp', 'mp'), pairs)]
    ppermute x5, starting transfers between devices: 9.51 us -> 7.79 us  [to_owner(): return lax.ppermute(value, ('dp', 'mp'), pairs)]
    pallas_call x18 -> x17, Pallas kernels: 28.4 us -> 29.1 us  [kernel(): pl.pallas_call(body, in_specs=[place] * len(inputs), out_specs=[VMEM] * l...]
where the time goes in v5:
time: 151 us; the launch traced here: 150 us
  waiting for transfers between devices  56.7 us (38%)
  starting transfers between devices  42.8 us (28%)
  Pallas kernels  29.1 us (19%)
  local copies, waits for them, and re-layouts  19 us (13%)
    pallas_call x17, Pallas kernels, kernel(): pl.pallas_call(body, in_specs=[place] * len(inputs), out_specs=[VMEM] * l...  29.1 us
    unnamed x32, local copies, waits for them, and re-layouts  17.5 us
    ppermute x6, waiting for transfers between devices, send(): return lax.ppermute(value, ('dp', 'mp'), pairs)  14.7 us
    ppermute x5, waiting for transfers between devices, to_owner(): return lax.ppermute(value, ('dp', 'mp'), pairs)  13.7 us
    ppermute x6, starting transfers between devices, send(): return lax.ppermute(value, ('dp', 'mp'), pairs)  10.8 us
    ppermute x2, waiting for transfers between devices, shards_line(): pair_one = [lax.ppermute(x, 'dp', pairs_on) for x in pieces]  9.17 us
    ppermute x5, starting transfers between devices, to_owner(): return lax.ppermute(value, ('dp', 'mp'), pairs)  7.79 us
    ppermute x2, starting transfers between devices, shards_line(): cross_one = [lax.ppermute(x, 'dp', middle_on) for x in pieces]  6.96 us
  transfers between devices with their start and end apart: 25, of which 13 were waited for; matrix products, arithmetic and copies ran while one was open for 2% of the time, Pallas kernels for 17%

profile of v5, /device:TPU:8, one launch (start us, length us, event | category | flops | bytes accessed | tf_op | source)
XLA Modules:
  0.0 149.8 jit_solution(15141164208915922581)
XLA Ops:
  0.6 2.1 %enter.1.refs_0_ = bf16[64,7168]{1,0:T(8,128)(2,1)} custom-call(bf16[128,3584]{1,0:T(8,128)(2,1)} %hidden_ref.5, bf16[128,3584]{1,0:T(8,128)(2,1)} %embed_ref.5), custom_call_target="tpu_custom_call" | custom-call | tf_op jit(solution)/shard_map/enter/pallas_call | solution.py:66
  2.9 5.0 %collective-permute-start.4 = (bf16[64,7168]{1,0:T(8,128)(2,1)}, bf16[64,7168]{1,0:T(8,128)(2,1)S(1)}, u32[]{:S(2)}, u32[]{:S(2)}) collective-permute-start(bf16[64,7168]{1,0:T(8,128)(2,1)} %enter.1.refs_0_), channel_id=1, source_target_pairs={{2,4},{4,2},{3,5},{5,3},{10,12},{12,10},{11,13},{13,11},{18,20},{2... | collective-permute-start | bytes 2752520 | tf_op jit(solution)/shard_map/ppermute | solution.py:414
  7.9 1.2 copy-done.4
  9.1 1.2 copy-done.5
  10.7 1.5 %collective-permute-start = (f32[128,128]{1,0:T(8,128)S(1)}, f32[128,128]{1,0:T(8,128)S(1)}, u32[]{:S(2)}, u32[]{:S(2)}) collective-permute-start(f32[128,128]{1,0:T(8,128)S(1)} %add_squares.1.sums_ref), channel_id=1, source_target_pairs={{0,1},{1,0},{2,3},{3,2},{4,5},{5,4},{6,7},{7,6},{8,9},{9,8},{10,11... | collective-permute-start | bytes 196616 | tf_op jit(solution)/shard_map/ppermute | solution.py:405
  12.3 2.7 %collective-permute-done.other_ref = f32[128,128]{1,0:T(8,128)S(1)} collective-permute-done((f32[128,128]{1,0:T(8,128)S(1)}, f32[128,128]{1,0:T(8,128)S(1)}, u32[]{:S(2)}, u32[]{:S(2)}) %collective-permute-start) | collective-permute-done | bytes 65568 | tf_op jit(solution)/shard_map/ppermute | solution.py:405
  15.2 1.9 %collective-permute-start.2 = (bf16[64,7296]{1,0:T(8,128)(2,1)S(1)}, bf16[64,7296]{1,0:T(8,128)(2,1)S(1)}, u32[]{:S(2)}, u32[]{:S(2)}) collective-permute-start(bf16[64,7296]{1,0:T(8,128)(2,1)S(1)} %get-tuple-element.46.refs_2_), channel_id=1, source_target_pairs={{2,4},{4,2},{3,5},{5,3},{10,12},{12,10},{11,13},{13,11},{18,20},{2... | collective-permute-start | bytes 2801672 | tf_op jit(solution)/shard_map/ppermute | solution.py:414
  17.1 9.2 %collective-permute-done.3.refs_0_ = bf16[64,7168]{1,0:T(8,128)(2,1)S(1)} collective-permute-done((bf16[64,7168]{1,0:T(8,128)(2,1)}, bf16[64,7168]{1,0:T(8,128)(2,1)S(1)}, u32[]{:S(2)}, u32[]{:S(2)}) %collective-permute-start.3) | collective-permute-done | bytes 917536 | tf_op jit(solution)/shard_map/ppermute | solution.py:413
  26.3 3.5 %collective-permute-start.7 = (bf16[64,7168]{1,0:T(8,128)(2,1)S(1)}, bf16[64,7168]{1,0:T(8,128)(2,1)S(1)}, u32[]{:S(2)}, u32[]{:S(2)}) collective-permute-start(bf16[64,7168]{1,0:T(8,128)(2,1)S(1)} %collective-permute-done.3.refs_0_), channel_id=1, source_target_pairs={{2,4},{4,2},{3,5},{5,3},{10,12},{12,10},{11,13},{13,11},{18,20},{2... | collective-permute-start | bytes 2752520 | tf_op jit(solution)/shard_map/ppermute | solution.py:416
  29.8 1.3 collective-permute-start.8
  33.3 4.6 %copy-done = bf16[3584,1792]{1,0:T(8,128)(2,1)S(1)} copy-done((bf16[3584,1792]{1,0:T(8,128)(2,1)S(1)}, bf16[3584,1792]{1,0:T(8,128)(2,1)}, u32[]{:S(2)}) %copy-start) | copy-done | bytes 12845080
  38.0 4.6 %copy-done.1 = bf16[3584,1792]{1,0:T(8,128)(2,1)S(1)} copy-done((bf16[3584,1792]{1,0:T(8,128)(2,1)S(1)}, bf16[3584,1792]{1,0:T(8,128)(2,1)}, u32[]{:S(2)}) %copy-start.1) | copy-done | bytes 12845080
  42.6 1.2 copy-done.6
  43.8 3.5 %project.6.refs_0_ = bf16[128,1792]{1,0:T(8,128)(2,1)S(1)} custom-call(bf16[64,7168]{1,0:T(8,128)(2,1)S(1)} %copy-done.6, f32[128,128]{1,0:T(8,128)S(1)} %get-tuple-element.48.refs_1_, bf16[64,7296]{1,0:T(8,128)(2,1)S(1)} %get-tuple-element.46.refs_2_, f32[1,3584]{1,0:T(1,128)S(1)} %broadcast_in_dim.17.refs_3_.refs_4_.refs_2_, ...), custom_call_target="tpu_custom_call" | custom-call | tf_op jit(solution)/shard_map/project/pallas_call | solution.py:66
  47.4 3.4 %collective-permute-done.2.refs_3_ = bf16[64,7296]{1,0:T(8,128)(2,1)S(1)} collective-permute-done((bf16[64,7296]{1,0:T(8,128)(2,1)S(1)}, bf16[64,7296]{1,0:T(8,128)(2,1)S(1)}, u32[]{:S(2)}, u32[]{:S(2)}) %collective-permute-start.2) | collective-permute-done | bytes 933920 | tf_op jit(solution)/shard_map/ppermute | solution.py:414
  50.8 3.9 %collective-permute-start.10 = (bf16[64,7296]{1,0:T(8,128)(2,1)S(1)}, bf16[64,7296]{1,0:T(8,128)(2,1)S(1)}, u32[]{:S(2)}, u32[]{:S(2)}) collective-permute-start(bf16[64,7296]{1,0:T(8,128)(2,1)S(1)} %collective-permute-done.1.refs_1_), channel_id=1, source_target_pairs={{2,4},{4,2},{3,5},{5,3},{10,12},{12,10},{11,13},{13,11},{18,20},{2... | collective-permute-start | bytes 2801672 | tf_op jit(solution)/shard_map/ppermute | solution.py:424
  54.7 1.3 collective-permute-start.11
  56.1 4.6 %copy-done.2 = bf16[3584,1792]{1,0:T(8,128)(2,1)S(1)} copy-done((bf16[3584,1792]{1,0:T(8,128)(2,1)S(1)}, bf16[3584,1792]{1,0:T(8,128)(2,1)}, u32[]{:S(2)}) %copy-start.2) | copy-done | bytes 12845080
  60.8 4.0 %project.8 = bf16[128,1792]{1,0:T(8,128)(2,1)S(1)} custom-call(bf16[64,7168]{1,0:T(8,128)(2,1)S(1)} %collective-permute-done.3.refs_0_, bf16[64,7296]{1,0:T(8,128)(2,1)S(1)} %collective-permute-done.1.refs_1_, bf16[64,7168]{1,0:T(8,128)(2,1)S(1)} %collective-permute-done.4.refs_2_, bf16[64,7296]{1,0:T(8,128)(2,1)S(1)} %collective-permute-done.2.refs_3_, ...), custom_call_target="tpu_custom_call" | custom-call | tf_op jit(solution)/shard_map/project/pallas_call | solution.py:66
  64.8 3.7 %collective-permute-start.9 = (bf16[128,1792]{1,0:T(8,128)(2,1)S(1)}, bf16[128,1792]{1,0:T(8,128)(2,1)S(1)}, u32[]{:S(2)}, u32[]{:S(2)}) collective-permute-start(bf16[128,1792]{1,0:T(8,128)(2,1)S(1)} %project.8), channel_id=1, source_target_pairs={{1,0},{3,2},{2,3},{5,4},{4,5},{6,7},{9,8},{11,10},{10,11},{13,12},... | collective-permute-start | bytes 1376264 | tf_op jit(solution)/shard_map/ppermute | solution.py:383
  68.5 7.8 %collective-permute-done.9.refs_1_ = bf16[128,1792]{1,0:T(8,128)(2,1)S(1)} collective-permute-done((bf16[128,1792]{1,0:T(8,128)(2,1)S(1)}, bf16[128,1792]{1,0:T(8,128)(2,1)S(1)}, u32[]{:S(2)}, u32[]{:S(2)}) %collective-permute-start.9) | collective-permute-done | bytes 458784 | tf_op jit(solution)/shard_map/ppermute | solution.py:383
  76.3 1.3 collective-permute-start.6
  77.6 1.3 collective-permute-start.13
  79.0 4.2 %project.7.refs_0_ = bf16[128,1792]{1,0:T(8,128)(2,1)S(1)} custom-call(bf16[64,7168]{1,0:T(8,128)(2,1)S(1)} %collective-permute-done.3.refs_0_, bf16[64,7296]{1,0:T(8,128)(2,1)S(1)} %collective-permute-done.1.refs_1_, bf16[64,7168]{1,0:T(8,128)(2,1)S(1)} %collective-permute-done.4.refs_2_, bf16[64,7296]{1,0:T(8,128)(2,1)S(1)} %collective-permute-done.2.refs_3_, ...), custom_call_target="tpu_custom_call" | custom-call | tf_op jit(solution)/shard_map/project/pallas_call | solution.py:66
  83.3 3.4 %collective-permute-done.6.refs_1_ = bf16[128,1792]{1,0:T(8,128)(2,1)S(1)} collective-permute-done((bf16[128,1792]{1,0:T(8,128)(2,1)S(1)}, bf16[128,1792]{1,0:T(8,128)(2,1)S(1)}, u32[]{:S(2)}, u32[]{:S(2)}) %collective-permute-start.6) | collective-permute-done | bytes 458784 | tf_op jit(solution)/shard_map/ppermute | solution.py:383
  86.7 2.5 %latent_partial.5 = (bf16[128,1792]{1,0:T(8,128)(2,1)S(1)}, bf16[64,2176]{1,0:T(8,128)(2,1)S(1)}, bf16[64,2176]{1,0:T(8,128)(2,1)S(1)}) custom-call(bf16[128,1792]{1,0:T(8,128)(2,1)S(1)} %project.6.refs_0_, bf16[128,1792]{1,0:T(8,128)(2,1)S(1)} %collective-permute-done.6.refs_1_, f32[1,1792]{1,0:T(1,128)S(1)} %broadcast_in_dim.19.refs_2_, ...), custom_call_target="tpu_custom_call" | custom-call | tf_op jit(solution)/shard_map/latent_partial/pallas_call | solution.py:66
  89.2 2.6 %latent_partial.6 = (bf16[128,1792]{1,0:T(8,128)(2,1)S(1)}, bf16[64,2176]{1,0:T(8,128)(2,1)S(1)}, bf16[64,2176]{1,0:T(8,128)(2,1)S(1)}) custom-call(bf16[128,1792]{1,0:T(8,128)(2,1)S(1)} %project.7.refs_0_, bf16[128,1792]{1,0:T(8,128)(2,1)S(1)} %collective-permute-done.9.refs_1_, f32[1,1792]{1,0:T(1,128)S(1)} %broadcast_in_dim.19.refs_2_, ...), custom_call_target="tpu_custom_call" | custom-call | tf_op jit(solution)/shard_map/latent_partial/pallas_call | solution.py:66
  91.8 1.3 collective-permute-start.15
  93.2 4.1 %project.9.refs_0_ = bf16[128,1792]{1,0:T(8,128)(2,1)S(1)} custom-call(bf16[64,7168]{1,0:T(8,128)(2,1)S(1)} %collective-permute-done.8.refs_0_, bf16[64,7296]{1,0:T(8,128)(2,1)S(1)} %collective-permute-done.11.refs_1_, bf16[64,7168]{1,0:T(8,128)(2,1)S(1)} %collective-permute-done.7.refs_2_, bf16[64,7296]{1,0:T(8,128)(2,1)S(1)} %collective-permute-done.10.refs_3_, ...), custom_call_target="tpu_custom_call" | custom-call | tf_op jit(solution)/shard_map/project/pallas_call | solution.py:66
  97.2 1.5 collective-permute-start.12
  98.7 5.8 %collective-permute-done.13.refs_0_ = bf16[64,7168]{1,0:T(8,128)(2,1)S(1)} collective-permute-done((bf16[64,7168]{1,0:T(8,128)(2,1)S(1)}, bf16[64,7168]{1,0:T(8,128)(2,1)S(1)}, u32[]{:S(2)}, u32[]{:S(2)}) %collective-permute-start.13) | collective-permute-done | bytes 917536 | tf_op jit(solution)/shard_map/ppermute | solution.py:441
  104.6 2.5 %collective-permute-done.12.refs_1_ = bf16[128,1792]{1,0:T(8,128)(2,1)S(1)} collective-permute-done((bf16[128,1792]{1,0:T(8,128)(2,1)S(1)}, bf16[128,1792]{1,0:T(8,128)(2,1)S(1)}, u32[]{:S(2)}, u32[]{:S(2)}) %collective-permute-start.12) | collective-permute-done | bytes 458784 | tf_op jit(solution)/shard_map/ppermute | solution.py:383
  107.0 2.7 %latent_partial.7 = (bf16[128,1792]{1,0:T(8,128)(2,1)S(1)}, bf16[64,2176]{1,0:T(8,128)(2,1)S(1)}, bf16[64,2176]{1,0:T(8,128)(2,1)S(1)}, bf16[128,2176]{1,0:T(8,128)(2,1)S(1)}) custom-call(bf16[128,1792]{1,0:T(8,128)(2,1)S(1)} %project.9.refs_0_, bf16[128,1792]{1,0:T(8,128)(2,1)S(1)} %collective-permute-done.12.refs_1_, ...), custom_call_target="tpu_custom_call" | custom-call | tf_op jit(solution)/shard_map/latent_partial/pallas_call | solution.py:66
  110.5 4.9 %collective-permute-start.19 = (bf16[128,2176]{1,0:T(8,128)(2,1)S(1)}, bf16[128,2176]{1,0:T(8,128)(2,1)S(1)}, u32[]{:S(2)}, u32[]{:S(2)}) collective-permute-start(bf16[128,2176]{1,0:T(8,128)(2,1)S(1)} %get-tuple-element.81), channel_id=1, source_target_pairs={{2,4},{4,2},{3,5},{5,3},{10,12},{12,10},{11,13},{13,11},{18,20},{2... | collective-permute-start | bytes 1671176 | tf_op jit(solution)/shard_map/ppermute | solution.py:478
  116.0 1.3 collective-permute-start.20
  117.4 1.3 collective-permute-start.21
  118.7 5.1 %collective-permute-done.15.refs_0_ = bf16[64,7296]{1,0:T(8,128)(2,1)S(1)} collective-permute-done((bf16[64,7296]{1,0:T(8,128)(2,1)S(1)}, bf16[64,7296]{1,0:T(8,128)(2,1)S(1)}, u32[]{:S(2)}, u32[]{:S(2)}) %collective-permute-start.15) | collective-permute-done | bytes 933920 | tf_op jit(solution)/shard_map/ppermute | solution.py:446
  124.5 7.3 %collective-permute-done.20.single_ref = bf16[64,2176]{1,0:T(8,128)(2,1)S(1)} collective-permute-done((bf16[64,2176]{1,0:T(8,128)(2,1)S(1)}, bf16[64,2176]{1,0:T(8,128)(2,1)S(1)}, u32[]{:S(2)}, u32[]{:S(2)}) %collective-permute-start.20) | collective-permute-done | bytes 278560 | tf_op jit(solution)/shard_map/ppermute | solution.py:478
  131.9 1.6 %collective-permute-done.21.far_ref = bf16[64,2176]{1,0:T(8,128)(2,1)S(1)} collective-permute-done((bf16[64,2176]{1,0:T(8,128)(2,1)S(1)}, bf16[64,2176]{1,0:T(8,128)(2,1)S(1)}, u32[]{:S(2)}, u32[]{:S(2)}) %collective-permute-start.21) | collective-permute-done | bytes 278560 | tf_op jit(solution)/shard_map/ppermute | solution.py:478
  133.5 2.6 %collective-permute-done.19.second_ref = bf16[128,2176]{1,0:T(8,128)(2,1)S(1)} collective-permute-done((bf16[128,2176]{1,0:T(8,128)(2,1)S(1)}, bf16[128,2176]{1,0:T(8,128)(2,1)S(1)}, u32[]{:S(2)}, u32[]{:S(2)}) %collective-permute-start.19) | collective-permute-done | bytes 557088 | tf_op jit(solution)/shard_map/ppermute | solution.py:478
  136.3 1.3 collective-permute-start.22
  138.6 1.3 collective-permute-start.23
  139.9 1.3 collective-permute-start.24
  141.2 1.0 multiply_sine_fusion
  142.3 1.0 place_rows.1
  143.3 3.2 %collective-permute-done.23.refs_1_ = bf16[32,2176]{1,0:T(8,128)(2,1)S(1)} collective-permute-done((bf16[32,2176]{1,0:T(8,128)(2,1)S(1)}, bf16[32,2176]{1,0:T(8,128)(2,1)S(1)}, u32[]{:S(2)}, u32[]{:S(2)}) %collective-permute-start.23) | collective-permute-done | bytes 139296 | tf_op jit(solution)/shard_map/ppermute | solution.py:478
  146.5 2.2 %collective-permute-done.24.refs_2_ = bf16[32,2176]{1,0:T(8,128)(2,1)S(1)} collective-permute-done((bf16[32,2176]{1,0:T(8,128)(2,1)S(1)}, bf16[32,2176]{1,0:T(8,128)(2,1)S(1)}, u32[]{:S(2)}, u32[]{:S(2)}) %collective-permute-start.24) | collective-permute-done | bytes 139296 | tf_op jit(solution)/shard_map/ppermute | solution.py:507
  148.7 1.1 finish.1
  (60 shorter events, 6.4 us)
Async XLA Ops:
  0.6 55.4 %slice-start = ((s8[12845056]{0:T(1024)(128)(4,1)}), s8[262144]{0:T(1024)(128)(4,1)S(1)}, s32[]{:S(2)}) async-start(s8[12845056]{0:T(1024)(128)(4,1)} %bitcast.2), calls=%async_computation | async-start | bytes 524288
  2.8 23.5 %collective-permute-start.3 = (bf16[64,7168]{1,0:T(8,128)(2,1)}, bf16[64,7168]{1,0:T(8,128)(2,1)S(1)}, u32[]{:S(2)}, u32[]{:S(2)}) collective-permute-start(bf16[64,7168]{1,0:T(8,128)(2,1)} %enter.1.refs_0_), channel_id=1, source_target_pairs={{0,2},{2,0},{4,6},{6,4},{1,3},{3,1},{5,7},{7,5},{8,10},{10,8},{12,... | collective-permute-start | bytes 2752520 | tf_op jit(solution)/shard_map/ppermute | solution.py:413
  2.9 26.9 %collective-permute-start.4 = (bf16[64,7168]{1,0:T(8,128)(2,1)}, bf16[64,7168]{1,0:T(8,128)(2,1)S(1)}, u32[]{:S(2)}, u32[]{:S(2)}) collective-permute-start(bf16[64,7168]{1,0:T(8,128)(2,1)} %enter.1.refs_0_), channel_id=1, source_target_pairs={{2,4},{4,2},{3,5},{5,3},{10,12},{12,10},{11,13},{13,11},{18,20},{2... | collective-permute-start | bytes 2752520 | tf_op jit(solution)/shard_map/ppermute | solution.py:414
  7.9 1.2 copy-start.4
  9.1 1.2 copy-start.5
  10.7 4.3 %collective-permute-start = (f32[128,128]{1,0:T(8,128)S(1)}, f32[128,128]{1,0:T(8,128)S(1)}, u32[]{:S(2)}, u32[]{:S(2)}) collective-permute-start(f32[128,128]{1,0:T(8,128)S(1)} %add_squares.1.sums_ref), channel_id=1, source_target_pairs={{0,1},{1,0},{2,3},{3,2},{4,5},{5,4},{6,7},{7,6},{8,9},{9,8},{10,11... | collective-permute-start | bytes 196616 | tf_op jit(solution)/shard_map/ppermute | solution.py:405
  15.1 32.2 %collective-permute-start.1 = (bf16[64,7296]{1,0:T(8,128)(2,1)S(1)}, bf16[64,7296]{1,0:T(8,128)(2,1)S(1)}, u32[]{:S(2)}, u32[]{:S(2)}) collective-permute-start(bf16[64,7296]{1,0:T(8,128)(2,1)S(1)} %get-tuple-element.46.refs_2_), channel_id=1, source_target_pairs={{0,2},{2,0},{4,6},{6,4},{1,3},{3,1},{5,7},{7,5},{8,10},{10,8},{12,... | collective-permute-start | bytes 2801672 | tf_op jit(solution)/shard_map/ppermute | solution.py:413
  15.2 35.5 %collective-permute-start.2 = (bf16[64,7296]{1,0:T(8,128)(2,1)S(1)}, bf16[64,7296]{1,0:T(8,128)(2,1)S(1)}, u32[]{:S(2)}, u32[]{:S(2)}) collective-permute-start(bf16[64,7296]{1,0:T(8,128)(2,1)S(1)} %get-tuple-element.46.refs_2_), channel_id=1, source_target_pairs={{2,4},{4,2},{3,5},{5,3},{10,12},{12,10},{11,13},{13,11},{18,20},{2... | collective-permute-start | bytes 2801672 | tf_op jit(solution)/shard_map/ppermute | solution.py:414
  26.3 51.3 %collective-permute-start.7 = (bf16[64,7168]{1,0:T(8,128)(2,1)S(1)}, bf16[64,7168]{1,0:T(8,128)(2,1)S(1)}, u32[]{:S(2)}, u32[]{:S(2)}) collective-permute-start(bf16[64,7168]{1,0:T(8,128)(2,1)S(1)} %collective-permute-done.3.refs_0_), channel_id=1, source_target_pairs={{2,4},{4,2},{3,5},{5,3},{10,12},{12,10},{11,13},{13,11},{18,20},{2... | collective-permute-start | bytes 2752520 | tf_op jit(solution)/shard_map/ppermute | solution.py:416
  29.8 47.8 %collective-permute-start.8 = (bf16[64,7168]{1,0:T(8,128)(2,1)S(1)}, bf16[64,7168]{1,0:T(8,128)(2,1)S(1)}, u32[]{:S(2)}, u32[]{:S(2)}) collective-permute-start(bf16[64,7168]{1,0:T(8,128)(2,1)S(1)} %collective-permute-done.4.refs_2_), channel_id=1, source_target_pairs={{4,6},{2,0},{5,7},{3,1},{12,14},{10,8},{13,15},{11,9},{20,22},{18,... | collective-permute-start | bytes 2752520 | tf_op jit(solution)/shard_map/ppermute | solution.py:415
  31.2 16.2 %collective-permute-start.5 = (f32[128,128]{1,0:T(8,128)S(1)}, f32[128,128]{1,0:T(8,128)S(1)}, u32[]{:S(2)}, u32[]{:S(2)}) collective-permute-start(f32[128,128]{1,0:T(8,128)S(1)} %get-tuple-element.48.refs_1_), channel_id=1, source_target_pairs={{0,6},{6,0},{1,7},{7,1},{8,14},{14,8},{9,15},{15,9},{16,22},{22,16... | collective-permute-start | bytes 196616 | tf_op jit(solution)/shard_map/ppermute | solution.py:408
  33.3 4.7 %copy-start = (bf16[3584,1792]{1,0:T(8,128)(2,1)S(1)}, bf16[3584,1792]{1,0:T(8,128)(2,1)}, u32[]{:S(2)}) copy-start(bf16[3584,1792]{1,0:T(8,128)(2,1)} %refs_4_.3) | copy-start | bytes 38535172
  38.0 4.7 %copy-start.1 = (bf16[3584,1792]{1,0:T(8,128)(2,1)S(1)}, bf16[3584,1792]{1,0:T(8,128)(2,1)}, u32[]{:S(2)}) copy-start(bf16[3584,1792]{1,0:T(8,128)(2,1)} %refs_5_.5) | copy-start | bytes 38535172
  42.6 1.2 copy-start.6
  43.8 12.3 %slice-start.1 = ((s8[12845056]{0:T(1024)(128)(4,1)}), s8[4194304]{0:T(1024)(128)(4,1)S(1)}, s32[]{:S(2)}) async-start(s8[12845056]{0:T(1024)(128)(4,1)} %bitcast.2), calls=%async_computation.1 | async-start | bytes 8388608
  43.8 12.3 %slice-start.2 = ((s8[12845056]{0:T(1024)(128)(4,1)}), s8[4194304]{0:T(1024)(128)(4,1)S(1)}, s32[]{:S(2)}) async-start(s8[12845056]{0:T(1024)(128)(4,1)} %bitcast.2), calls=%async_computation.2 | async-start | bytes 8388608
  43.8 12.3 %slice-start.3 = ((s8[12845056]{0:T(1024)(128)(4,1)}), s8[4194304]{0:T(1024)(128)(4,1)S(1)}, s32[]{:S(2)}) async-start(s8[12845056]{0:T(1024)(128)(4,1)} %bitcast.2), calls=%async_computation.3 | async-start | bytes 8388608
  43.8 35.2 %copy-start.9 = (f32[1792]{0:T(1024)S(1)}, f32[1792]{0:T(1024)}, u32[]{:S(2)}) copy-start(f32[1792]{0:T(1024)} %param.16) | copy-start | bytes 21508
  50.8 41.1 %collective-permute-start.10 = (bf16[64,7296]{1,0:T(8,128)(2,1)S(1)}, bf16[64,7296]{1,0:T(8,128)(2,1)S(1)}, u32[]{:S(2)}, u32[]{:S(2)}) collective-permute-start(bf16[64,7296]{1,0:T(8,128)(2,1)S(1)} %collective-permute-done.1.refs_1_), channel_id=1, source_target_pairs={{2,4},{4,2},{3,5},{5,3},{10,12},{12,10},{11,13},{13,11},{18,20},{2... | collective-permute-start | bytes 2801672 | tf_op jit(solution)/shard_map/ppermute | solution.py:424
  54.7 37.1 %collective-permute-start.11 = (bf16[64,7296]{1,0:T(8,128)(2,1)S(1)}, bf16[64,7296]{1,0:T(8,128)(2,1)S(1)}, u32[]{:S(2)}, u32[]{:S(2)}) collective-permute-start(bf16[64,7296]{1,0:T(8,128)(2,1)S(1)} %collective-permute-done.2.refs_3_), channel_id=1, source_target_pairs={{4,6},{2,0},{5,7},{3,1},{12,14},{10,8},{13,15},{11,9},{20,22},{18,... | collective-permute-start | bytes 2801672 | tf_op jit(solution)/shard_map/ppermute | solution.py:423
  56.1 4.7 %copy-start.2 = (bf16[3584,1792]{1,0:T(8,128)(2,1)S(1)}, bf16[3584,1792]{1,0:T(8,128)(2,1)}, u32[]{:S(2)}) copy-start(bf16[3584,1792]{1,0:T(8,128)(2,1)} %refs_5_.5) | copy-start | bytes 38535172
  60.8 18.2 %copy-start.3 = (bf16[3584,1792]{1,0:T(8,128)(2,1)S(1)}, bf16[3584,1792]{1,0:T(8,128)(2,1)}, u32[]{:S(2)}) copy-start(bf16[3584,1792]{1,0:T(8,128)(2,1)} %refs_5_.5) | copy-start | bytes 38535172
  60.8 25.9 %slice-start.4 = ((s8[7569408]{0:T(1024)(128)(4,1)}), s8[4194304]{0:T(1024)(128)(4,1)S(1)}, s32[]{:S(2)}) async-start(s8[7569408]{0:T(1024)(128)(4,1)} %bitcast.4), calls=%async_computation.4 | async-start | bytes 8388608
  64.8 21.9 %slice-start.5 = ((s8[7569408]{0:T(1024)(128)(4,1)}), s8[3375104]{0:T(1024)(128)(4,1)S(1)}, s32[]{:S(2)}) async-start(s8[7569408]{0:T(1024)(128)(4,1)} %bitcast.4), calls=%async_computation.5 | async-start | bytes 6750208
  64.8 11.5 %collective-permute-start.9 = (bf16[128,1792]{1,0:T(8,128)(2,1)S(1)}, bf16[128,1792]{1,0:T(8,128)(2,1)S(1)}, u32[]{:S(2)}, u32[]{:S(2)}) collective-permute-start(bf16[128,1792]{1,0:T(8,128)(2,1)S(1)} %project.8), channel_id=1, source_target_pairs={{1,0},{3,2},{2,3},{5,4},{4,5},{6,7},{9,8},{11,10},{10,11},{13,12},... | collective-permute-start | bytes 1376264 | tf_op jit(solution)/shard_map/ppermute | solution.py:383
  76.3 10.4 %collective-permute-start.6 = (bf16[128,1792]{1,0:T(8,128)(2,1)S(1)}, bf16[128,1792]{1,0:T(8,128)(2,1)S(1)}, u32[]{:S(2)}, u32[]{:S(2)}) collective-permute-start(bf16[128,1792]{1,0:T(8,128)(2,1)S(1)} %project.6.refs_0_), channel_id=1, source_target_pairs={{1,0},{3,2},{4,5},{6,7},{9,8},{11,10},{12,13},{14,15},{17,16},{19,... | collective-permute-start | bytes 1376264 | tf_op jit(solution)/shard_map/ppermute | solution.py:383
  77.6 26.9 %collective-permute-start.13 = (bf16[64,7168]{1,0:T(8,128)(2,1)S(1)}, bf16[64,7168]{1,0:T(8,128)(2,1)S(1)}, u32[]{:S(2)}, u32[]{:S(2)}) collective-permute-start(bf16[64,7168]{1,0:T(8,128)(2,1)S(1)} %collective-permute-done.7.refs_2_), channel_id=1, source_target_pairs={{4,6},{2,0},{5,7},{3,1},{12,14},{10,8},{13,15},{11,9},{20,22},{18,... | collective-permute-start | bytes 2752520 | tf_op jit(solution)/shard_map/ppermute | solution.py:441
  91.8 31.9 %collective-permute-start.15 = (bf16[64,7296]{1,0:T(8,128)(2,1)S(1)}, bf16[64,7296]{1,0:T(8,128)(2,1)S(1)}, u32[]{:S(2)}, u32[]{:S(2)}) collective-permute-start(bf16[64,7296]{1,0:T(8,128)(2,1)S(1)} %collective-permute-done.10.refs_3_), channel_id=1, source_target_pairs={{4,6},{2,0},{5,7},{3,1},{12,14},{10,8},{13,15},{11,9},{20,22},{18,... | collective-permute-start | bytes 2801672 | tf_op jit(solution)/shard_map/ppermute | solution.py:446
  97.2 9.8 %collective-permute-start.12 = (bf16[128,1792]{1,0:T(8,128)(2,1)S(1)}, bf16[128,1792]{1,0:T(8,128)(2,1)S(1)}, u32[]{:S(2)}, u32[]{:S(2)}) collective-permute-start(bf16[128,1792]{1,0:T(8,128)(2,1)S(1)} %project.9.refs_0_), channel_id=1, source_target_pairs={{0,1},{2,3},{5,4},{7,6},{8,9},{10,11},{13,12},{15,14},{16,17},{18,... | collective-permute-start | bytes 1376264 | tf_op jit(solution)/shard_map/ppermute | solution.py:383
  109.7 23.7 %collective-permute-start.18 = (bf16[128,2176]{1,0:T(8,128)(2,1)S(1)}, bf16[128,2176]{1,0:T(8,128)(2,1)S(1)}, u32[]{:S(2)}, u32[]{:S(2)}) collective-permute-start(bf16[128,2176]{1,0:T(8,128)(2,1)S(1)} %get-tuple-element.81), channel_id=1, source_target_pairs={{0,4},{7,3},{8,12},{15,11},{16,20},{23,19},{24,28},{31,27}} | collective-permute-start | bytes 1671176 | tf_op jit(solution)/shard_map/ppermute | solution.py:478
  110.5 25.6 %collective-permute-start.19 = (bf16[128,2176]{1,0:T(8,128)(2,1)S(1)}, bf16[128,2176]{1,0:T(8,128)(2,1)S(1)}, u32[]{:S(2)}, u32[]{:S(2)}) collective-permute-start(bf16[128,2176]{1,0:T(8,128)(2,1)S(1)} %get-tuple-element.81), channel_id=1, source_target_pairs={{2,4},{4,2},{3,5},{5,3},{10,12},{12,10},{11,13},{13,11},{18,20},{2... | collective-permute-start | bytes 1671176 | tf_op jit(solution)/shard_map/ppermute | solution.py:478
  115.4 2.0 %collective-permute-start.14 = (bf16[64,1792]{1,0:T(8,128)(2,1)S(1)}, bf16[64,1792]{1,0:T(8,128)(2,1)S(1)}, u32[]{:S(2)}, u32[]{:S(2)}) collective-permute-start(bf16[64,1792]{1,0:T(8,128)(2,1)S(1)} %project.10.refs_0_), channel_id=1, source_target_pairs={{0,1},{7,6},{8,9},{15,14},{16,17},{23,22},{24,25},{31,30}} | collective-permute-start | bytes 688136 | tf_op jit(solution)/shard_map/ppermute | solution.py:383
  116.0 15.9 %collective-permute-start.20 = (bf16[64,2176]{1,0:T(8,128)(2,1)S(1)}, bf16[64,2176]{1,0:T(8,128)(2,1)S(1)}, u32[]{:S(2)}, u32[]{:S(2)}) collective-permute-start(bf16[64,2176]{1,0:T(8,128)(2,1)S(1)} %get-tuple-element.74.inner_ref), channel_id=1, source_target_pairs={{0,2},{6,4},{1,3},{7,5},{8,10},{14,12},{9,11},{15,13},{16,18},{22,... | collective-permute-start | bytes 835592 | tf_op jit(solution)/shard_map/ppermute | solution.py:478
  117.4 24.9 %copy-start.8 = (f32[1536]{0:T(1024)S(1)}, f32[1536]{0:T(1024)}, u32[]{:S(2)}) copy-start(f32[1536]{0:T(1024)} %param.18) | copy-start | bytes 18436
  117.4 16.1 %collective-permute-start.21 = (bf16[64,2176]{1,0:T(8,128)(2,1)S(1)}, bf16[64,2176]{1,0:T(8,128)(2,1)S(1)}, u32[]{:S(2)}, u32[]{:S(2)}) collective-permute-start(bf16[64,2176]{1,0:T(8,128)(2,1)S(1)} %get-tuple-element.75), channel_id=1, source_target_pairs={{6,2},{1,5},{14,10},{9,13},{22,18},{17,21},{30,26},{25,29}} | collective-permute-start | bytes 835592 | tf_op jit(solution)/shard_map/ppermute | solution.py:478
  123.7 25.0 %copy-start.7 = (f32[512]{0:T(512)S(1)}, f32[512]{0:T(512)}, u32[]{:S(2)}) copy-start(f32[512]{0:T(512)} %param.19) | copy-start | bytes 6148
  123.7 14.6 %collective-permute-start.16 = (bf16[32,1792]{1,0:T(8,128)(2,1)S(1)}, bf16[32,1792]{1,0:T(8,128)(2,1)S(1)}, u32[]{:S(2)}, u32[]{:S(2)}) collective-permute-start(bf16[32,1792]{1,0:T(8,128)(2,1)S(1)} %get-tuple-element.78.refs_5_.refs_12_), channel_id=1, source_target_pairs={{0,1},{1,0},{6,7},{7,6},{8,9},{9,8},{14,15},{15,14},{16,17},{17,16... | collective-permute-start | bytes 344072 | tf_op jit(solution)/shard_map/ppermute | solution.py:498
  136.3 12.4 %collective-permute-start.22 = (bf16[64,2304]{1,0:T(8,128)(2,1)S(1)}, bf16[64,2304]{1,0:T(8,128)(2,1)S(1)}, u32[]{:S(2)}, u32[]{:S(2)}) collective-permute-start(bf16[64,2304]{1,0:T(8,128)(2,1)S(1)} %get-tuple-element.83), channel_id=1, source_target_pairs={{2,0},{4,6},{3,1},{5,7},{10,8},{12,14},{11,9},{13,15},{18,16},{20,... | collective-permute-start | bytes 884744 | tf_op jit(solution)/shard_map/ppermute | solution.py:478
  137.7 4.6 %collective-permute-start.17 = (bf16[32,1792]{1,0:T(8,128)(2,1)S(1)}, bf16[32,1792]{1,0:T(8,128)(2,1)S(1)}, u32[]{:S(2)}, u32[]{:S(2)}) collective-permute-start(bf16[32,1792]{1,0:T(8,128)(2,1)S(1)} %get-tuple-element.77.refs_0_), channel_id=1, source_target_pairs={{7,6},{0,1},{15,14},{8,9},{23,22},{16,17},{31,30},{24,25}} | collective-permute-start | bytes 344072 | tf_op jit(solution)/shard_map/ppermute | solution.py:383
  138.6 7.8 %collective-permute-start.23 = (bf16[32,2176]{1,0:T(8,128)(2,1)S(1)}, bf16[32,2176]{1,0:T(8,128)(2,1)S(1)}, u32[]{:S(2)}, u32[]{:S(2)}) collective-permute-start(bf16[32,2176]{1,0:T(8,128)(2,1)S(1)} %get-tuple-element.84), channel_id=1, source_target_pairs={{6,2},{1,5},{14,10},{9,13},{22,18},{17,21},{30,26},{25,29}} | collective-permute-start | bytes 417800 | tf_op jit(solution)/shard_map/ppermute | solution.py:478
  139.9 8.7 %collective-permute-start.24 = (bf16[32,2176]{1,0:T(8,128)(2,1)S(1)}, bf16[32,2176]{1,0:T(8,128)(2,1)S(1)}, u32[]{:S(2)}, u32[]{:S(2)}) collective-permute-start(bf16[32,2176]{1,0:T(8,128)(2,1)S(1)} %get-tuple-element.84), channel_id=1, source_target_pairs={{7,2},{0,5},{15,10},{8,13},{23,18},{16,21},{31,26},{24,29}} | collective-permute-start | bytes 417800 | tf_op jit(solution)/shard_map/ppermute | solution.py:507

commit v6 on v5

--- a/solution.py
+++ b/solution.py
@@ -491,7 +491,7 @@
     )
     mtp_three = [mtp]
     far = send(lat, to_middle)
-    sums_three = after(sums_three, got_three[0], inner, lat)
+    sums_three = after(sums_three, got_three[0], inner)
     part = rows_out // 2
     kept, given = project([(three[1], sums_three, rows_out)], weights, keeps_first=lambda: mine() == 0, needed=is_end)
     ends = (0, last)

time: 151 us -> 151 us (level)
  no operation moved by 1% of the time
where the time goes in v6:
time: 151 us; the launch traced here: 150 us
  waiting for transfers between devices  56.7 us (38%)
  starting transfers between devices  42.8 us (28%)
  Pallas kernels  29.1 us (19%)
  local copies, waits for them, and re-layouts  19 us (13%)
    pallas_call x17, Pallas kernels, kernel(): pl.pallas_call(body, in_specs=[place] * len(inputs), out_specs=[VMEM] * l...  29.1 us
    unnamed x32, local copies, waits for them, and re-layouts  17.5 us
    ppermute x6, waiting for transfers between devices, send(): return lax.ppermute(value, ('dp', 'mp'), pairs)  14.7 us
    ppermute x5, waiting for transfers between devices, to_owner(): return lax.ppermute(value, ('dp', 'mp'), pairs)  13.7 us
    ppermute x6, starting transfers between devices, send(): return lax.ppermute(value, ('dp', 'mp'), pairs)  10.8 us
    ppermute x2, waiting for transfers between devices, shards_line(): pair_one = [lax.ppermute(x, 'dp', pairs_on) for x in pieces]  9.17 us
    ppermute x5, starting transfers between devices, to_owner(): return lax.ppermute(value, ('dp', 'mp'), pairs)  7.79 us
    ppermute x2, starting transfers between devices, shards_line(): cross_one = [lax.ppermute(x, 'dp', middle_on) for x in pieces]  6.96 us
  transfers between devices with their start and end apart: 25, of which 13 were waited for; matrix products, arithmetic and copies ran while one was open for 2% of the time, Pallas kernels for 17%

profile of v6, /device:TPU:8, one launch (start us, length us, event | category | flops | bytes accessed | tf_op | source)
XLA Modules:
  0.0 149.8 jit_solution(15141164208915922581)
XLA Ops:
  0.6 2.1 %enter.1.refs_0_ = bf16[64,7168]{1,0:T(8,128)(2,1)} custom-call(bf16[128,3584]{1,0:T(8,128)(2,1)} %hidden_ref.5, bf16[128,3584]{1,0:T(8,128)(2,1)} %embed_ref.5), custom_call_target="tpu_custom_call" | custom-call | tf_op jit(solution)/shard_map/enter/pallas_call | solution.py:66
  2.9 5.0 %collective-permute-start.4 = (bf16[64,7168]{1,0:T(8,128)(2,1)}, bf16[64,7168]{1,0:T(8,128)(2,1)S(1)}, u32[]{:S(2)}, u32[]{:S(2)}) collective-permute-start(bf16[64,7168]{1,0:T(8,128)(2,1)} %enter.1.refs_0_), channel_id=1, source_target_pairs={{2,4},{4,2},{3,5},{5,3},{10,12},{12,10},{11,13},{13,11},{18,20},{2... | collective-permute-start | bytes 2752520 | tf_op jit(solution)/shard_map/ppermute | solution.py:414
  7.9 1.2 copy-done.4
  9.1 1.2 copy-done.5
  10.7 1.5 %collective-permute-start = (f32[128,128]{1,0:T(8,128)S(1)}, f32[128,128]{1,0:T(8,128)S(1)}, u32[]{:S(2)}, u32[]{:S(2)}) collective-permute-start(f32[128,128]{1,0:T(8,128)S(1)} %add_squares.1.sums_ref), channel_id=1, source_target_pairs={{0,1},{1,0},{2,3},{3,2},{4,5},{5,4},{6,7},{7,6},{8,9},{9,8},{10,11... | collective-permute-start | bytes 196616 | tf_op jit(solution)/shard_map/ppermute | solution.py:405
  12.3 2.7 %collective-permute-done.other_ref = f32[128,128]{1,0:T(8,128)S(1)} collective-permute-done((f32[128,128]{1,0:T(8,128)S(1)}, f32[128,128]{1,0:T(8,128)S(1)}, u32[]{:S(2)}, u32[]{:S(2)}) %collective-permute-start) | collective-permute-done | bytes 65568 | tf_op jit(solution)/shard_map/ppermute | solution.py:405
  15.2 1.9 %collective-permute-start.2 = (bf16[64,7296]{1,0:T(8,128)(2,1)S(1)}, bf16[64,7296]{1,0:T(8,128)(2,1)S(1)}, u32[]{:S(2)}, u32[]{:S(2)}) collective-permute-start(bf16[64,7296]{1,0:T(8,128)(2,1)S(1)} %get-tuple-element.46.refs_2_), channel_id=1, source_target_pairs={{2,4},{4,2},{3,5},{5,3},{10,12},{12,10},{11,13},{13,11},{18,20},{2... | collective-permute-start | bytes 2801672 | tf_op jit(solution)/shard_map/ppermute | solution.py:414
  17.1 9.2 %collective-permute-done.3.refs_0_ = bf16[64,7168]{1,0:T(8,128)(2,1)S(1)} collective-permute-done((bf16[64,7168]{1,0:T(8,128)(2,1)}, bf16[64,7168]{1,0:T(8,128)(2,1)S(1)}, u32[]{:S(2)}, u32[]{:S(2)}) %collective-permute-start.3) | collective-permute-done | bytes 917536 | tf_op jit(solution)/shard_map/ppermute | solution.py:413
  26.3 3.5 %collective-permute-start.7 = (bf16[64,7168]{1,0:T(8,128)(2,1)S(1)}, bf16[64,7168]{1,0:T(8,128)(2,1)S(1)}, u32[]{:S(2)}, u32[]{:S(2)}) collective-permute-start(bf16[64,7168]{1,0:T(8,128)(2,1)S(1)} %collective-permute-done.3.refs_0_), channel_id=1, source_target_pairs={{2,4},{4,2},{3,5},{5,3},{10,12},{12,10},{11,13},{13,11},{18,20},{2... | collective-permute-start | bytes 2752520 | tf_op jit(solution)/shard_map/ppermute | solution.py:416
  29.8 1.3 collective-permute-start.8
  33.3 4.6 %copy-done = bf16[3584,1792]{1,0:T(8,128)(2,1)S(1)} copy-done((bf16[3584,1792]{1,0:T(8,128)(2,1)S(1)}, bf16[3584,1792]{1,0:T(8,128)(2,1)}, u32[]{:S(2)}) %copy-start) | copy-done | bytes 12845080
  38.0 4.6 %copy-done.1 = bf16[3584,1792]{1,0:T(8,128)(2,1)S(1)} copy-done((bf16[3584,1792]{1,0:T(8,128)(2,1)S(1)}, bf16[3584,1792]{1,0:T(8,128)(2,1)}, u32[]{:S(2)}) %copy-start.1) | copy-done | bytes 12845080
  42.6 1.2 copy-done.6
  43.8 3.5 %project.6.refs_0_ = bf16[128,1792]{1,0:T(8,128)(2,1)S(1)} custom-call(bf16[64,7168]{1,0:T(8,128)(2,1)S(1)} %copy-done.6, f32[128,128]{1,0:T(8,128)S(1)} %get-tuple-element.48.refs_1_, bf16[64,7296]{1,0:T(8,128)(2,1)S(1)} %get-tuple-element.46.refs_2_, f32[1,3584]{1,0:T(1,128)S(1)} %broadcast_in_dim.17.refs_3_.refs_4_.refs_2_, ...), custom_call_target="tpu_custom_call" | custom-call | tf_op jit(solution)/shard_map/project/pallas_call | solution.py:66
  47.4 3.4 %collective-permute-done.2.refs_3_ = bf16[64,7296]{1,0:T(8,128)(2,1)S(1)} collective-permute-done((bf16[64,7296]{1,0:T(8,128)(2,1)S(1)}, bf16[64,7296]{1,0:T(8,128)(2,1)S(1)}, u32[]{:S(2)}, u32[]{:S(2)}) %collective-permute-start.2) | collective-permute-done | bytes 933920 | tf_op jit(solution)/shard_map/ppermute | solution.py:414
  50.8 3.9 %collective-permute-start.10 = (bf16[64,7296]{1,0:T(8,128)(2,1)S(1)}, bf16[64,7296]{1,0:T(8,128)(2,1)S(1)}, u32[]{:S(2)}, u32[]{:S(2)}) collective-permute-start(bf16[64,7296]{1,0:T(8,128)(2,1)S(1)} %collective-permute-done.1.refs_1_), channel_id=1, source_target_pairs={{2,4},{4,2},{3,5},{5,3},{10,12},{12,10},{11,13},{13,11},{18,20},{2... | collective-permute-start | bytes 2801672 | tf_op jit(solution)/shard_map/ppermute | solution.py:424
  54.7 1.3 collective-permute-start.11
  56.1 4.6 %copy-done.2 = bf16[3584,1792]{1,0:T(8,128)(2,1)S(1)} copy-done((bf16[3584,1792]{1,0:T(8,128)(2,1)S(1)}, bf16[3584,1792]{1,0:T(8,128)(2,1)}, u32[]{:S(2)}) %copy-start.2) | copy-done | bytes 12845080
  60.8 4.0 %project.8 = bf16[128,1792]{1,0:T(8,128)(2,1)S(1)} custom-call(bf16[64,7168]{1,0:T(8,128)(2,1)S(1)} %collective-permute-done.3.refs_0_, bf16[64,7296]{1,0:T(8,128)(2,1)S(1)} %collective-permute-done.1.refs_1_, bf16[64,7168]{1,0:T(8,128)(2,1)S(1)} %collective-permute-done.4.refs_2_, bf16[64,7296]{1,0:T(8,128)(2,1)S(1)} %collective-permute-done.2.refs_3_, ...), custom_call_target="tpu_custom_call" | custom-call | tf_op jit(solution)/shard_map/project/pallas_call | solution.py:66
  64.8 3.7 %collective-permute-start.9 = (bf16[128,1792]{1,0:T(8,128)(2,1)S(1)}, bf16[128,1792]{1,0:T(8,128)(2,1)S(1)}, u32[]{:S(2)}, u32[]{:S(2)}) collective-permute-start(bf16[128,1792]{1,0:T(8,128)(2,1)S(1)} %project.8), channel_id=1, source_target_pairs={{1,0},{3,2},{2,3},{5,4},{4,5},{6,7},{9,8},{11,10},{10,11},{13,12},... | collective-permute-start | bytes 1376264 | tf_op jit(solution)/shard_map/ppermute | solution.py:383
  68.5 7.8 %collective-permute-done.9.refs_1_ = bf16[128,1792]{1,0:T(8,128)(2,1)S(1)} collective-permute-done((bf16[128,1792]{1,0:T(8,128)(2,1)S(1)}, bf16[128,1792]{1,0:T(8,128)(2,1)S(1)}, u32[]{:S(2)}, u32[]{:S(2)}) %collective-permute-start.9) | collective-permute-done | bytes 458784 | tf_op jit(solution)/shard_map/ppermute | solution.py:383
  76.3 1.3 collective-permute-start.6
  77.6 1.3 collective-permute-start.13
  79.0 4.2 %project.7.refs_0_ = bf16[128,1792]{1,0:T(8,128)(2,1)S(1)} custom-call(bf16[64,7168]{1,0:T(8,128)(2,1)S(1)} %collective-permute-done.3.refs_0_, bf16[64,7296]{1,0:T(8,128)(2,1)S(1)} %collective-permute-done.1.refs_1_, bf16[64,7168]{1,0:T(8,128)(2,1)S(1)} %collective-permute-done.4.refs_2_, bf16[64,7296]{1,0:T(8,128)(2,1)S(1)} %collective-permute-done.2.refs_3_, ...), custom_call_target="tpu_custom_call" | custom-call | tf_op jit(solution)/shard_map/project/pallas_call | solution.py:66
  83.3 3.4 %collective-permute-done.6.refs_1_ = bf16[128,1792]{1,0:T(8,128)(2,1)S(1)} collective-permute-done((bf16[128,1792]{1,0:T(8,128)(2,1)S(1)}, bf16[128,1792]{1,0:T(8,128)(2,1)S(1)}, u32[]{:S(2)}, u32[]{:S(2)}) %collective-permute-start.6) | collective-permute-done | bytes 458784 | tf_op jit(solution)/shard_map/ppermute | solution.py:383
  86.7 2.5 %latent_partial.5 = (bf16[128,1792]{1,0:T(8,128)(2,1)S(1)}, bf16[64,2176]{1,0:T(8,128)(2,1)S(1)}, bf16[64,2176]{1,0:T(8,128)(2,1)S(1)}) custom-call(bf16[128,1792]{1,0:T(8,128)(2,1)S(1)} %project.6.refs_0_, bf16[128,1792]{1,0:T(8,128)(2,1)S(1)} %collective-permute-done.6.refs_1_, f32[1,1792]{1,0:T(1,128)S(1)} %broadcast_in_dim.19.refs_2_, ...), custom_call_target="tpu_custom_call" | custom-call | tf_op jit(solution)/shard_map/latent_partial/pallas_call | solution.py:66
  89.2 2.6 %latent_partial.6 = (bf16[128,1792]{1,0:T(8,128)(2,1)S(1)}, bf16[64,2176]{1,0:T(8,128)(2,1)S(1)}, bf16[64,2176]{1,0:T(8,128)(2,1)S(1)}) custom-call(bf16[128,1792]{1,0:T(8,128)(2,1)S(1)} %project.7.refs_0_, bf16[128,1792]{1,0:T(8,128)(2,1)S(1)} %collective-permute-done.9.refs_1_, f32[1,1792]{1,0:T(1,128)S(1)} %broadcast_in_dim.19.refs_2_, ...), custom_call_target="tpu_custom_call" | custom-call | tf_op jit(solution)/shard_map/latent_partial/pallas_call | solution.py:66
  91.8 1.3 collective-permute-start.15
  93.2 4.1 %project.9.refs_0_ = bf16[128,1792]{1,0:T(8,128)(2,1)S(1)} custom-call(bf16[64,7168]{1,0:T(8,128)(2,1)S(1)} %collective-permute-done.8.refs_0_, bf16[64,7296]{1,0:T(8,128)(2,1)S(1)} %collective-permute-done.11.refs_1_, bf16[64,7168]{1,0:T(8,128)(2,1)S(1)} %collective-permute-done.7.refs_2_, bf16[64,7296]{1,0:T(8,128)(2,1)S(1)} %collective-permute-done.10.refs_3_, ...), custom_call_target="tpu_custom_call" | custom-call | tf_op jit(solution)/shard_map/project/pallas_call | solution.py:66
  97.2 1.5 collective-permute-start.12
  98.7 5.8 %collective-permute-done.13.refs_0_ = bf16[64,7168]{1,0:T(8,128)(2,1)S(1)} collective-permute-done((bf16[64,7168]{1,0:T(8,128)(2,1)S(1)}, bf16[64,7168]{1,0:T(8,128)(2,1)S(1)}, u32[]{:S(2)}, u32[]{:S(2)}) %collective-permute-start.13) | collective-permute-done | bytes 917536 | tf_op jit(solution)/shard_map/ppermute | solution.py:441
  104.6 2.5 %collective-permute-done.12.refs_1_ = bf16[128,1792]{1,0:T(8,128)(2,1)S(1)} collective-permute-done((bf16[128,1792]{1,0:T(8,128)(2,1)S(1)}, bf16[128,1792]{1,0:T(8,128)(2,1)S(1)}, u32[]{:S(2)}, u32[]{:S(2)}) %collective-permute-start.12) | collective-permute-done | bytes 458784 | tf_op jit(solution)/shard_map/ppermute | solution.py:383
  107.0 2.7 %latent_partial.7 = (bf16[128,1792]{1,0:T(8,128)(2,1)S(1)}, bf16[64,2176]{1,0:T(8,128)(2,1)S(1)}, bf16[64,2176]{1,0:T(8,128)(2,1)S(1)}, bf16[128,2176]{1,0:T(8,128)(2,1)S(1)}) custom-call(bf16[128,1792]{1,0:T(8,128)(2,1)S(1)} %project.9.refs_0_, bf16[128,1792]{1,0:T(8,128)(2,1)S(1)} %collective-permute-done.12.refs_1_, ...), custom_call_target="tpu_custom_call" | custom-call | tf_op jit(solution)/shard_map/latent_partial/pallas_call | solution.py:66
  110.5 4.9 %collective-permute-start.19 = (bf16[128,2176]{1,0:T(8,128)(2,1)S(1)}, bf16[128,2176]{1,0:T(8,128)(2,1)S(1)}, u32[]{:S(2)}, u32[]{:S(2)}) collective-permute-start(bf16[128,2176]{1,0:T(8,128)(2,1)S(1)} %get-tuple-element.80), channel_id=1, source_target_pairs={{2,4},{4,2},{3,5},{5,3},{10,12},{12,10},{11,13},{13,11},{18,20},{2... | collective-permute-start | bytes 1671176 | tf_op jit(solution)/shard_map/ppermute | solution.py:478
  116.0 1.3 collective-permute-start.20
  117.4 1.3 collective-permute-start.21
  118.7 5.1 %collective-permute-done.15.refs_0_ = bf16[64,7296]{1,0:T(8,128)(2,1)S(1)} collective-permute-done((bf16[64,7296]{1,0:T(8,128)(2,1)S(1)}, bf16[64,7296]{1,0:T(8,128)(2,1)S(1)}, u32[]{:S(2)}, u32[]{:S(2)}) %collective-permute-start.15) | collective-permute-done | bytes 933920 | tf_op jit(solution)/shard_map/ppermute | solution.py:446
  124.5 7.3 %collective-permute-done.20.single_ref = bf16[64,2176]{1,0:T(8,128)(2,1)S(1)} collective-permute-done((bf16[64,2176]{1,0:T(8,128)(2,1)S(1)}, bf16[64,2176]{1,0:T(8,128)(2,1)S(1)}, u32[]{:S(2)}, u32[]{:S(2)}) %collective-permute-start.20) | collective-permute-done | bytes 278560 | tf_op jit(solution)/shard_map/ppermute | solution.py:478
  131.9 1.6 %collective-permute-done.21.far_ref = bf16[64,2176]{1,0:T(8,128)(2,1)S(1)} collective-permute-done((bf16[64,2176]{1,0:T(8,128)(2,1)S(1)}, bf16[64,2176]{1,0:T(8,128)(2,1)S(1)}, u32[]{:S(2)}, u32[]{:S(2)}) %collective-permute-start.21) | collective-permute-done | bytes 278560 | tf_op jit(solution)/shard_map/ppermute | solution.py:478
  133.5 2.6 %collective-permute-done.19.second_ref = bf16[128,2176]{1,0:T(8,128)(2,1)S(1)} collective-permute-done((bf16[128,2176]{1,0:T(8,128)(2,1)S(1)}, bf16[128,2176]{1,0:T(8,128)(2,1)S(1)}, u32[]{:S(2)}, u32[]{:S(2)}) %collective-permute-start.19) | collective-permute-done | bytes 557088 | tf_op jit(solution)/shard_map/ppermute | solution.py:478
  136.3 1.3 collective-permute-start.22
  138.6 1.3 collective-permute-start.23
  139.9 1.3 collective-permute-start.24
  141.2 1.0 multiply_sine_fusion
  142.3 1.0 place_rows.1
  143.3 3.2 %collective-permute-done.23.refs_1_ = bf16[32,2176]{1,0:T(8,128)(2,1)S(1)} collective-permute-done((bf16[32,2176]{1,0:T(8,128)(2,1)S(1)}, bf16[32,2176]{1,0:T(8,128)(2,1)S(1)}, u32[]{:S(2)}, u32[]{:S(2)}) %collective-permute-start.23) | collective-permute-done | bytes 139296 | tf_op jit(solution)/shard_map/ppermute | solution.py:478
  146.5 2.2 %collective-permute-done.24.refs_2_ = bf16[32,2176]{1,0:T(8,128)(2,1)S(1)} collective-permute-done((bf16[32,2176]{1,0:T(8,128)(2,1)S(1)}, bf16[32,2176]{1,0:T(8,128)(2,1)S(1)}, u32[]{:S(2)}, u32[]{:S(2)}) %collective-permute-start.24) | collective-permute-done | bytes 139296 | tf_op jit(solution)/shard_map/ppermute | solution.py:507
  148.7 1.1 finish.1
  (60 shorter events, 6.4 us)
Async XLA Ops:
  0.6 55.4 %slice-start = ((s8[12845056]{0:T(1024)(128)(4,1)}), s8[262144]{0:T(1024)(128)(4,1)S(1)}, s32[]{:S(2)}) async-start(s8[12845056]{0:T(1024)(128)(4,1)} %bitcast.2), calls=%async_computation | async-start | bytes 524288
  2.8 23.5 %collective-permute-start.3 = (bf16[64,7168]{1,0:T(8,128)(2,1)}, bf16[64,7168]{1,0:T(8,128)(2,1)S(1)}, u32[]{:S(2)}, u32[]{:S(2)}) collective-permute-start(bf16[64,7168]{1,0:T(8,128)(2,1)} %enter.1.refs_0_), channel_id=1, source_target_pairs={{0,2},{2,0},{4,6},{6,4},{1,3},{3,1},{5,7},{7,5},{8,10},{10,8},{12,... | collective-permute-start | bytes 2752520 | tf_op jit(solution)/shard_map/ppermute | solution.py:413
  2.9 26.9 %collective-permute-start.4 = (bf16[64,7168]{1,0:T(8,128)(2,1)}, bf16[64,7168]{1,0:T(8,128)(2,1)S(1)}, u32[]{:S(2)}, u32[]{:S(2)}) collective-permute-start(bf16[64,7168]{1,0:T(8,128)(2,1)} %enter.1.refs_0_), channel_id=1, source_target_pairs={{2,4},{4,2},{3,5},{5,3},{10,12},{12,10},{11,13},{13,11},{18,20},{2... | collective-permute-start | bytes 2752520 | tf_op jit(solution)/shard_map/ppermute | solution.py:414
  7.9 1.2 copy-start.4
  9.1 1.2 copy-start.5
  10.7 4.3 %collective-permute-start = (f32[128,128]{1,0:T(8,128)S(1)}, f32[128,128]{1,0:T(8,128)S(1)}, u32[]{:S(2)}, u32[]{:S(2)}) collective-permute-start(f32[128,128]{1,0:T(8,128)S(1)} %add_squares.1.sums_ref), channel_id=1, source_target_pairs={{0,1},{1,0},{2,3},{3,2},{4,5},{5,4},{6,7},{7,6},{8,9},{9,8},{10,11... | collective-permute-start | bytes 196616 | tf_op jit(solution)/shard_map/ppermute | solution.py:405
  15.1 32.2 %collective-permute-start.1 = (bf16[64,7296]{1,0:T(8,128)(2,1)S(1)}, bf16[64,7296]{1,0:T(8,128)(2,1)S(1)}, u32[]{:S(2)}, u32[]{:S(2)}) collective-permute-start(bf16[64,7296]{1,0:T(8,128)(2,1)S(1)} %get-tuple-element.46.refs_2_), channel_id=1, source_target_pairs={{0,2},{2,0},{4,6},{6,4},{1,3},{3,1},{5,7},{7,5},{8,10},{10,8},{12,... | collective-permute-start | bytes 2801672 | tf_op jit(solution)/shard_map/ppermute | solution.py:413
  15.2 35.5 %collective-permute-start.2 = (bf16[64,7296]{1,0:T(8,128)(2,1)S(1)}, bf16[64,7296]{1,0:T(8,128)(2,1)S(1)}, u32[]{:S(2)}, u32[]{:S(2)}) collective-permute-start(bf16[64,7296]{1,0:T(8,128)(2,1)S(1)} %get-tuple-element.46.refs_2_), channel_id=1, source_target_pairs={{2,4},{4,2},{3,5},{5,3},{10,12},{12,10},{11,13},{13,11},{18,20},{2... | collective-permute-start | bytes 2801672 | tf_op jit(solution)/shard_map/ppermute | solution.py:414
  26.3 51.3 %collective-permute-start.7 = (bf16[64,7168]{1,0:T(8,128)(2,1)S(1)}, bf16[64,7168]{1,0:T(8,128)(2,1)S(1)}, u32[]{:S(2)}, u32[]{:S(2)}) collective-permute-start(bf16[64,7168]{1,0:T(8,128)(2,1)S(1)} %collective-permute-done.3.refs_0_), channel_id=1, source_target_pairs={{2,4},{4,2},{3,5},{5,3},{10,12},{12,10},{11,13},{13,11},{18,20},{2... | collective-permute-start | bytes 2752520 | tf_op jit(solution)/shard_map/ppermute | solution.py:416
  29.8 47.8 %collective-permute-start.8 = (bf16[64,7168]{1,0:T(8,128)(2,1)S(1)}, bf16[64,7168]{1,0:T(8,128)(2,1)S(1)}, u32[]{:S(2)}, u32[]{:S(2)}) collective-permute-start(bf16[64,7168]{1,0:T(8,128)(2,1)S(1)} %collective-permute-done.4.refs_2_), channel_id=1, source_target_pairs={{4,6},{2,0},{5,7},{3,1},{12,14},{10,8},{13,15},{11,9},{20,22},{18,... | collective-permute-start | bytes 2752520 | tf_op jit(solution)/shard_map/ppermute | solution.py:415
  31.2 16.2 %collective-permute-start.5 = (f32[128,128]{1,0:T(8,128)S(1)}, f32[128,128]{1,0:T(8,128)S(1)}, u32[]{:S(2)}, u32[]{:S(2)}) collective-permute-start(f32[128,128]{1,0:T(8,128)S(1)} %get-tuple-element.48.refs_1_), channel_id=1, source_target_pairs={{0,6},{6,0},{1,7},{7,1},{8,14},{14,8},{9,15},{15,9},{16,22},{22,16... | collective-permute-start | bytes 196616 | tf_op jit(solution)/shard_map/ppermute | solution.py:408
  33.3 4.7 %copy-start = (bf16[3584,1792]{1,0:T(8,128)(2,1)S(1)}, bf16[3584,1792]{1,0:T(8,128)(2,1)}, u32[]{:S(2)}) copy-start(bf16[3584,1792]{1,0:T(8,128)(2,1)} %refs_4_.3) | copy-start | bytes 38535172
  38.0 4.7 %copy-start.1 = (bf16[3584,1792]{1,0:T(8,128)(2,1)S(1)}, bf16[3584,1792]{1,0:T(8,128)(2,1)}, u32[]{:S(2)}) copy-start(bf16[3584,1792]{1,0:T(8,128)(2,1)} %refs_5_.5) | copy-start | bytes 38535172
  42.6 1.2 copy-start.6
  43.8 12.3 %slice-start.1 = ((s8[12845056]{0:T(1024)(128)(4,1)}), s8[4194304]{0:T(1024)(128)(4,1)S(1)}, s32[]{:S(2)}) async-start(s8[12845056]{0:T(1024)(128)(4,1)} %bitcast.2), calls=%async_computation.1 | async-start | bytes 8388608
  43.8 12.3 %slice-start.2 = ((s8[12845056]{0:T(1024)(128)(4,1)}), s8[4194304]{0:T(1024)(128)(4,1)S(1)}, s32[]{:S(2)}) async-start(s8[12845056]{0:T(1024)(128)(4,1)} %bitcast.2), calls=%async_computation.2 | async-start | bytes 8388608
  43.8 12.3 %slice-start.3 = ((s8[12845056]{0:T(1024)(128)(4,1)}), s8[4194304]{0:T(1024)(128)(4,1)S(1)}, s32[]{:S(2)}) async-start(s8[12845056]{0:T(1024)(128)(4,1)} %bitcast.2), calls=%async_computation.3 | async-start | bytes 8388608
  43.8 35.2 %copy-start.9 = (f32[1792]{0:T(1024)S(1)}, f32[1792]{0:T(1024)}, u32[]{:S(2)}) copy-start(f32[1792]{0:T(1024)} %param.16) | copy-start | bytes 21508
  50.8 41.1 %collective-permute-start.10 = (bf16[64,7296]{1,0:T(8,128)(2,1)S(1)}, bf16[64,7296]{1,0:T(8,128)(2,1)S(1)}, u32[]{:S(2)}, u32[]{:S(2)}) collective-permute-start(bf16[64,7296]{1,0:T(8,128)(2,1)S(1)} %collective-permute-done.1.refs_1_), channel_id=1, source_target_pairs={{2,4},{4,2},{3,5},{5,3},{10,12},{12,10},{11,13},{13,11},{18,20},{2... | collective-permute-start | bytes 2801672 | tf_op jit(solution)/shard_map/ppermute | solution.py:424
  54.7 37.1 %collective-permute-start.11 = (bf16[64,7296]{1,0:T(8,128)(2,1)S(1)}, bf16[64,7296]{1,0:T(8,128)(2,1)S(1)}, u32[]{:S(2)}, u32[]{:S(2)}) collective-permute-start(bf16[64,7296]{1,0:T(8,128)(2,1)S(1)} %collective-permute-done.2.refs_3_), channel_id=1, source_target_pairs={{4,6},{2,0},{5,7},{3,1},{12,14},{10,8},{13,15},{11,9},{20,22},{18,... | collective-permute-start | bytes 2801672 | tf_op jit(solution)/shard_map/ppermute | solution.py:423
  56.1 4.7 %copy-start.2 = (bf16[3584,1792]{1,0:T(8,128)(2,1)S(1)}, bf16[3584,1792]{1,0:T(8,128)(2,1)}, u32[]{:S(2)}) copy-start(bf16[3584,1792]{1,0:T(8,128)(2,1)} %refs_5_.5) | copy-start | bytes 38535172
  60.8 18.2 %copy-start.3 = (bf16[3584,1792]{1,0:T(8,128)(2,1)S(1)}, bf16[3584,1792]{1,0:T(8,128)(2,1)}, u32[]{:S(2)}) copy-start(bf16[3584,1792]{1,0:T(8,128)(2,1)} %refs_5_.5) | copy-start | bytes 38535172
  60.8 25.9 %slice-start.4 = ((s8[7569408]{0:T(1024)(128)(4,1)}), s8[4194304]{0:T(1024)(128)(4,1)S(1)}, s32[]{:S(2)}) async-start(s8[7569408]{0:T(1024)(128)(4,1)} %bitcast.4), calls=%async_computation.4 | async-start | bytes 8388608
  64.8 21.9 %slice-start.5 = ((s8[7569408]{0:T(1024)(128)(4,1)}), s8[3375104]{0:T(1024)(128)(4,1)S(1)}, s32[]{:S(2)}) async-start(s8[7569408]{0:T(1024)(128)(4,1)} %bitcast.4), calls=%async_computation.5 | async-start | bytes 6750208
  64.8 11.5 %collective-permute-start.9 = (bf16[128,1792]{1,0:T(8,128)(2,1)S(1)}, bf16[128,1792]{1,0:T(8,128)(2,1)S(1)}, u32[]{:S(2)}, u32[]{:S(2)}) collective-permute-start(bf16[128,1792]{1,0:T(8,128)(2,1)S(1)} %project.8), channel_id=1, source_target_pairs={{1,0},{3,2},{2,3},{5,4},{4,5},{6,7},{9,8},{11,10},{10,11},{13,12},... | collective-permute-start | bytes 1376264 | tf_op jit(solution)/shard_map/ppermute | solution.py:383
  76.3 10.4 %collective-permute-start.6 = (bf16[128,1792]{1,0:T(8,128)(2,1)S(1)}, bf16[128,1792]{1,0:T(8,128)(2,1)S(1)}, u32[]{:S(2)}, u32[]{:S(2)}) collective-permute-start(bf16[128,1792]{1,0:T(8,128)(2,1)S(1)} %project.6.refs_0_), channel_id=1, source_target_pairs={{1,0},{3,2},{4,5},{6,7},{9,8},{11,10},{12,13},{14,15},{17,16},{19,... | collective-permute-start | bytes 1376264 | tf_op jit(solution)/shard_map/ppermute | solution.py:383
  77.6 26.9 %collective-permute-start.13 = (bf16[64,7168]{1,0:T(8,128)(2,1)S(1)}, bf16[64,7168]{1,0:T(8,128)(2,1)S(1)}, u32[]{:S(2)}, u32[]{:S(2)}) collective-permute-start(bf16[64,7168]{1,0:T(8,128)(2,1)S(1)} %collective-permute-done.7.refs_2_), channel_id=1, source_target_pairs={{4,6},{2,0},{5,7},{3,1},{12,14},{10,8},{13,15},{11,9},{20,22},{18,... | collective-permute-start | bytes 2752520 | tf_op jit(solution)/shard_map/ppermute | solution.py:441
  91.8 31.9 %collective-permute-start.15 = (bf16[64,7296]{1,0:T(8,128)(2,1)S(1)}, bf16[64,7296]{1,0:T(8,128)(2,1)S(1)}, u32[]{:S(2)}, u32[]{:S(2)}) collective-permute-start(bf16[64,7296]{1,0:T(8,128)(2,1)S(1)} %collective-permute-done.10.refs_3_), channel_id=1, source_target_pairs={{4,6},{2,0},{5,7},{3,1},{12,14},{10,8},{13,15},{11,9},{20,22},{18,... | collective-permute-start | bytes 2801672 | tf_op jit(solution)/shard_map/ppermute | solution.py:446
  97.2 9.8 %collective-permute-start.12 = (bf16[128,1792]{1,0:T(8,128)(2,1)S(1)}, bf16[128,1792]{1,0:T(8,128)(2,1)S(1)}, u32[]{:S(2)}, u32[]{:S(2)}) collective-permute-start(bf16[128,1792]{1,0:T(8,128)(2,1)S(1)} %project.9.refs_0_), channel_id=1, source_target_pairs={{0,1},{2,3},{5,4},{7,6},{8,9},{10,11},{13,12},{15,14},{16,17},{18,... | collective-permute-start | bytes 1376264 | tf_op jit(solution)/shard_map/ppermute | solution.py:383
  109.7 23.7 %collective-permute-start.18 = (bf16[128,2176]{1,0:T(8,128)(2,1)S(1)}, bf16[128,2176]{1,0:T(8,128)(2,1)S(1)}, u32[]{:S(2)}, u32[]{:S(2)}) collective-permute-start(bf16[128,2176]{1,0:T(8,128)(2,1)S(1)} %get-tuple-element.80), channel_id=1, source_target_pairs={{0,4},{7,3},{8,12},{15,11},{16,20},{23,19},{24,28},{31,27}} | collective-permute-start | bytes 1671176 | tf_op jit(solution)/shard_map/ppermute | solution.py:478
  110.5 25.6 %collective-permute-start.19 = (bf16[128,2176]{1,0:T(8,128)(2,1)S(1)}, bf16[128,2176]{1,0:T(8,128)(2,1)S(1)}, u32[]{:S(2)}, u32[]{:S(2)}) collective-permute-start(bf16[128,2176]{1,0:T(8,128)(2,1)S(1)} %get-tuple-element.80), channel_id=1, source_target_pairs={{2,4},{4,2},{3,5},{5,3},{10,12},{12,10},{11,13},{13,11},{18,20},{2... | collective-permute-start | bytes 1671176 | tf_op jit(solution)/shard_map/ppermute | solution.py:478
  115.4 2.0 %collective-permute-start.14 = (bf16[64,1792]{1,0:T(8,128)(2,1)S(1)}, bf16[64,1792]{1,0:T(8,128)(2,1)S(1)}, u32[]{:S(2)}, u32[]{:S(2)}) collective-permute-start(bf16[64,1792]{1,0:T(8,128)(2,1)S(1)} %project.10.refs_0_), channel_id=1, source_target_pairs={{0,1},{7,6},{8,9},{15,14},{16,17},{23,22},{24,25},{31,30}} | collective-permute-start | bytes 688136 | tf_op jit(solution)/shard_map/ppermute | solution.py:383
  116.0 15.9 %collective-permute-start.20 = (bf16[64,2176]{1,0:T(8,128)(2,1)S(1)}, bf16[64,2176]{1,0:T(8,128)(2,1)S(1)}, u32[]{:S(2)}, u32[]{:S(2)}) collective-permute-start(bf16[64,2176]{1,0:T(8,128)(2,1)S(1)} %get-tuple-element.74.inner_ref), channel_id=1, source_target_pairs={{0,2},{6,4},{1,3},{7,5},{8,10},{14,12},{9,11},{15,13},{16,18},{22,... | collective-permute-start | bytes 835592 | tf_op jit(solution)/shard_map/ppermute | solution.py:478
  117.4 24.9 %copy-start.8 = (f32[1536]{0:T(1024)S(1)}, f32[1536]{0:T(1024)}, u32[]{:S(2)}) copy-start(f32[1536]{0:T(1024)} %param.18) | copy-start | bytes 18436
  117.4 16.1 %collective-permute-start.21 = (bf16[64,2176]{1,0:T(8,128)(2,1)S(1)}, bf16[64,2176]{1,0:T(8,128)(2,1)S(1)}, u32[]{:S(2)}, u32[]{:S(2)}) collective-permute-start(bf16[64,2176]{1,0:T(8,128)(2,1)S(1)} %get-tuple-element.81), channel_id=1, source_target_pairs={{6,2},{1,5},{14,10},{9,13},{22,18},{17,21},{30,26},{25,29}} | collective-permute-start | bytes 835592 | tf_op jit(solution)/shard_map/ppermute | solution.py:478
  123.7 25.0 %copy-start.7 = (f32[512]{0:T(512)S(1)}, f32[512]{0:T(512)}, u32[]{:S(2)}) copy-start(f32[512]{0:T(512)} %param.19) | copy-start | bytes 6148
  123.7 14.6 %collective-permute-start.16 = (bf16[32,1792]{1,0:T(8,128)(2,1)S(1)}, bf16[32,1792]{1,0:T(8,128)(2,1)S(1)}, u32[]{:S(2)}, u32[]{:S(2)}) collective-permute-start(bf16[32,1792]{1,0:T(8,128)(2,1)S(1)} %get-tuple-element.77.refs_5_.refs_12_), channel_id=1, source_target_pairs={{0,1},{1,0},{6,7},{7,6},{8,9},{9,8},{14,15},{15,14},{16,17},{17,16... | collective-permute-start | bytes 344072 | tf_op jit(solution)/shard_map/ppermute | solution.py:498
  136.3 12.4 %collective-permute-start.22 = (bf16[64,2304]{1,0:T(8,128)(2,1)S(1)}, bf16[64,2304]{1,0:T(8,128)(2,1)S(1)}, u32[]{:S(2)}, u32[]{:S(2)}) collective-permute-start(bf16[64,2304]{1,0:T(8,128)(2,1)S(1)} %get-tuple-element.83), channel_id=1, source_target_pairs={{2,0},{4,6},{3,1},{5,7},{10,8},{12,14},{11,9},{13,15},{18,16},{20,... | collective-permute-start | bytes 884744 | tf_op jit(solution)/shard_map/ppermute | solution.py:478
  137.7 4.6 %collective-permute-start.17 = (bf16[32,1792]{1,0:T(8,128)(2,1)S(1)}, bf16[32,1792]{1,0:T(8,128)(2,1)S(1)}, u32[]{:S(2)}, u32[]{:S(2)}) collective-permute-start(bf16[32,1792]{1,0:T(8,128)(2,1)S(1)} %get-tuple-element.76.refs_0_), channel_id=1, source_target_pairs={{7,6},{0,1},{15,14},{8,9},{23,22},{16,17},{31,30},{24,25}} | collective-permute-start | bytes 344072 | tf_op jit(solution)/shard_map/ppermute | solution.py:383
  138.6 7.8 %collective-permute-start.23 = (bf16[32,2176]{1,0:T(8,128)(2,1)S(1)}, bf16[32,2176]{1,0:T(8,128)(2,1)S(1)}, u32[]{:S(2)}, u32[]{:S(2)}) collective-permute-start(bf16[32,2176]{1,0:T(8,128)(2,1)S(1)} %get-tuple-element.84), channel_id=1, source_target_pairs={{6,2},{1,5},{14,10},{9,13},{22,18},{17,21},{30,26},{25,29}} | collective-permute-start | bytes 417800 | tf_op jit(solution)/shard_map/ppermute | solution.py:478
  139.9 8.7 %collective-permute-start.24 = (bf16[32,2176]{1,0:T(8,128)(2,1)S(1)}, bf16[32,2176]{1,0:T(8,128)(2,1)S(1)}, u32[]{:S(2)}, u32[]{:S(2)}) collective-permute-start(bf16[32,2176]{1,0:T(8,128)(2,1)S(1)} %get-tuple-element.84), channel_id=1, source_target_pairs={{7,2},{0,5},{15,10},{8,13},{23,18},{16,21},{31,26},{24,29}} | collective-permute-start | bytes 417800 | tf_op jit(solution)/shard_map/ppermute | solution.py:507
